TPU v7x, 32 devices: a whole 2x2x4 slice. The times are simulated.
32 devices in a mesh: ctx: 8 (over y, x, core), head: 4 (over z).
Axes of the slice: x: 2, y: 2, z: 4, core: 2. Of those that a mesh axis runs over, the one named last changes fastest.
Arguments:
- hidden: bfloat16 [4096, 5376], P('ctx'), may hold values from -18 to 18
- w_query: bfloat16 [5376, 2048], P(None, 'head'), may hold values from -0.078125 to 0.078125
- key_weight_matrix: bfloat16 [5376, 1024], P(None, 'head'), may hold values from -0.078125 to 0.078125
- value_weight_matrix: bfloat16 [5376, 1024], P(None, 'head'), may hold values from -0.078125 to 0.078125
- attention_output_gradient: bfloat16 [4096, 2048], P('ctx', 'head'), may hold values from -6 to 6
- doc_start: int32 [4096], P('ctx'), may hold values from 0 to 4095, as said below
Outputs:
- d_hidden: float32 [4096, 5376], P(('ctx', 'head'))
Inputs may be any that keep to these rules, and one draw needn't show every extreme that they name: doc_start is non-decreasing, doc_start[i] <= i, constant within a document and equal to i at a document's first token; doc_start[0] = 0, and the last token begins a document of its own.
All inputs are finite; a program needn't handle non-finite values.
Results may differ from a plain program's by a relative error of at most 0.014.
The roundings to bfloat16 on the way count: a program that leaves them out, or rounds other values in their place, can miss the bound.
Values may be sent and summed in bfloat16 or wider, within the bound.
No kernel may reach another device: no remote copies, remote signals or barrier semaphores. Data moves between devices by JAX's collectives and lax.ppermute only.
A program may use at most 128 MiB of HBM per device.

v0:
```python
import jax
import jax.numpy as jnp
from jax import lax
from jax.sharding import PartitionSpec as P

HEAD_SIZE = 128
W = 1024
HALO = 2


SCALE = 168.0 ** (-0.5)


def from_behind(array, axis, by):
    devices = lax.axis_size(axis)
    pairs = [(i, i + by) for i in range(devices) if 0 <= i + by < devices]
    return lax.ppermute(array, axis, pairs)


def back_project(grad, weight):
    return lax.dot_general(
        grad, weight, (((1,), (1,)), ((), ())), preferred_element_type=jnp.float32
    )


def segment_scores(query_four, key_tile_block, query_position, lower_bound, key_position):
    scores = (
        jnp.einsum("ikgd,jkd->kgij", query_four, key_tile_block, preferred_element_type=jnp.float32)
        * SCALE
    )
    allowed = (key_position[None, :] >= lower_bound[:, None]) & (
        key_position[None, :] <= query_position[:, None]
    )
    return jnp.where(allowed[None, None], scores, -jnp.inf)


def shards(
    hidden, w_query, key_weight_matrix, value_weight_matrix, attention_output_gradient, doc_start
):
    row_count = hidden.shape[0]
    kv_local = key_weight_matrix.shape[1] // HEAD_SIZE
    query_group_count = w_query.shape[1] // key_weight_matrix.shape[1]
    kv_width = kv_local * HEAD_SIZE
    leading_row = lax.axis_index("ctx") * row_count
    query_rows = jnp.dot(hidden, w_query, preferred_element_type=jnp.float32).astype(jnp.bfloat16)
    projected_keys = jnp.dot(hidden, key_weight_matrix, preferred_element_type=jnp.float32).astype(
        jnp.bfloat16
    )
    projected_values = jnp.dot(
        hidden, value_weight_matrix, preferred_element_type=jnp.float32
    ).astype(jnp.bfloat16)
    packed = jnp.concatenate([projected_keys, projected_values], axis=1)
    earlier = []
    moving = packed
    for distance in range(HALO):
        moving = from_behind(moving, "ctx", 1)
        earlier.append(moving)
    query_position = leading_row + jnp.arange(row_count, dtype=jnp.int32)
    lower_bound = jnp.maximum(doc_start, query_position - W + 1)
    query_four = query_rows.reshape(row_count, kv_local, query_group_count, HEAD_SIZE)
    output_gradient = attention_output_gradient.reshape(
        row_count, kv_local, query_group_count, HEAD_SIZE
    )
    ordered = earlier[::-1] + [packed]
    halo_first = leading_row - HALO * row_count
    segments = [jnp.concatenate(ordered, axis=0)]
    seg_firsts = [halo_first]
    key_blocks = []
    value_blocks = []
    score_list = []
    for segment, seg_first in zip(segments, seg_firsts):
        seg_rows = segment.shape[0]
        key_tile_block = segment[:, :kv_width].reshape(seg_rows, kv_local, HEAD_SIZE)
        value_tile_block = segment[:, kv_width:].reshape(seg_rows, kv_local, HEAD_SIZE)
        key_position = seg_first + jnp.arange(seg_rows, dtype=jnp.int32)
        key_blocks.append(key_tile_block)
        value_blocks.append(value_tile_block)
        score_list.append(
            segment_scores(query_four, key_tile_block, query_position, lower_bound, key_position)
        )
    row_max = score_list[0].max(axis=-1)
    scores = score_list[0]
    denominator = jnp.sum(jnp.exp(scores - row_max[..., None]), axis=-1)
    log_total = row_max + jnp.log(denominator)
    prob_list = []
    output = jnp.zeros((row_count, kv_local, query_group_count, HEAD_SIZE), jnp.float32)
    for scores, value_tile_block in zip(score_list, value_blocks):
        probability = jnp.exp(scores - log_total[..., None])
        probability_low = probability.astype(jnp.bfloat16)
        prob_list.append((probability, probability_low))
        output = jnp.einsum(
            "kgij,jkd->ikgd", probability_low, value_tile_block, preferred_element_type=jnp.float32
        )
    row_dot = jnp.einsum("ikgd,ikgd->kgi", output_gradient.astype(jnp.float32), output)
    d_query = jnp.zeros((row_count, kv_local, query_group_count, HEAD_SIZE), jnp.float32)
    grad_list = []
    for (probability, probability_low), key_tile_block, value_tile_block in zip(
        prob_list, key_blocks, value_blocks
    ):
        d_probs = jnp.einsum(
            "ikgd,jkd->kgij", output_gradient, value_tile_block, preferred_element_type=jnp.float32
        )
        d_scores = (probability * (d_probs - row_dot[..., None]) * SCALE).astype(jnp.bfloat16)
        d_query = jnp.einsum(
            "kgij,jkd->ikgd", d_scores, key_tile_block, preferred_element_type=jnp.float32
        )
        d_key = jnp.einsum(
            "kgij,ikgd->jkd", d_scores, query_four, preferred_element_type=jnp.float32
        )
        d_value = jnp.einsum(
            "kgij,ikgd->jkd", probability_low, output_gradient, preferred_element_type=jnp.float32
        )
        seg_rows = key_tile_block.shape[0]
        grad_list.append(
            jnp.concatenate(
                [d_key.reshape(seg_rows, kv_width), d_value.reshape(seg_rows, kv_width)], axis=1
            )
        )
    full_grad = grad_list[0]
    own_grad = full_grad[HALO * row_count :]
    passing = jnp.zeros_like(own_grad)
    for distance in range(HALO, 0, -1):
        passing = from_behind(
            passing + full_grad[(HALO - distance) * row_count : (HALO - distance + 1) * row_count],
            "ctx",
            -1,
        )
    combined = own_grad + passing
    d_query_low = d_query.reshape(row_count, kv_local * query_group_count * HEAD_SIZE).astype(
        jnp.bfloat16
    )
    key_gradient_rows = combined[:, :kv_width].astype(jnp.bfloat16)
    value_gradient_rows = combined[:, kv_width:].astype(jnp.bfloat16)
    contribution = back_project(d_query_low, w_query)
    contribution = contribution + back_project(key_gradient_rows, key_weight_matrix)
    return lax.psum_scatter(
        contribution + back_project(value_gradient_rows, value_weight_matrix),
        "head",
        scatter_dimension=0,
        tiled=True,
    )


def solution(mesh):
    in_specs = (
        P("ctx", None),
        P(None, "head"),
        P(None, "head"),
        P(None, "head"),
        P("ctx", "head"),
        P("ctx"),
    )
    out_specs = P(("ctx", "head"), None)
    return jax.shard_map(shards, mesh=mesh, in_specs=in_specs, out_specs=out_specs, check_vma=False)
```

profile of v0, /device:TPU:12, one launch (start us, length us, event | category | flops | bytes accessed | tf_op | source)
XLA Modules:
  0.0 326.4 jit_solution(7894330286402523850)
XLA Ops:
  6.5 0.0 copy-start
  6.5 0.0 reduce-scatter.2.cloned.1.call-start
  6.5 1.8 copy-done
  8.3 4.3 %convolution_convert_fusion.3 = bf16[512,256]{0,1:T(8,128)(2,1)S(1)} fusion(bf16[512,5376]{1,0:T(8,128)(2,1)} %param.6, bf16[5376,256]{1,0:T(8,128)(2,1)S(1)} %copy-done), kind=kOutput, calls=%fused_computation.19 | convolution fusion | flops 1409417216 | bytes 8519680 | tf_op jit(solution)/shard_map/dot_general | solution.py:46
  12.7 0.0 copy-done.8
  12.7 0.0 slice-start.1
  12.7 0.0 slice-start.5
  12.7 4.7 %convolution_convert_fusion.2 = bf16[512,256]{0,1:T(8,128)(2,1)S(1)} fusion(bf16[512,5376]{1,0:T(8,128)(2,1)} %param.6, bf16[5376,256]{1,0:T(8,128)(2,1)S(1)} %copy-done.8), kind=kOutput, calls=%fused_computation.18 | convolution fusion | flops 1409417216 | bytes 8519680 | tf_op jit(solution)/shard_map/dot_general | solution.py:49
  17.4 0.0 copy-start.9
  17.4 0.7 copy-done.9
  18.1 0.0 copy-start.15
  18.1 1.9 collective-permute-start
  20.1 0.0 slice-done
  20.1 0.0 slice-done.4
  20.1 0.0 slice-done.1
  20.1 0.0 slice-done.5
  20.1 3.9 %convolution_convert_fusion.1 = bf16[512,512]{0,1:T(8,128)(2,1)} fusion(bf16[512,5376]{1,0:T(8,128)(2,1)S(1)} %bitcast.100, bf16[5376,512]{1,0:T(8,128)(2,1)S(1)} %bitcast.89), kind=kOutput, calls=%fused_computation.17 | convolution fusion | flops 2818834432 | bytes 11534336 | tf_op jit(solution)/shard_map/dot_general | solution.py:45
  24.0 0.0 copy-done.15
  24.0 5.7 %collective-permute-done = bf16[512,512]{0,1:T(8,128)(2,1)} collective-permute-done((bf16[512,512]{0,1:T(8,128)(2,1)S(1)}, bf16[512,512]{0,1:T(8,128)(2,1)}, u32[]{:S(2)}, u32[]{:S(2)}) %collective-permute-start) | collective-permute-done | bytes 524320 | tf_op jit(solution)/shard_map/ppermute | solution.py:17
  29.6 2.1 collective-permute-start.1
  31.8 1.2 reshape.93
  32.9 1.4 copy.14
  34.4 0.7 compare_and_fusion
  35.1 0.0 copy-start.4
  35.1 6.3 %collective-permute-done.1 = bf16[512,512]{0,1:T(8,128)(2,1)} collective-permute-done((bf16[512,512]{0,1:T(8,128)(2,1)}, bf16[512,512]{0,1:T(8,128)(2,1)}, u32[]{:S(2)}, u32[]{:S(2)}) %collective-permute-start.1) | collective-permute-done | bytes 524320 | tf_op jit(solution)/shard_map/ppermute | solution.py:17
  41.4 1.4 maximum_maximum_fusion
  42.7 0.1 fusion.18
  42.9 0.0 copy-start.6
  42.9 2.4 fusion.4
  45.2 0.0 copy-done.6
  45.3 2.7 exponential_reduce_fusion
  48.0 0.0 copy-done.4
  48.0 0.0 copy-done.10
  48.0 1.7 copy-done.3
  49.8 4.3 %fusion.16 = f32[2,128,2,512]{3,1,2,0:T(8,128)} fusion(bf16[1536,2,128,1]{0,2,3,1:T(8,128)(2,1)S(1)} %bitcast.95, f32[2,1536,512,2]{2,1,3,0:T(8,128)S(1)} %get-tuple-element.8, f32[2,2,512]{2,1,0:T(2,128)S(1)} %log_add_fusion, pred[512,1536]{0,1:T(8,128)(4,1)S(1)} %compare_and_fusion), kind=kOutput, calls=%fused_computation.37 | convolution fusion | flops 817889280 | bytes 15212544 | tf_op jit(solution)/shard_map/kgij,jkd->ikgd/dot_general | solution.py:91
  54.1 2.3 copy.38
  56.4 3.5 %fusion.10 = f32[2,2,512]{1,0,2:T(2,128)} fusion(f32[2,128,2,512]{1,2,0,3:T(2,128)} %copy.38, bf16[512,2,2,128]{3,2,1,0:T(2,128)(2,1)S(1)} %reshape.93), kind=kLoop, calls=%fused_computation.27 | loop fusion | flops 784384 | bytes 1581056
  59.9 1.2 copy.26
  61.1 8.3 %fusion.14 = f32[2,1536,128,1]{1,2,3,0:T(8,128)S(1)} fusion(bf16[512,2,2,128]{0,3,2,1:T(8,128)(2,1)} %copy.14, f32[2,1536,512,2]{2,1,3,0:T(8,128)} %copy-done.3, f32[2,2,512]{2,1,0:T(2,128)S(1)} %log_add_fusion, pred[512,1536]{0,1:T(8,128)(4,1)} %copy-done.4), kind=kOutput, calls=%fused_computation.36 | convolution fusion | flops 817889280 | bytes 15474688 | tf_op jit(solution)/shard_map/kgij,ikgd->jkd/dot_general | solution.py:110
  69.4 0.0 copy-done.5
  69.5 0.0 copy-done.11
  69.5 0.0 copy-done.14
  69.5 0.0 copy-start.1
  69.5 8.3 %fusion.2 = bf16[2,2,512,1536]{2,3,1,0:T(8,128)(2,1)S(1)} fusion(f32[2,1536,512,2]{2,1,3,0:T(8,128)} %copy-done.3, bf16[1536,2,128,1]{0,2,3,1:T(8,128)(2,1)S(1)} %bitcast.96, bf16[512,2,2,128]{0,3,2,1:T(8,128)(2,1)S(1)} %copy-done.14, f32[2,2,512]{2,1,0:T(2,128)S(1)} %copy.26, f32[2,2,512]{2,1,0:T(2,128)S(1)} %log_add_fusion, pred[512,1536]{0,1:T(8,128)(4,1)S(1)} %copy-done.5), kind=kOutput, calls=%fused_computation.3 | convolution fusion | flops 827326464 | bytes 20987904 | tf_op jit(solution)/shard_map/ikgd,jkd->kgij/dot_general | solution.py:100
  77.8 2.1 fusion.20
  80.0 0.1 fusion.5
  80.1 0.0 slice-start.2
  80.1 2.2 collective-permute-start.2
  82.3 12.3 %collective-permute-done.2 = f32[512,512]{0,1:T(8,128)S(1)} collective-permute-done((f32[512,512]{0,1:T(8,128)S(1)}, f32[512,512]{0,1:T(8,128)S(1)}, u32[]{:S(2)}, u32[]{:S(2)}) %collective-permute-start.2) | collective-permute-done | bytes 1048608 | tf_op jit(solution)/shard_map/ppermute | solution.py:17
  94.6 0.0 copy-done.1
  94.6 1.2 fusion.9
  95.8 4.8 %collective-permute-start.3 = (f32[512,512]{0,1:T(8,128)}, f32[512,512]{0,1:T(8,128)}, u32[]{:S(2)}, u32[]{:S(2)}) collective-permute-start(f32[512,512]{0,1:T(8,128)} %fusion.9), channel_id=1, source_target_pairs={{4,0},{8,4},{12,8},{16,12},{20,16},{24,20},{28,24},{5,1},{9,5},{13... | collective-permute-start | bytes 3145736 | tf_op jit(solution)/shard_map/ppermute | solution.py:17
  100.6 1.0 convolution_convert_fusion
  101.6 0.0 slice-done.2
  101.6 0.0 slice-done.3
  101.7 0.0 copy-start.2
  101.7 3.1 fusion.19
  104.8 8.5 %collective-permute-done.3 = f32[512,512]{0,1:T(8,128)} collective-permute-done((f32[512,512]{0,1:T(8,128)}, f32[512,512]{0,1:T(8,128)}, u32[]{:S(2)}, u32[]{:S(2)}) %collective-permute-start.3) | collective-permute-done | bytes 1048608 | tf_op jit(solution)/shard_map/ppermute | solution.py:17
  113.2 0.0 copy-done.2
  113.2 1.4 fusion.8
  114.7 5.9 %fusion.12 = f32[512,5376]{1,0:T(8,128)} fusion(bf16[5376,256]{1,0:T(8,128)(2,1)S(1)} %copy-done, bf16[512,512]{0,1:T(8,128)(2,1)S(1)} %fusion.8), kind=kOutput, calls=%fused_computation.30 | convolution fusion | flops 1409286144 | bytes 14024704 | tf_op jit(solution)/shard_map/dot_general | solution.py:21
  120.5 10.8 %add_add_fusion = f32[512,5376]{1,0:T(8,128)} fusion(f32[512,5376]{1,0:T(8,128)S(1)} %fusion.19, f32[512,5376]{1,0:T(8,128)} %fusion.12, bf16[5376,256]{1,0:T(8,128)(2,1)} %param.9, bf16[512,512]{0,1:T(8,128)(2,1)S(1)} %fusion.8), kind=kOutput, calls=%fused_computation.8 | convolution fusion | flops 1414791168 | bytes 36044800 | tf_op jit(solution)/shard_map/dot_general | solution.py:21
  131.3 0.0 reduce-scatter.2.cloned.1.call-update
  131.4 188.2 %reduce-scatter.2.cloned.1.call-done = f32[128,5376]{1,0:T(8,128)} async-done(((f32[512,5376]{1,0:T(8,128)}), f32[128,5376]{1,0:T(8,128)}) %reduce-scatter.2.cloned.1.call-update) | async-done | bytes 2752528 | tf_op jit(solution)/shard_map/reduce_scatter | solution.py:136
  (22 shorter events, 0.1 us)
Async XLA Ops:
  6.5 1.8 copy-start
  6.5 313.0 %reduce-scatter.2.cloned.1.call-start = ((), (), s32[]{:S(2)}) async-start(), calls=%async_computation.1 | async-start | bytes 13762560 | tf_op jit(solution)/shard_map/reduce_scatter | solution.py:136
  8.3 4.4 %copy-start.8 = (bf16[5376,256]{1,0:T(8,128)(2,1)S(1)}, bf16[5376,256]{1,0:T(8,128)(2,1)}, u32[]{:S(2)}) copy-start(bf16[5376,256]{1,0:T(8,128)(2,1)} %param.9) | copy-start | bytes 8257540
  8.3 11.8 %slice-start = ((s8[5505024]{0:T(1024)(128)(4,1)}), s8[4194304]{0:T(1024)(128)(4,1)S(1)}, s32[]{:S(2)}) async-start(s8[5505024]{0:T(1024)(128)(4,1)} %bitcast.88), calls=%async_computation.2 | async-start | bytes 8388608
  8.3 11.8 %slice-start.4 = ((s8[5505024]{0:T(1024)(128)(4,1)}), s8[4194304]{0:T(1024)(128)(4,1)S(1)}, s32[]{:S(2)}) async-start(s8[5505024]{0:T(1024)(128)(4,1)} %bitcast.99), calls=%async_computation.6 | async-start | bytes 8388608
  12.7 7.4 %slice-start.1 = ((s8[5505024]{0:T(1024)(128)(4,1)}), s8[1310720]{0:T(1024)(128)(4,1)S(1)}, s32[]{:S(2)}) async-start(s8[5505024]{0:T(1024)(128)(4,1)} %bitcast.88), calls=%async_computation.3 | async-start | bytes 2621440
  12.7 7.4 %slice-start.5 = ((s8[5505024]{0:T(1024)(128)(4,1)}), s8[1310720]{0:T(1024)(128)(4,1)S(1)}, s32[]{:S(2)}) async-start(s8[5505024]{0:T(1024)(128)(4,1)} %bitcast.99), calls=%async_computation.7 | async-start | bytes 2621440
  17.4 0.7 copy-start.9
  18.1 5.9 %copy-start.15 = (s32[512]{0:T(512)S(1)}, s32[512]{0:T(512)}, u32[]{:S(2)}) copy-start(s32[512]{0:T(512)} %param.11) | copy-start | bytes 6148
  18.1 11.5 %collective-permute-start = (bf16[512,512]{0,1:T(8,128)(2,1)S(1)}, bf16[512,512]{0,1:T(8,128)(2,1)}, u32[]{:S(2)}, u32[]{:S(2)}) collective-permute-start(bf16[512,512]{0,1:T(8,128)(2,1)S(1)} %pad_maximum_fusion.1), channel_id=1, source_target_pairs={{0,4},{4,8},{8,12},{12,16},{16,20},{20,24},{24,28},{1,5},{5,9},{9,... | collective-permute-start | bytes 1572872 | tf_op jit(solution)/shard_map/ppermute | solution.py:17
  29.6 11.7 %collective-permute-start.1 = (bf16[512,512]{0,1:T(8,128)(2,1)}, bf16[512,512]{0,1:T(8,128)(2,1)}, u32[]{:S(2)}, u32[]{:S(2)}) collective-permute-start(bf16[512,512]{0,1:T(8,128)(2,1)} %collective-permute-done), channel_id=1, source_target_pairs={{0,4},{4,8},{8,12},{12,16},{16,20},{20,24},{24,28},{1,5},{5,9},{9,... | collective-permute-start | bytes 1572872 | tf_op jit(solution)/shard_map/ppermute | solution.py:17
  34.4 8.5 %copy-start.12 = (bf16[512,512]{0,1:T(8,128)(2,1)S(1)}, bf16[512,512]{0,1:T(8,128)(2,1)}, u32[]{:S(2)}) copy-start(bf16[512,512]{0,1:T(8,128)(2,1)} %convolution_convert_fusion.1) | copy-start | bytes 1572868
  35.1 13.0 %copy-start.4 = (pred[512,1536]{0,1:T(8,128)(4,1)}, pred[512,1536]{0,1:T(8,128)(4,1)S(1)}, u32[]{:S(2)}) copy-start(pred[512,1536]{0,1:T(8,128)(4,1)S(1)} %compare_and_fusion) | copy-start | bytes 2359300
  42.9 2.4 copy-start.6
  42.9 5.2 %copy-start.10 = (bf16[1536,256]{0,1:T(8,128)(2,1)}, bf16[1536,256]{0,1:T(8,128)(2,1)S(1)}, u32[]{:S(2)}) copy-start(bf16[1536,256]{0,1:T(8,128)(2,1)S(1)} %get-tuple-element.5) | copy-start | bytes 2359300
  45.3 4.5 %copy-start.3 = (f32[2,1536,512,2]{2,1,3,0:T(8,128)}, f32[2,1536,512,2]{2,1,3,0:T(8,128)S(1)}, u32[]{:S(2)}) copy-start(f32[2,1536,512,2]{2,1,3,0:T(8,128)S(1)} %get-tuple-element.8) | copy-start | bytes 37748740
  61.1 8.4 %copy-start.5 = (pred[512,1536]{0,1:T(8,128)(4,1)S(1)}, pred[512,1536]{0,1:T(8,128)(4,1)}, u32[]{:S(2)}) copy-start(pred[512,1536]{0,1:T(8,128)(4,1)} %copy-done.4) | copy-start | bytes 2359300
  61.1 8.4 %copy-start.11 = (bf16[1536,256]{0,1:T(8,128)(2,1)S(1)}, bf16[1536,256]{0,1:T(8,128)(2,1)}, u32[]{:S(2)}) copy-start(bf16[1536,256]{0,1:T(8,128)(2,1)} %copy-done.10) | copy-start | bytes 2359300
  61.1 8.4 %copy-start.14 = (bf16[512,2,2,128]{0,3,2,1:T(8,128)(2,1)S(1)}, bf16[512,2,2,128]{0,3,2,1:T(8,128)(2,1)}, u32[]{:S(2)}) copy-start(bf16[512,2,2,128]{0,3,2,1:T(8,128)(2,1)} %copy.14) | copy-start | bytes 1572868
  69.5 25.1 %copy-start.1 = (f32[2,1536,128,1]{1,2,3,0:T(8,128)}, f32[2,1536,128,1]{1,2,3,0:T(8,128)S(1)}, u32[]{:S(2)}) copy-start(f32[2,1536,128,1]{1,2,3,0:T(8,128)S(1)} %fusion.14) | copy-start | bytes 4718596
  69.5 8.3 %copy-start.13 = (bf16[512,512]{0,1:T(8,128)(2,1)S(1)}, bf16[512,512]{0,1:T(8,128)(2,1)}, u32[]{:S(2)}) copy-start(bf16[512,512]{0,1:T(8,128)(2,1)} %convolution_convert_fusion.1) | copy-start | bytes 1572868
  80.0 20.7 %copy-start.7 = (bf16[1536,256]{0,1:T(8,128)(2,1)S(1)}, bf16[1536,256]{0,1:T(8,128)(2,1)}, u32[]{:S(2)}) copy-start(bf16[1536,256]{0,1:T(8,128)(2,1)} %copy-done.6) | copy-start | bytes 2359300
  80.1 21.6 %slice-start.2 = ((s8[5505024]{0:T(1024)(128)(4,1)}), s8[4194304]{0:T(1024)(128)(4,1)S(1)}, s32[]{:S(2)}) async-start(s8[5505024]{0:T(1024)(128)(4,1)} %bitcast.90), calls=%async_computation.4 | async-start | bytes 8388608
  80.1 14.5 %collective-permute-start.2 = (f32[512,512]{0,1:T(8,128)S(1)}, f32[512,512]{0,1:T(8,128)S(1)}, u32[]{:S(2)}, u32[]{:S(2)}) collective-permute-start(f32[512,512]{0,1:T(8,128)S(1)} %fusion.5), channel_id=1, source_target_pairs={{4,0},{8,4},{12,8},{16,12},{20,16},{24,20},{28,24},{5,1},{9,5},{13... | collective-permute-start | bytes 3145736 | tf_op jit(solution)/shard_map/ppermute | solution.py:17
  95.8 5.9 %slice-start.3 = ((s8[5505024]{0:T(1024)(128)(4,1)}), s8[1310720]{0:T(1024)(128)(4,1)S(1)}, s32[]{:S(2)}) async-start(s8[5505024]{0:T(1024)(128)(4,1)} %bitcast.90), calls=%async_computation.5 | async-start | bytes 2621440
  95.8 17.5 %collective-permute-start.3 = (f32[512,512]{0,1:T(8,128)}, f32[512,512]{0,1:T(8,128)}, u32[]{:S(2)}, u32[]{:S(2)}) collective-permute-start(f32[512,512]{0,1:T(8,128)} %fusion.9), channel_id=1, source_target_pairs={{4,0},{8,4},{12,8},{16,12},{20,16},{24,20},{28,24},{5,1},{9,5},{13... | collective-permute-start | bytes 3145736 | tf_op jit(solution)/shard_map/ppermute | solution.py:17
  101.7 11.6 %copy-start.2 = (f32[2,1536,128,1]{1,2,3,0:T(8,128)S(1)}, f32[2,1536,128,1]{1,2,3,0:T(8,128)}, u32[]{:S(2)}) copy-start(f32[2,1536,128,1]{1,2,3,0:T(8,128)} %copy-done.1) | copy-start | bytes 4718596
Sparse Core Ops, SparseCore 0:
  131.5 188.0 reduce-scatter.1
where the time goes:
time: 328 us; the launch traced here: 326 us
  waiting for transfers between devices  221 us (67%)
  matrix products  59.1 us (18%)
  between operations  13.8 us (4%)
  starting transfers between devices  11 us (3%)
  other arithmetic  11 us (3%)
  local copies, waits for them, and re-layouts  10.5 us (3%)
    reduce_scatter x1, waiting for transfers between devices, shards(): lax.psum_scatter(contribution + back_project(value_gradient_rows, value_w...  188 us
    ppermute x4, waiting for transfers between devices, from_behind(): return lax.ppermute(array, axis, pairs)  32.7 us
    dot_general x3, matrix products, back_project(): lax.dot_general(grad, weight, (((1,), (1,)), ((), ())), preferred_element...  19.8 us
    ppermute x4, starting transfers between devices, from_behind(): return lax.ppermute(array, axis, pairs)  11 us
    dot_general x1, matrix products, shards(): jnp.einsum('kgij,ikgd->jkd', probability_low, output_gradient, preferred_...  8.34 us
    dot_general x1, matrix products, shards(): jnp.einsum('ikgd,jkd->kgij', output_gradient, value_tile_block, preferred...  8.32 us
    unnamed x45, local copies, waits for them, and re-layouts  6.56 us
  transfers between devices with their start and end apart: 5, of which 5 were waited for; matrix products, arithmetic and copies ran while one was open for 3% of the time, Pallas kernels for 0%

commit v1 on v0

v1 whole, which is shorter than its diff:
```python
import functools

import jax
import jax.numpy as jnp
from jax import lax
from jax.experimental import pallas as pl
from jax.experimental.pallas import tpu as pltpu
from jax.sharding import PartitionSpec as P

HEAD_SIZE = 128
W = 1024
HALO = 2
SCALE = 168.0 ** (-0.5)
LOG2E = 1.4426950408889634
BLOCK = 128
MASKED = -1e30
VMEM_LIMIT = 48 * 1024 * 1024

NT = (((1,), (1,)), ((), ()))


def project_kernel(hidden_ref, wk_ref, wv_ref, *refs):
    outs, acc_ref = refs[:-1], refs[-1]
    step = pl.program_id(0)
    width = wk_ref.shape[1]

    @pl.when(step == 0)
    def _():
        acc_ref[...] = jnp.zeros_like(acc_ref)

    hidden = hidden_ref[...]
    acc_ref[:, :width] += jnp.dot(hidden, wk_ref[...], preferred_element_type=jnp.float32)
    acc_ref[:, width:] += jnp.dot(hidden, wv_ref[...], preferred_element_type=jnp.float32)

    @pl.when(step == pl.num_programs(0) - 1)
    def _():
        for head, out in enumerate(outs):
            cols = slice(head * HEAD_SIZE, (head + 1) * HEAD_SIZE)
            out[:, :HEAD_SIZE] = acc_ref[:, cols].astype(out.dtype)
            cols = slice(width + head * HEAD_SIZE, width + (head + 1) * HEAD_SIZE)
            out[:, HEAD_SIZE:] = acc_ref[:, cols].astype(out.dtype)


def project_keys_values(hidden, wk, wv):
    rows, depth = hidden.shape
    width = wk.shape[1]
    heads = width // HEAD_SIZE
    tile = 896
    return pl.pallas_call(
        project_kernel,
        grid=(depth // tile,),
        in_specs=[
            pl.BlockSpec((rows, tile), lambda k: (0, k)),
            pl.BlockSpec((tile, width), lambda k: (k, 0)),
            pl.BlockSpec((tile, width), lambda k: (k, 0)),
        ],
        out_specs=[pl.BlockSpec((rows, 2 * HEAD_SIZE), lambda k: (0, 0))] * heads,
        out_shape=[jax.ShapeDtypeStruct((rows, 2 * HEAD_SIZE), jnp.bfloat16)] * heads,
        scratch_shapes=[pltpu.VMEM((rows, 2 * width), jnp.float32)],
        compiler_params=pltpu.CompilerParams(vmem_limit_bytes=VMEM_LIMIT),
        cost_estimate=pl.CostEstimate(
            flops=4 * rows * depth * width,
            bytes_accessed=2 * (rows * depth + 2 * depth * width),
            transcendentals=0,
        ),
        name="project_kv",
    )(hidden, wk, wv)


def attention_kernel(
    q_ref, do_ref, far_ref, near_ref, own_ref, low_ref,
    dq_ref, gfar_ref, gnear_ref, gown_ref,
    k_ref, v_ref, dkt_ref, dvt_ref,
):
    rows = q_ref.shape[0]
    window = W + BLOCK
    for at, ref in enumerate((far_ref, near_ref, own_ref)):
        k_ref[at * rows : (at + 1) * rows, :] = ref[:, :HEAD_SIZE]
        v_ref[at * rows : (at + 1) * rows, :] = ref[:, HEAD_SIZE:]
    dkt_ref[...] = jnp.zeros_like(dkt_ref)
    dvt_ref[...] = jnp.zeros_like(dvt_ref)
    for block in range(rows // BLOCK):
        at = slice(block * BLOCK, (block + 1) * BLOCK)
        span = slice(block * BLOCK, block * BLOCK + window)
        q = jnp.concatenate([q_ref[at, :HEAD_SIZE], q_ref[at, HEAD_SIZE:]], axis=0)
        do = jnp.concatenate([do_ref[at, :HEAD_SIZE], do_ref[at, HEAD_SIZE:]], axis=0)
        k = k_ref[span, :]
        v = v_ref[span, :]
        low = low_ref[at, :]
        low = jnp.concatenate([low, low], axis=0) - block * BLOCK
        scores = lax.dot_general(q, k, NT, preferred_element_type=jnp.float32)
        col = lax.broadcasted_iota(jnp.int32, scores.shape, 1)
        row = lax.broadcasted_iota(jnp.int32, scores.shape, 0) & (BLOCK - 1)
        allowed = (col >= low) & (col <= row + W)
        scores = jnp.where(allowed, scores * (SCALE * LOG2E), MASKED)
        top = jnp.max(scores, axis=1, keepdims=True)
        e = jnp.exp2(scores - top)
        inverse = 1.0 / jnp.sum(e, axis=1, keepdims=True)
        probability = e * inverse
        probability_low = probability.astype(jnp.bfloat16)
        d_probs = lax.dot_general(do, v, NT, preferred_element_type=jnp.float32)
        row_dot = jnp.sum(
            probability_low.astype(jnp.float32) * d_probs, axis=1, keepdims=True
        )
        d_scores = (probability * ((d_probs - row_dot) * SCALE)).astype(jnp.bfloat16)
        dq = jnp.dot(d_scores, k, preferred_element_type=jnp.float32).astype(dq_ref.dtype)
        dq_ref[at, :HEAD_SIZE] = dq[:BLOCK]
        dq_ref[at, HEAD_SIZE:] = dq[BLOCK:]
        dkt_ref[:, span] += jnp.dot(q.T, d_scores, preferred_element_type=jnp.float32)
        dvt_ref[:, span] += jnp.dot(do.T, probability_low, preferred_element_type=jnp.float32)
    for at, ref in enumerate((gfar_ref, gnear_ref, gown_ref)):
        part = slice(at * rows, (at + 1) * rows)
        ref[:, :HEAD_SIZE] = dkt_ref[:, part].T.astype(ref.dtype)
        ref[:, HEAD_SIZE:] = dvt_ref[:, part].T.astype(ref.dtype)


def attend(head, queries, cotangent, far, near, own, low):
    rows = queries.shape[0]
    pair = 2 * HEAD_SIZE
    covered = (HALO + 1) * rows
    whole = pl.BlockSpec((rows, pair), lambda i: (0, 0))
    column = pl.BlockSpec((rows, pair), lambda i: (0, head))
    work = 2 * rows * (W + BLOCK) * HEAD_SIZE
    return pl.pallas_call(
        attention_kernel,
        grid=(1,),
        in_specs=[column, column, whole, whole, whole, pl.BlockSpec((rows, 1), lambda i: (0, 0))],
        out_specs=[whole] * 4,
        out_shape=[
            jax.ShapeDtypeStruct((rows, pair), jnp.bfloat16),
            jax.ShapeDtypeStruct((rows, pair), jnp.bfloat16),
            jax.ShapeDtypeStruct((rows, pair), jnp.bfloat16),
            jax.ShapeDtypeStruct((rows, pair), jnp.float32),
        ],
        scratch_shapes=[
            pltpu.VMEM((covered, HEAD_SIZE), jnp.bfloat16),
            pltpu.VMEM((covered, HEAD_SIZE), jnp.bfloat16),
            pltpu.VMEM((HEAD_SIZE, covered), jnp.float32),
            pltpu.VMEM((HEAD_SIZE, covered), jnp.float32),
        ],
        compiler_params=pltpu.CompilerParams(vmem_limit_bytes=VMEM_LIMIT),
        cost_estimate=pl.CostEstimate(
            flops=16 * work, bytes_accessed=16 * rows * pair, transcendentals=work // HEAD_SIZE
        ),
        name="attention",
    )(queries, cotangent, far, near, own, low)


def back_kernel(dq0_ref, dq1_ref, g0_ref, g1_ref, wq_ref, wk_ref, wv_ref, out_ref):
    def nt(x, w):
        return lax.dot_general(x, w, NT, preferred_element_type=jnp.float32)

    pair = 2 * HEAD_SIZE
    total = nt(dq0_ref[...], wq_ref[:, :pair]) + nt(dq1_ref[...], wq_ref[:, pair:])
    dk = jnp.concatenate([g0_ref[:, :HEAD_SIZE], g1_ref[:, :HEAD_SIZE]], axis=1)
    dv = jnp.concatenate([g0_ref[:, HEAD_SIZE:], g1_ref[:, HEAD_SIZE:]], axis=1)
    out_ref[...] = (total + nt(dk, wk_ref[...]) + nt(dv, wv_ref[...])).astype(out_ref.dtype)


def back_project(dq0, dq1, g0, g1, wq, wk, wv, part, parts):
    rows = dq0.shape[0]
    pair = 2 * HEAD_SIZE
    columns = wq.shape[0] // parts
    tile = columns // 2
    first = part * 2
    whole = pl.BlockSpec((rows, pair), lambda j: (0, 0))
    return pl.pallas_call(
        back_kernel,
        grid=(columns // tile,),
        in_specs=[whole] * 4
        + [pl.BlockSpec((tile, w.shape[1]), lambda j: (first + j, 0)) for w in (wq, wk, wv)],
        out_specs=pl.BlockSpec((rows, tile), lambda j: (0, j)),
        out_shape=jax.ShapeDtypeStruct((rows, columns), jnp.bfloat16),
        compiler_params=pltpu.CompilerParams(vmem_limit_bytes=VMEM_LIMIT),
        cost_estimate=pl.CostEstimate(
            flops=8 * rows * columns * pair,
            bytes_accessed=2 * columns * (4 * pair + rows),
            transcendentals=0,
        ),
        name="back_project",
    )(dq0, dq1, g0, g1, wq, wk, wv)


def shards(hidden, w_query, w_key, w_value, cotangent, doc_start):
    rows = hidden.shape[0]
    contexts = lax.axis_size("ctx")
    planes = lax.axis_size("head")
    ctx = lax.axis_index("ctx")
    plane = lax.axis_index("head")
    odd = (ctx % 2) == 1
    heads = w_key.shape[1] // HEAD_SIZE
    swap = [(i, i ^ 1) for i in range(contexts)]
    ahead = [(i, i + 2) for i in range(contexts - 2)]
    behind = [(i + 2, i) for i in range(contexts - 2)]

    low = jnp.maximum(
        doc_start - ctx * rows + HALO * rows,
        jnp.arange(rows, dtype=jnp.int32) + (HALO * rows - W + 1),
    ).reshape(rows, 1)
    own = project_keys_values(hidden, w_key, w_value)
    far = [lax.ppermute(x, "ctx", ahead) for x in own]
    queries = jnp.dot(hidden, w_query, preferred_element_type=jnp.float32).astype(jnp.bfloat16)
    d_queries, gradients = [], []
    for h in range(heads):
        near = lax.ppermute(jnp.where(odd, far[h], own[h]), "ctx", swap)
        dq, gfar, gnear, gown = attend(h, queries, cotangent, far[h], near, own[h], low)
        swapped = lax.ppermute(gnear, "ctx", swap)
        passed = jnp.where(odd, gfar + swapped, gfar)
        returned = lax.ppermute(passed, "ctx", behind)
        total = gown + returned.astype(jnp.float32)
        total = total + jnp.where(odd, 0.0, swapped.astype(jnp.float32))
        d_queries.append(dq)
        gradients.append(total.astype(jnp.bfloat16))

    parts = 3
    chunk = rows // planes
    finished = []
    for part in range(parts):
        mine = back_project(*d_queries, *gradients, w_query, w_key, w_value, part, parts)

        def take(index):
            index = jnp.clip(index, 0, planes - 1)
            return lax.dynamic_slice_in_dim(mine, index * chunk, chunk, 0)

        right = left = None
        for step in range(planes - 1):
            rightward = take(planes - 1 - step + plane)
            leftward = take(step + plane - (planes - 1))
            if step > 0:
                rightward = (rightward.astype(jnp.float32) + right).astype(jnp.bfloat16)
                leftward = (leftward.astype(jnp.float32) + left).astype(jnp.bfloat16)
            right = lax.ppermute(
                rightward, "head", [(i, i + 1) for i in range(step + 1)]
            ).astype(jnp.float32)
            left = lax.ppermute(
                leftward, "head", [(planes - 1 - i, planes - 2 - i) for i in range(step + 1)]
            ).astype(jnp.float32)
        finished.append(take(plane).astype(jnp.float32) + right + left)
    return jnp.concatenate(finished, axis=1)


def solution(mesh):
    in_specs = (
        P("ctx", None),
        P(None, "head"),
        P(None, "head"),
        P(None, "head"),
        P("ctx", "head"),
        P("ctx"),
    )
    out_specs = P(("ctx", "head"), None)
    return jax.shard_map(shards, mesh=mesh, in_specs=in_specs, out_specs=out_specs, check_vma=False)
```

time: 328 us -> 176 us (0.54)
  waiting for transfers between devices: 221 us -> 80.2 us
  matrix products: 59.1 us -> 5.56 us
  starting transfers between devices: 11 us -> 45.6 us
  Pallas kernels: 0 us -> 29.3 us
  between operations: 13.8 us -> 0.52 us
  local copies, waits for them, and re-layouts: 10.5 us -> 5.5 us
    reduce_scatter x1 -> x0, waiting for transfers between devices: 188 us -> none  [shards(): lax.psum_scatter(contribution + back_project(value_gradient_rows, value_w...]
    dot_general x11 -> x0, matrix products: 55.3 us -> none  [the longest x3 19.8 us: back_project(): lax.dot_general(grad, weight, (((1,), (1,)), ((), ())), preferred_element...]
    ppermute x4 -> x26, waiting for transfers between devices: 32.7 us -> 80.2 us  [the longest x9 35.9 us: shards(): lax.ppermute(rightward, 'head', [(i, i + 1) for i in range(step + 1)])]
    ppermute x4 -> x26, starting transfers between devices: 11 us -> 45.6 us  [the longest x9 23.3 us: shards(): lax.ppermute(rightward, 'head', [(i, i + 1) for i in range(step + 1)])]
    pallas_call x0 -> x6, Pallas kernels: none -> 29.3 us  [the longest x3 12.1 us: back_project(): pl.pallas_call(back_kernel, grid=(columns // tile,), in_specs=[whole] * 4...]
    convert_element_type x0 -> x11, other arithmetic: none -> 3.92 us  [the longest x2 2.49 us: shards(): gradients.append(total.astype(jnp.bfloat16))]
    unnamed x4 -> x0, other arithmetic: 3.49 us -> none
    unnamed x45 -> x18, local copies, waits for them, and re-layouts: 6.56 us -> 5.15 us
  transfers between devices with their start and end apart: 5 -> 26, of which waited for: 5 -> 14; matrix products, arithmetic and copies ran while one was open for 3% -> 6% of each run, Pallas kernels for 0% -> 8%
where the time goes in v1:
time: 176 us; the launch traced here: 175 us
  waiting for transfers between devices  80.2 us (46%)
  starting transfers between devices  45.6 us (26%)
  Pallas kernels  29.3 us (17%)
  other arithmetic  8.46 us (5%)
  matrix products  5.56 us (3%)
  local copies, waits for them, and re-layouts  5.5 us (3%)
    ppermute x9, waiting for transfers between devices, shards(): lax.ppermute(rightward, 'head', [(i, i + 1) for i in range(step + 1)])  35.9 us
    ppermute x9, waiting for transfers between devices, shards(): lax.ppermute(leftward, 'head', [(planes - 1 - i, planes - 2 - i) for i in...  29 us
    ppermute x9, starting transfers between devices, shards(): lax.ppermute(rightward, 'head', [(i, i + 1) for i in range(step + 1)])  23.3 us
    pallas_call x3, Pallas kernels, back_project(): pl.pallas_call(back_kernel, grid=(columns // tile,), in_specs=[whole] * 4...  12.1 us
    ppermute x9, starting transfers between devices, shards(): lax.ppermute(leftward, 'head', [(planes - 1 - i, planes - 2 - i) for i in...  11.7 us
    pallas_call x2, Pallas kernels, attend(): pl.pallas_call(attention_kernel, grid=(1,), in_specs=[column, column, who...  10.4 us
    ppermute x2, waiting for transfers between devices, shards(): returned = lax.ppermute(passed, 'ctx', behind)  9.92 us
    pallas_call x1, Pallas kernels, project_keys_values(): pl.pallas_call(project_kernel, grid=(depth // tile,), in_specs=[pl.BlockS...  6.86 us
  transfers between devices with their start and end apart: 26, of which 14 were waited for; matrix products, arithmetic and copies ran while one was open for 6% of the time, Pallas kernels for 8%

profile of v1, /device:TPU:12, one launch (start us, length us, event | category | flops | bytes accessed | tf_op | source)
XLA Modules:
  0.0 175.2 jit_solution(17119938568227204221)
XLA Ops:
  0.0 1.8 %copy-done = bf16[5376,256]{1,0:T(8,128)(2,1)S(1)} copy-done((bf16[5376,256]{1,0:T(8,128)(2,1)S(1)}, bf16[5376,256]{1,0:T(8,128)(2,1)}, u32[]{:S(2)}) %copy-start) | copy-done | bytes 2752536
  1.8 1.8 %copy-done.2 = bf16[5376,256]{1,0:T(8,128)(2,1)S(1)} copy-done((bf16[5376,256]{1,0:T(8,128)(2,1)S(1)}, bf16[5376,256]{1,0:T(8,128)(2,1)}, u32[]{:S(2)}) %copy-start.2) | copy-done | bytes 2752536
  3.6 6.9 %project_kv.1 = (bf16[512,256]{1,0:T(8,128)(2,1)S(1)}, bf16[512,256]{1,0:T(8,128)(2,1)S(1)}) custom-call(bf16[512,5376]{1,0:T(8,128)(2,1)} %hidden_ref.1, bf16[5376,256]{1,0:T(8,128)(2,1)S(1)} %copy-done, bf16[5376,256]{1,0:T(8,128)(2,1)S(1)} %copy-done.2), custom_call_target="tpu_custom_call" | custom-call | flops 2818572288 | bytes 11010048 | tf_op jit(solution)/shard_map/project_kv/pallas_call | solution.py:49
  10.4 3.4 %collective-permute-start.2 = (bf16[512,256]{1,0:T(8,128)(2,1)S(1)}, bf16[512,256]{1,0:T(8,128)(2,1)S(1)}, u32[]{:S(2)}, u32[]{:S(2)}) collective-permute-start(bf16[512,256]{1,0:T(8,128)(2,1)S(1)} %get-tuple-element.17.own_ref), channel_id=1, source_target_pairs={{0,8},{4,12},{8,16},{12,20},{16,24},{20,28},{1,9},{5,13},{9,17},{1... | collective-permute-start | bytes 786440 | tf_op jit(solution)/shard_map/ppermute | solution.py:201
  13.8 1.9 %collective-permute-start = (bf16[512,256]{1,0:T(8,128)(2,1)S(1)}, bf16[512,256]{1,0:T(8,128)(2,1)S(1)}, u32[]{:S(2)}, u32[]{:S(2)}) collective-permute-start(bf16[512,256]{1,0:T(8,128)(2,1)S(1)} %get-tuple-element.15.own_ref), channel_id=1, source_target_pairs={{0,8},{4,12},{8,16},{12,20},{16,24},{20,28},{1,9},{5,13},{9,17},{1... | collective-permute-start | bytes 786440 | tf_op jit(solution)/shard_map/ppermute | solution.py:201
  15.8 5.6 %convolution_convert_fusion.q_ref = bf16[512,512]{1,0:T(8,128)(2,1)S(1)} fusion(bf16[512,5376]{1,0:T(8,128)(2,1)} %hidden_ref.1, bf16[5376,512]{1,0:T(8,128)(2,1)S(1)} %copy-done.6), kind=kOutput, calls=%fused_computation.1 | convolution fusion | flops 2818834432 | bytes 11534336 | tf_op jit(solution)/shard_map/dot_general | solution.py:202
  21.4 1.0 collective-permute-done.2.far_ref
  22.5 4.4 %collective-permute-done.far_ref = bf16[512,256]{1,0:T(8,128)(2,1)S(1)} collective-permute-done((bf16[512,256]{1,0:T(8,128)(2,1)S(1)}, bf16[512,256]{1,0:T(8,128)(2,1)S(1)}, u32[]{:S(2)}, u32[]{:S(2)}) %collective-permute-start) | collective-permute-done | bytes 262176 | tf_op jit(solution)/shard_map/ppermute | solution.py:201
  26.9 0.7 broadcast_select_fusion.1
  27.6 0.1 copy.7.low_ref
  27.8 5.2 %attention.3 = (bf16[512,256]{1,0:T(8,128)(2,1)S(1)}, bf16[512,256]{1,0:T(8,128)(2,1)S(1)}, bf16[512,256]{1,0:T(8,128)(2,1)S(1)}, f32[512,256]{1,0:T(8,128)S(1)}) custom-call(bf16[512,512]{1,0:T(8,128)(2,1)S(1)} %convolution_convert_fusion.q_ref, bf16[512,512]{1,0:T(8,128)(2,1)S(1)} %copy-done.5, bf16[512,256]{1,0:T(8,128)(2,1)S(1)} %collective-permute-done.2.far_ref, ...), custom_call_target="tpu_custom_call" | custom-call | flops 2415919104 | bytes 2097152 | tf_op jit(solution)/shard_map/attention/pallas_call | solution.py:124
  33.0 0.8 copy-done.3
  33.8 0.5 collective-permute-start.6
  34.3 5.2 %attention.2 = (bf16[512,256]{1,0:T(8,128)(2,1)S(1)}, bf16[512,256]{1,0:T(8,128)(2,1)S(1)}, bf16[512,256]{1,0:T(8,128)(2,1)S(1)}, f32[512,256]{1,0:T(8,128)S(1)}) custom-call(bf16[512,512]{1,0:T(8,128)(2,1)S(1)} %convolution_convert_fusion.q_ref, bf16[512,512]{1,0:T(8,128)(2,1)S(1)} %copy-done.5, bf16[512,256]{1,0:T(8,128)(2,1)S(1)} %collective-permute-done.far_ref, ...), custom_call_target="tpu_custom_call" | custom-call | flops 2415919104 | bytes 2097152 | tf_op jit(solution)/shard_map/attention/pallas_call | solution.py:124
  39.5 0.8 copy-done.4
  40.3 0.7 add_select_fusion
  41.1 2.9 %collective-permute-start.7 = (bf16[512,256]{1,0:T(8,128)(2,1)}, bf16[512,256]{1,0:T(8,128)(2,1)}, u32[]{:S(2)}, u32[]{:S(2)}) collective-permute-start(bf16[512,256]{1,0:T(8,128)(2,1)} %add_select_fusion), channel_id=1, source_target_pairs={{8,0},{12,4},{16,8},{20,12},{24,16},{28,20},{9,1},{13,5},{17,9},{2... | collective-permute-start | bytes 786440 | tf_op jit(solution)/shard_map/ppermute | solution.py:209
  44.0 0.8 add_select_fusion.1
  44.8 1.9 %collective-permute-start.5 = (bf16[512,256]{1,0:T(8,128)(2,1)}, bf16[512,256]{1,0:T(8,128)(2,1)}, u32[]{:S(2)}, u32[]{:S(2)}) collective-permute-start(bf16[512,256]{1,0:T(8,128)(2,1)} %add_select_fusion.1), channel_id=1, source_target_pairs={{8,0},{12,4},{16,8},{20,12},{24,16},{28,20},{9,1},{13,5},{17,9},{2... | collective-permute-start | bytes 786440 | tf_op jit(solution)/shard_map/ppermute | solution.py:209
  46.7 5.9 %collective-permute-done.7 = bf16[512,256]{1,0:T(8,128)(2,1)} collective-permute-done((bf16[512,256]{1,0:T(8,128)(2,1)}, bf16[512,256]{1,0:T(8,128)(2,1)}, u32[]{:S(2)}, u32[]{:S(2)}) %collective-permute-start.7) | collective-permute-done | bytes 262176 | tf_op jit(solution)/shard_map/ppermute | solution.py:209
  52.6 1.2 add_convert_fusion.12.g1_ref
  53.8 4.0 %collective-permute-done.5 = bf16[512,256]{1,0:T(8,128)(2,1)} collective-permute-done((bf16[512,256]{1,0:T(8,128)(2,1)}, bf16[512,256]{1,0:T(8,128)(2,1)}, u32[]{:S(2)}, u32[]{:S(2)}) %collective-permute-start.5) | collective-permute-done | bytes 262176 | tf_op jit(solution)/shard_map/ppermute | solution.py:209
  57.8 1.3 add_convert_fusion.13.g0_ref
  59.1 4.0 %back_project.3 = bf16[512,1792]{1,0:T(8,128)(2,1)S(1)} custom-call(bf16[512,256]{1,0:T(8,128)(2,1)S(1)} %get-tuple-element.16.dq0_ref, bf16[512,256]{1,0:T(8,128)(2,1)S(1)} %get-tuple-element.18.dq1_ref, bf16[512,256]{1,0:T(8,128)(2,1)S(1)} %add_convert_fusion.13.g0_ref, bf16[512,256]{1,0:T(8,128)(2,1)S(1)} %add_convert_fusion.12.g1_ref, ...), custom_call_target="tpu_custom_call" | custom-call | flops 1879048192 | bytes 5505024 | tf_op jit(solution)/shard_map/back_project/pallas_call | solution.py:167
  63.2 4.0 %back_project.4 = bf16[512,1792]{1,0:T(8,128)(2,1)S(1)} custom-call(bf16[512,256]{1,0:T(8,128)(2,1)S(1)} %get-tuple-element.16.dq0_ref, bf16[512,256]{1,0:T(8,128)(2,1)S(1)} %get-tuple-element.18.dq1_ref, bf16[512,256]{1,0:T(8,128)(2,1)S(1)} %add_convert_fusion.13.g0_ref, bf16[512,256]{1,0:T(8,128)(2,1)S(1)} %add_convert_fusion.12.g1_ref, ...), custom_call_target="tpu_custom_call" | custom-call | flops 1879048192 | bytes 5505024 | tf_op jit(solution)/shard_map/back_project/pallas_call | solution.py:167
  67.3 1.3 collective-permute-start.8
  68.6 0.7 collective-permute-start.11
  69.4 1.3 collective-permute-start.14
  70.7 0.7 collective-permute-start.17
  71.4 4.0 %back_project.5 = bf16[512,1792]{1,0:T(8,128)(2,1)S(1)} custom-call(bf16[512,256]{1,0:T(8,128)(2,1)S(1)} %get-tuple-element.16.dq0_ref, bf16[512,256]{1,0:T(8,128)(2,1)S(1)} %get-tuple-element.18.dq1_ref, bf16[512,256]{1,0:T(8,128)(2,1)S(1)} %add_convert_fusion.13.g0_ref, bf16[512,256]{1,0:T(8,128)(2,1)S(1)} %add_convert_fusion.12.g1_ref, ...), custom_call_target="tpu_custom_call" | custom-call | flops 1879048192 | bytes 5505024 | tf_op jit(solution)/shard_map/back_project/pallas_call | solution.py:167
  75.5 1.3 collective-permute-start.20
  76.8 5.8 %collective-permute-done.8 = bf16[128,1792]{1,0:T(8,128)(2,1)S(1)} collective-permute-done((bf16[128,1792]{1,0:T(8,128)(2,1)S(1)}, bf16[128,1792]{1,0:T(8,128)(2,1)S(1)}, u32[]{:S(2)}, u32[]{:S(2)}) %collective-permute-start.8) | collective-permute-done | bytes 458784 | tf_op jit(solution)/shard_map/ppermute | solution.py:232
  82.6 0.7 collective-permute-start.23
  83.3 0.1 add_convert_fusion.11
  83.4 9.0 %collective-permute-done.14 = bf16[128,1792]{1,0:T(8,128)(2,1)S(1)} collective-permute-done((bf16[128,1792]{1,0:T(8,128)(2,1)S(1)}, bf16[128,1792]{1,0:T(8,128)(2,1)S(1)}, u32[]{:S(2)}, u32[]{:S(2)}) %collective-permute-start.14) | collective-permute-done | bytes 458784 | tf_op jit(solution)/shard_map/ppermute | solution.py:232
  92.4 1.9 %collective-permute-start.9 = (bf16[128,1792]{1,0:T(8,128)(2,1)S(1)}, bf16[128,1792]{1,0:T(8,128)(2,1)S(1)}, u32[]{:S(2)}, u32[]{:S(2)}) collective-permute-start(bf16[128,1792]{1,0:T(8,128)(2,1)S(1)} %add_convert_fusion.11), channel_id=1, source_target_pairs={{0,1},{1,2},{4,5},{5,6},{8,9},{9,10},{12,13},{13,14},{16,17},{17,1... | collective-permute-start | bytes 1376264 | tf_op jit(solution)/shard_map/ppermute | solution.py:232
  94.5 7.8 %collective-permute-done.20 = bf16[128,1792]{1,0:T(8,128)(2,1)S(1)} collective-permute-done((bf16[128,1792]{1,0:T(8,128)(2,1)S(1)}, bf16[128,1792]{1,0:T(8,128)(2,1)S(1)}, u32[]{:S(2)}, u32[]{:S(2)}) %collective-permute-start.20) | collective-permute-done | bytes 458784 | tf_op jit(solution)/shard_map/ppermute | solution.py:232
  102.3 1.9 %collective-permute-start.15 = (bf16[128,1792]{1,0:T(8,128)(2,1)S(1)}, bf16[128,1792]{1,0:T(8,128)(2,1)S(1)}, u32[]{:S(2)}, u32[]{:S(2)}) collective-permute-start(bf16[128,1792]{1,0:T(8,128)(2,1)S(1)} %add_convert_fusion.7), channel_id=1, source_target_pairs={{0,1},{1,2},{4,5},{5,6},{8,9},{9,10},{12,13},{13,14},{16,17},{17,1... | collective-permute-start | bytes 1376264 | tf_op jit(solution)/shard_map/ppermute | solution.py:232
  104.2 0.1 add_convert_fusion.3
  104.3 1.9 %collective-permute-start.21 = (bf16[128,1792]{1,0:T(8,128)(2,1)S(1)}, bf16[128,1792]{1,0:T(8,128)(2,1)S(1)}, u32[]{:S(2)}, u32[]{:S(2)}) collective-permute-start(bf16[128,1792]{1,0:T(8,128)(2,1)S(1)} %add_convert_fusion.3), channel_id=1, source_target_pairs={{0,1},{1,2},{4,5},{5,6},{8,9},{9,10},{12,13},{13,14},{16,17},{17,1... | collective-permute-start | bytes 1376264 | tf_op jit(solution)/shard_map/ppermute | solution.py:232
  106.3 5.8 %collective-permute-done.9 = bf16[128,1792]{1,0:T(8,128)(2,1)S(1)} collective-permute-done((bf16[128,1792]{1,0:T(8,128)(2,1)S(1)}, bf16[128,1792]{1,0:T(8,128)(2,1)S(1)}, u32[]{:S(2)}, u32[]{:S(2)}) %collective-permute-start.9) | collective-permute-done | bytes 458784 | tf_op jit(solution)/shard_map/ppermute | solution.py:232
  112.1 0.2 add_convert_fusion.10
  112.3 1.3 collective-permute-start.12
  113.6 4.6 %collective-permute-start.10 = (bf16[128,1792]{1,0:T(8,128)(2,1)S(1)}, bf16[128,1792]{1,0:T(8,128)(2,1)S(1)}, u32[]{:S(2)}, u32[]{:S(2)}) collective-permute-start(bf16[128,1792]{1,0:T(8,128)(2,1)S(1)} %get-tuple-element.25), channel_id=1, source_target_pairs={{0,1},{1,2},{2,3},{4,5},{5,6},{6,7},{8,9},{9,10},{10,11},{12,13},{... | collective-permute-start | bytes 1376264 | tf_op jit(solution)/shard_map/ppermute | solution.py:232
  118.2 3.7 %collective-permute-done.15 = bf16[128,1792]{1,0:T(8,128)(2,1)S(1)} collective-permute-done((bf16[128,1792]{1,0:T(8,128)(2,1)S(1)}, bf16[128,1792]{1,0:T(8,128)(2,1)S(1)}, u32[]{:S(2)}, u32[]{:S(2)}) %collective-permute-start.15) | collective-permute-done | bytes 458784 | tf_op jit(solution)/shard_map/ppermute | solution.py:232
  121.9 0.2 add_convert_fusion.6
  122.2 1.3 collective-permute-start.18
  123.5 4.6 %collective-permute-start.16 = (bf16[128,1792]{1,0:T(8,128)(2,1)S(1)}, bf16[128,1792]{1,0:T(8,128)(2,1)S(1)}, u32[]{:S(2)}, u32[]{:S(2)}) collective-permute-start(bf16[128,1792]{1,0:T(8,128)(2,1)S(1)} %get-tuple-element.29), channel_id=1, source_target_pairs={{0,1},{1,2},{2,3},{4,5},{5,6},{6,7},{8,9},{9,10},{10,11},{12,13},{... | collective-permute-start | bytes 1376264 | tf_op jit(solution)/shard_map/ppermute | solution.py:232
  128.0 3.7 %collective-permute-done.21 = bf16[128,1792]{1,0:T(8,128)(2,1)S(1)} collective-permute-done((bf16[128,1792]{1,0:T(8,128)(2,1)S(1)}, bf16[128,1792]{1,0:T(8,128)(2,1)S(1)}, u32[]{:S(2)}, u32[]{:S(2)}) %collective-permute-start.21) | collective-permute-done | bytes 458784 | tf_op jit(solution)/shard_map/ppermute | solution.py:232
  131.8 0.2 add_convert_fusion.2
  132.0 1.3 collective-permute-start.24
  133.3 4.6 %collective-permute-start.22 = (bf16[128,1792]{1,0:T(8,128)(2,1)S(1)}, bf16[128,1792]{1,0:T(8,128)(2,1)S(1)}, u32[]{:S(2)}, u32[]{:S(2)}) collective-permute-start(bf16[128,1792]{1,0:T(8,128)(2,1)S(1)} %get-tuple-element.33), channel_id=1, source_target_pairs={{0,1},{1,2},{2,3},{4,5},{5,6},{6,7},{8,9},{9,10},{10,11},{12,13},{... | collective-permute-start | bytes 1376264 | tf_op jit(solution)/shard_map/ppermute | solution.py:232
  138.0 1.9 %collective-permute-start.13 = (bf16[128,1792]{1,0:T(8,128)(2,1)S(1)}, bf16[128,1792]{1,0:T(8,128)(2,1)S(1)}, u32[]{:S(2)}, u32[]{:S(2)}) collective-permute-start(bf16[128,1792]{1,0:T(8,128)(2,1)S(1)} %add_convert_fusion.8), channel_id=1, source_target_pairs={{3,2},{2,1},{1,0},{7,6},{6,5},{5,4},{11,10},{10,9},{9,8},{15,14},{... | collective-permute-start | bytes 1376264 | tf_op jit(solution)/shard_map/ppermute | solution.py:235
  139.9 0.1 add_convert_fusion.4
  140.1 7.3 %collective-permute-done.24 = bf16[128,1792]{1,0:T(8,128)(2,1)S(1)} collective-permute-done((bf16[128,1792]{1,0:T(8,128)(2,1)S(1)}, bf16[128,1792]{1,0:T(8,128)(2,1)S(1)}, u32[]{:S(2)}, u32[]{:S(2)}) %collective-permute-start.24) | collective-permute-done | bytes 458784 | tf_op jit(solution)/shard_map/ppermute | solution.py:235
  147.4 1.9 %collective-permute-start.19 = (bf16[128,1792]{1,0:T(8,128)(2,1)S(1)}, bf16[128,1792]{1,0:T(8,128)(2,1)S(1)}, u32[]{:S(2)}, u32[]{:S(2)}) collective-permute-start(bf16[128,1792]{1,0:T(8,128)(2,1)S(1)} %add_convert_fusion.4), channel_id=1, source_target_pairs={{3,2},{2,1},{1,0},{7,6},{6,5},{5,4},{11,10},{10,9},{9,8},{15,14},{... | collective-permute-start | bytes 1376264 | tf_op jit(solution)/shard_map/ppermute | solution.py:235
  149.4 1.9 %collective-permute-start.25 = (bf16[128,1792]{1,0:T(8,128)(2,1)S(1)}, bf16[128,1792]{1,0:T(8,128)(2,1)S(1)}, u32[]{:S(2)}, u32[]{:S(2)}) collective-permute-start(bf16[128,1792]{1,0:T(8,128)(2,1)S(1)} %add_convert_fusion), channel_id=1, source_target_pairs={{3,2},{2,1},{1,0},{7,6},{6,5},{5,4},{11,10},{10,9},{9,8},{15,14},{... | collective-permute-start | bytes 1376264 | tf_op jit(solution)/shard_map/ppermute | solution.py:235
  151.3 5.9 %collective-permute-done.13 = bf16[128,1792]{1,0:T(8,128)(2,1)S(1)} collective-permute-done((bf16[128,1792]{1,0:T(8,128)(2,1)S(1)}, bf16[128,1792]{1,0:T(8,128)(2,1)S(1)}, u32[]{:S(2)}, u32[]{:S(2)}) %collective-permute-start.13) | collective-permute-done | bytes 458784 | tf_op jit(solution)/shard_map/ppermute | solution.py:235
  157.2 0.2 convert_add_fusion.2
  157.4 9.6 %collective-permute-done.19 = bf16[128,1792]{1,0:T(8,128)(2,1)S(1)} collective-permute-done((bf16[128,1792]{1,0:T(8,128)(2,1)S(1)}, bf16[128,1792]{1,0:T(8,128)(2,1)S(1)}, u32[]{:S(2)}, u32[]{:S(2)}) %collective-permute-start.19) | collective-permute-done | bytes 458784 | tf_op jit(solution)/shard_map/ppermute | solution.py:235
  167.0 0.2 convert_add_fusion.1
  167.2 6.2 %collective-permute-done.25 = bf16[128,1792]{1,0:T(8,128)(2,1)S(1)} collective-permute-done((bf16[128,1792]{1,0:T(8,128)(2,1)S(1)}, bf16[128,1792]{1,0:T(8,128)(2,1)S(1)}, u32[]{:S(2)}, u32[]{:S(2)}) %collective-permute-start.25) | collective-permute-done | bytes 458784 | tf_op jit(solution)/shard_map/ppermute | solution.py:235
  173.4 0.2 convert_add_fusion
  173.5 1.7 pad_maximum_fusion
  (37 shorter events, 0.7 us)
Async XLA Ops:
  0.0 1.8 %copy-start = (bf16[5376,256]{1,0:T(8,128)(2,1)S(1)}, bf16[5376,256]{1,0:T(8,128)(2,1)}, u32[]{:S(2)}) copy-start(bf16[5376,256]{1,0:T(8,128)(2,1)} %wk_ref.7) | copy-start | bytes 8257540
  1.8 1.8 %copy-start.2 = (bf16[5376,256]{1,0:T(8,128)(2,1)S(1)}, bf16[5376,256]{1,0:T(8,128)(2,1)}, u32[]{:S(2)}) copy-start(bf16[5376,256]{1,0:T(8,128)(2,1)} %wv_ref.7) | copy-start | bytes 8257540
  3.6 12.2 %copy-start.6 = (bf16[5376,512]{1,0:T(8,128)(2,1)S(1)}, bf16[5376,512]{1,0:T(8,128)(2,1)}, u32[]{:S(2)}) copy-start(bf16[5376,512]{1,0:T(8,128)(2,1)} %wq_ref.5) | copy-start | bytes 16515076
  10.4 12.0 %collective-permute-start.2 = (bf16[512,256]{1,0:T(8,128)(2,1)S(1)}, bf16[512,256]{1,0:T(8,128)(2,1)S(1)}, u32[]{:S(2)}, u32[]{:S(2)}) collective-permute-start(bf16[512,256]{1,0:T(8,128)(2,1)S(1)} %get-tuple-element.17.own_ref), channel_id=1, source_target_pairs={{0,8},{4,12},{8,16},{12,20},{16,24},{20,28},{1,9},{5,13},{9,17},{1... | collective-permute-start | bytes 786440 | tf_op jit(solution)/shard_map/ppermute | solution.py:201
  13.8 13.8 %copy-start.8 = (s32[512]{0:T(512)S(1)}, s32[512]{0:T(512)}, u32[]{:S(2)}) copy-start(s32[512]{0:T(512)} %param.11) | copy-start | bytes 6148
  13.8 13.0 %collective-permute-start = (bf16[512,256]{1,0:T(8,128)(2,1)S(1)}, bf16[512,256]{1,0:T(8,128)(2,1)S(1)}, u32[]{:S(2)}, u32[]{:S(2)}) collective-permute-start(bf16[512,256]{1,0:T(8,128)(2,1)S(1)} %get-tuple-element.15.own_ref), channel_id=1, source_target_pairs={{0,8},{4,12},{8,16},{12,20},{16,24},{20,28},{1,9},{5,13},{9,17},{1... | collective-permute-start | bytes 786440 | tf_op jit(solution)/shard_map/ppermute | solution.py:201
  21.3 6.4 %copy-start.5 = (bf16[512,512]{1,0:T(8,128)(2,1)S(1)}, bf16[512,512]{1,0:T(8,128)(2,1)}, u32[]{:S(2)}) copy-start(bf16[512,512]{1,0:T(8,128)(2,1)} %do_ref.3) | copy-start | bytes 1572868
  22.4 5.3 %collective-permute-start.3 = (bf16[512,256]{1,0:T(8,128)(2,1)S(1)}, bf16[512,256]{1,0:T(8,128)(2,1)S(1)}, u32[]{:S(2)}, u32[]{:S(2)}) collective-permute-start(bf16[512,256]{1,0:T(8,128)(2,1)S(1)} %broadcast_select_fusion), channel_id=1, source_target_pairs={{0,4},{4,0},{8,12},{12,8},{16,20},{20,16},{24,28},{28,24},{1,5},{5... | collective-permute-start | bytes 786440 | tf_op jit(solution)/shard_map/ppermute | solution.py:205
  27.6 6.7 %collective-permute-start.1 = (bf16[512,256]{1,0:T(8,128)(2,1)}, bf16[512,256]{1,0:T(8,128)(2,1)S(1)}, u32[]{:S(2)}, u32[]{:S(2)}) collective-permute-start(bf16[512,256]{1,0:T(8,128)(2,1)} %broadcast_select_fusion.1), channel_id=1, source_target_pairs={{0,4},{4,0},{8,12},{12,8},{16,20},{20,16},{24,28},{28,24},{1,5},{5... | collective-permute-start | bytes 786440 | tf_op jit(solution)/shard_map/ppermute | solution.py:205
  33.0 0.8 copy-start.3
  33.8 6.5 %collective-permute-start.6 = (bf16[512,256]{1,0:T(8,128)(2,1)S(1)}, bf16[512,256]{1,0:T(8,128)(2,1)S(1)}, u32[]{:S(2)}, u32[]{:S(2)}) collective-permute-start(bf16[512,256]{1,0:T(8,128)(2,1)S(1)} %get-tuple-element.24), channel_id=1, source_target_pairs={{0,4},{4,0},{8,12},{12,8},{16,20},{20,16},{24,28},{28,24},{1,5},{5... | collective-permute-start | bytes 786440 | tf_op jit(solution)/shard_map/ppermute | solution.py:207
  39.5 0.8 copy-start.4
  40.3 3.6 %collective-permute-start.4 = (bf16[512,256]{1,0:T(8,128)(2,1)S(1)}, bf16[512,256]{1,0:T(8,128)(2,1)S(1)}, u32[]{:S(2)}, u32[]{:S(2)}) collective-permute-start(bf16[512,256]{1,0:T(8,128)(2,1)S(1)} %get-tuple-element.21), channel_id=1, source_target_pairs={{0,4},{4,0},{8,12},{12,8},{16,20},{20,16},{24,28},{28,24},{1,5},{5... | collective-permute-start | bytes 786440 | tf_op jit(solution)/shard_map/ppermute | solution.py:207
  41.1 18.1 %copy-start.1 = (bf16[5376,256]{1,0:T(8,128)(2,1)S(1)}, bf16[5376,256]{1,0:T(8,128)(2,1)}, u32[]{:S(2)}) copy-start(bf16[5376,256]{1,0:T(8,128)(2,1)} %wk_ref.7) | copy-start | bytes 8257540
  41.1 11.6 %collective-permute-start.7 = (bf16[512,256]{1,0:T(8,128)(2,1)}, bf16[512,256]{1,0:T(8,128)(2,1)}, u32[]{:S(2)}, u32[]{:S(2)}) collective-permute-start(bf16[512,256]{1,0:T(8,128)(2,1)} %add_select_fusion), channel_id=1, source_target_pairs={{8,0},{12,4},{16,8},{20,12},{24,16},{28,20},{9,1},{13,5},{17,9},{2... | collective-permute-start | bytes 786440 | tf_op jit(solution)/shard_map/ppermute | solution.py:209
  43.9 0.8 copy-start.7
  44.8 13.1 %collective-permute-start.5 = (bf16[512,256]{1,0:T(8,128)(2,1)}, bf16[512,256]{1,0:T(8,128)(2,1)}, u32[]{:S(2)}, u32[]{:S(2)}) collective-permute-start(bf16[512,256]{1,0:T(8,128)(2,1)} %add_select_fusion.1), channel_id=1, source_target_pairs={{8,0},{12,4},{16,8},{20,12},{24,16},{28,20},{9,1},{13,5},{17,9},{2... | collective-permute-start | bytes 786440 | tf_op jit(solution)/shard_map/ppermute | solution.py:209
  67.3 15.3 %collective-permute-start.8 = (bf16[128,1792]{1,0:T(8,128)(2,1)S(1)}, bf16[128,1792]{1,0:T(8,128)(2,1)S(1)}, u32[]{:S(2)}, u32[]{:S(2)}) collective-permute-start(bf16[128,1792]{1,0:T(8,128)(2,1)S(1)} %get-tuple-element.27), channel_id=1, source_target_pairs={{0,1},{4,5},{8,9},{12,13},{16,17},{20,21},{24,25},{28,29}} | collective-permute-start | bytes 1376264 | tf_op jit(solution)/shard_map/ppermute | solution.py:232
  68.6 35.7 %collective-permute-start.11 = (bf16[128,1792]{1,0:T(8,128)(2,1)S(1)}, bf16[128,1792]{1,0:T(8,128)(2,1)S(1)}, u32[]{:S(2)}, u32[]{:S(2)}) collective-permute-start(bf16[128,1792]{1,0:T(8,128)(2,1)S(1)} %get-tuple-element.28), channel_id=1, source_target_pairs={{3,2},{7,6},{11,10},{15,14},{19,18},{23,22},{27,26},{31,30}} | collective-permute-start | bytes 1376264 | tf_op jit(solution)/shard_map/ppermute | solution.py:235
  69.4 23.1 %collective-permute-start.14 = (bf16[128,1792]{1,0:T(8,128)(2,1)S(1)}, bf16[128,1792]{1,0:T(8,128)(2,1)S(1)}, u32[]{:S(2)}, u32[]{:S(2)}) collective-permute-start(bf16[128,1792]{1,0:T(8,128)(2,1)S(1)} %get-tuple-element.31), channel_id=1, source_target_pairs={{0,1},{4,5},{8,9},{12,13},{16,17},{20,21},{24,25},{28,29}} | collective-permute-start | bytes 1376264 | tf_op jit(solution)/shard_map/ppermute | solution.py:232
  70.7 43.0 %collective-permute-start.17 = (bf16[128,1792]{1,0:T(8,128)(2,1)S(1)}, bf16[128,1792]{1,0:T(8,128)(2,1)S(1)}, u32[]{:S(2)}, u32[]{:S(2)}) collective-permute-start(bf16[128,1792]{1,0:T(8,128)(2,1)S(1)} %get-tuple-element.32), channel_id=1, source_target_pairs={{3,2},{7,6},{11,10},{15,14},{19,18},{23,22},{27,26},{31,30}} | collective-permute-start | bytes 1376264 | tf_op jit(solution)/shard_map/ppermute | solution.py:235
  75.5 26.8 %collective-permute-start.20 = (bf16[128,1792]{1,0:T(8,128)(2,1)S(1)}, bf16[128,1792]{1,0:T(8,128)(2,1)S(1)}, u32[]{:S(2)}, u32[]{:S(2)}) collective-permute-start(bf16[128,1792]{1,0:T(8,128)(2,1)S(1)} %get-tuple-element.35), channel_id=1, source_target_pairs={{0,1},{4,5},{8,9},{12,13},{16,17},{20,21},{24,25},{28,29}} | collective-permute-start | bytes 1376264 | tf_op jit(solution)/shard_map/ppermute | solution.py:232
  82.6 40.9 %collective-permute-start.23 = (bf16[128,1792]{1,0:T(8,128)(2,1)S(1)}, bf16[128,1792]{1,0:T(8,128)(2,1)S(1)}, u32[]{:S(2)}, u32[]{:S(2)}) collective-permute-start(bf16[128,1792]{1,0:T(8,128)(2,1)S(1)} %get-tuple-element.36), channel_id=1, source_target_pairs={{3,2},{7,6},{11,10},{15,14},{19,18},{23,22},{27,26},{31,30}} | collective-permute-start | bytes 1376264 | tf_op jit(solution)/shard_map/ppermute | solution.py:235
  92.4 19.7 %collective-permute-start.9 = (bf16[128,1792]{1,0:T(8,128)(2,1)S(1)}, bf16[128,1792]{1,0:T(8,128)(2,1)S(1)}, u32[]{:S(2)}, u32[]{:S(2)}) collective-permute-start(bf16[128,1792]{1,0:T(8,128)(2,1)S(1)} %add_convert_fusion.11), channel_id=1, source_target_pairs={{0,1},{1,2},{4,5},{5,6},{8,9},{9,10},{12,13},{13,14},{16,17},{17,1... | collective-permute-start | bytes 1376264 | tf_op jit(solution)/shard_map/ppermute | solution.py:232
  102.3 19.7 %collective-permute-start.15 = (bf16[128,1792]{1,0:T(8,128)(2,1)S(1)}, bf16[128,1792]{1,0:T(8,128)(2,1)S(1)}, u32[]{:S(2)}, u32[]{:S(2)}) collective-permute-start(bf16[128,1792]{1,0:T(8,128)(2,1)S(1)} %add_convert_fusion.7), channel_id=1, source_target_pairs={{0,1},{1,2},{4,5},{5,6},{8,9},{9,10},{12,13},{13,14},{16,17},{17,1... | collective-permute-start | bytes 1376264 | tf_op jit(solution)/shard_map/ppermute | solution.py:232
  104.3 27.4 %collective-permute-start.21 = (bf16[128,1792]{1,0:T(8,128)(2,1)S(1)}, bf16[128,1792]{1,0:T(8,128)(2,1)S(1)}, u32[]{:S(2)}, u32[]{:S(2)}) collective-permute-start(bf16[128,1792]{1,0:T(8,128)(2,1)S(1)} %add_convert_fusion.3), channel_id=1, source_target_pairs={{0,1},{1,2},{4,5},{5,6},{8,9},{9,10},{12,13},{13,14},{16,17},{17,1... | collective-permute-start | bytes 1376264 | tf_op jit(solution)/shard_map/ppermute | solution.py:232
  112.3 21.0 %collective-permute-start.12 = (bf16[128,1792]{1,0:T(8,128)(2,1)S(1)}, bf16[128,1792]{1,0:T(8,128)(2,1)S(1)}, u32[]{:S(2)}, u32[]{:S(2)}) collective-permute-start(bf16[128,1792]{1,0:T(8,128)(2,1)S(1)} %get-tuple-element.26), channel_id=1, source_target_pairs={{3,2},{2,1},{7,6},{6,5},{11,10},{10,9},{15,14},{14,13},{19,18},{18... | collective-permute-start | bytes 1376264 | tf_op jit(solution)/shard_map/ppermute | solution.py:235
  113.6 35.8 %collective-permute-start.10 = (bf16[128,1792]{1,0:T(8,128)(2,1)S(1)}, bf16[128,1792]{1,0:T(8,128)(2,1)S(1)}, u32[]{:S(2)}, u32[]{:S(2)}) collective-permute-start(bf16[128,1792]{1,0:T(8,128)(2,1)S(1)} %get-tuple-element.25), channel_id=1, source_target_pairs={{0,1},{1,2},{2,3},{4,5},{5,6},{6,7},{8,9},{9,10},{10,11},{12,13},{... | collective-permute-start | bytes 1376264 | tf_op jit(solution)/shard_map/ppermute | solution.py:232
  122.2 15.8 %collective-permute-start.18 = (bf16[128,1792]{1,0:T(8,128)(2,1)S(1)}, bf16[128,1792]{1,0:T(8,128)(2,1)S(1)}, u32[]{:S(2)}, u32[]{:S(2)}) collective-permute-start(bf16[128,1792]{1,0:T(8,128)(2,1)S(1)} %get-tuple-element.30), channel_id=1, source_target_pairs={{3,2},{2,1},{7,6},{6,5},{11,10},{10,9},{15,14},{14,13},{19,18},{18... | collective-permute-start | bytes 1376264 | tf_op jit(solution)/shard_map/ppermute | solution.py:235
  123.5 33.9 %collective-permute-start.16 = (bf16[128,1792]{1,0:T(8,128)(2,1)S(1)}, bf16[128,1792]{1,0:T(8,128)(2,1)S(1)}, u32[]{:S(2)}, u32[]{:S(2)}) collective-permute-start(bf16[128,1792]{1,0:T(8,128)(2,1)S(1)} %get-tuple-element.29), channel_id=1, source_target_pairs={{0,1},{1,2},{2,3},{4,5},{5,6},{6,7},{8,9},{9,10},{10,11},{12,13},{... | collective-permute-start | bytes 1376264 | tf_op jit(solution)/shard_map/ppermute | solution.py:232
  132.0 15.3 %collective-permute-start.24 = (bf16[128,1792]{1,0:T(8,128)(2,1)S(1)}, bf16[128,1792]{1,0:T(8,128)(2,1)S(1)}, u32[]{:S(2)}, u32[]{:S(2)}) collective-permute-start(bf16[128,1792]{1,0:T(8,128)(2,1)S(1)} %get-tuple-element.34), channel_id=1, source_target_pairs={{3,2},{2,1},{7,6},{6,5},{11,10},{10,9},{15,14},{14,13},{19,18},{18... | collective-permute-start | bytes 1376264 | tf_op jit(solution)/shard_map/ppermute | solution.py:235
  133.3 33.9 %collective-permute-start.22 = (bf16[128,1792]{1,0:T(8,128)(2,1)S(1)}, bf16[128,1792]{1,0:T(8,128)(2,1)S(1)}, u32[]{:S(2)}, u32[]{:S(2)}) collective-permute-start(bf16[128,1792]{1,0:T(8,128)(2,1)S(1)} %get-tuple-element.33), channel_id=1, source_target_pairs={{0,1},{1,2},{2,3},{4,5},{5,6},{6,7},{8,9},{9,10},{10,11},{12,13},{... | collective-permute-start | bytes 1376264 | tf_op jit(solution)/shard_map/ppermute | solution.py:232
  138.0 19.2 %collective-permute-start.13 = (bf16[128,1792]{1,0:T(8,128)(2,1)S(1)}, bf16[128,1792]{1,0:T(8,128)(2,1)S(1)}, u32[]{:S(2)}, u32[]{:S(2)}) collective-permute-start(bf16[128,1792]{1,0:T(8,128)(2,1)S(1)} %add_convert_fusion.8), channel_id=1, source_target_pairs={{3,2},{2,1},{1,0},{7,6},{6,5},{5,4},{11,10},{10,9},{9,8},{15,14},{... | collective-permute-start | bytes 1376264 | tf_op jit(solution)/shard_map/ppermute | solution.py:235
  147.4 19.7 %collective-permute-start.19 = (bf16[128,1792]{1,0:T(8,128)(2,1)S(1)}, bf16[128,1792]{1,0:T(8,128)(2,1)S(1)}, u32[]{:S(2)}, u32[]{:S(2)}) collective-permute-start(bf16[128,1792]{1,0:T(8,128)(2,1)S(1)} %add_convert_fusion.4), channel_id=1, source_target_pairs={{3,2},{2,1},{1,0},{7,6},{6,5},{5,4},{11,10},{10,9},{9,8},{15,14},{... | collective-permute-start | bytes 1376264 | tf_op jit(solution)/shard_map/ppermute | solution.py:235
  149.4 24.0 %collective-permute-start.25 = (bf16[128,1792]{1,0:T(8,128)(2,1)S(1)}, bf16[128,1792]{1,0:T(8,128)(2,1)S(1)}, u32[]{:S(2)}, u32[]{:S(2)}) collective-permute-start(bf16[128,1792]{1,0:T(8,128)(2,1)S(1)} %add_convert_fusion), channel_id=1, source_target_pairs={{3,2},{2,1},{1,0},{7,6},{6,5},{5,4},{11,10},{10,9},{9,8},{15,14},{... | collective-permute-start | bytes 1376264 | tf_op jit(solution)/shard_map/ppermute | solution.py:235

commit v2 on v1

v2 whole, which is shorter than its diff:
```python
import functools

import jax
import jax.numpy as jnp
from jax import lax
from jax.experimental import pallas as pl
from jax.experimental.pallas import tpu as pltpu
from jax.sharding import PartitionSpec as P

HEAD_SIZE = 128
W = 1024
HALO = 2
SCALE = 168.0 ** (-0.5)
LOG2E = 1.4426950408889634
BLOCK = 128
MASKED = -1e30
MIB = 1024 * 1024
KV_CHUNKS = ((0, 768), (768, 1536), (2304, 1536), (3840, 1024), (4864, 512))
Q_CHUNKS = ((0, 768), (768, 1536), (2304, 1536), (3840, 1536))
PIECES = ((0, 768, 768), (768, 1536, 768), (2304, 1536, 768), (3840, 1536, 768))
PROJECT_LIMIT = 18 * MIB
ATTENTION_LIMIT = 24 * MIB
BACK_LIMIT = 20 * MIB

NT = (((1,), (1,)), ((), ()))


def column_chunks(chunks, hidden_ref, hidden_buf, pairs, sems):
    copies = []
    for at, (first, size) in enumerate(chunks):
        span = pl.ds(first, size)
        group = [pltpu.make_async_copy(hidden_ref.at[:, span], hidden_buf.at[:, span], sems.at[at, 0])]
        for n, (ref, buf) in enumerate(pairs):
            group.append(
                pltpu.make_async_copy(ref.at[span, :], buf.at[span, :], sems.at[at, n + 1])
            )
        for copy in group:
            copy.start()
        copies.append(group)
    return copies


def accumulate(chunks, copies, hidden_buf, bufs):
    totals = [None] * len(bufs)
    for at, (first, size) in enumerate(chunks):
        for copy in copies[at]:
            copy.wait()
        span = slice(first, first + size)
        part = hidden_buf[:, span]
        for n, buf in enumerate(bufs):
            dot = jnp.dot(part, buf[span, :], preferred_element_type=jnp.float32)
            totals[n] = dot if at == 0 else totals[n] + dot
    return totals


def project_kernel(hidden_ref, wk_ref, wv_ref, *refs):
    heads = wk_ref.shape[1] // HEAD_SIZE
    outs, (hidden_buf, k_buf, v_buf, sems) = refs[:heads], refs[heads:]
    copies = column_chunks(
        KV_CHUNKS, hidden_ref, hidden_buf, ((wk_ref, k_buf), (wv_ref, v_buf)), sems
    )
    keys, values = accumulate(KV_CHUNKS, copies, hidden_buf, (k_buf, v_buf))
    for head, out in enumerate(outs):
        cols = slice(head * HEAD_SIZE, (head + 1) * HEAD_SIZE)
        out[:, :HEAD_SIZE] = keys[:, cols].astype(out.dtype)
        out[:, HEAD_SIZE:] = values[:, cols].astype(out.dtype)


def project_keys_values(hidden, wk, wv):
    rows, depth = hidden.shape
    width = wk.shape[1]
    heads = width // HEAD_SIZE
    hbm = pl.BlockSpec(memory_space=pl.ANY)
    vmem = pl.BlockSpec(memory_space=pltpu.VMEM)
    return pl.pallas_call(
        project_kernel,
        in_specs=[hbm] * 3,
        out_specs=[vmem] * heads,
        out_shape=[jax.ShapeDtypeStruct((rows, 2 * HEAD_SIZE), jnp.bfloat16)] * heads,
        scratch_shapes=[
            pltpu.VMEM((rows, depth), jnp.bfloat16),
            pltpu.VMEM((depth, width), jnp.bfloat16),
            pltpu.VMEM((depth, width), jnp.bfloat16),
            pltpu.SemaphoreType.DMA((len(KV_CHUNKS), 3)),
        ],
        compiler_params=pltpu.CompilerParams(vmem_limit_bytes=PROJECT_LIMIT),
        cost_estimate=pl.CostEstimate(
            flops=4 * rows * depth * width,
            bytes_accessed=2 * (rows * depth + 2 * depth * width),
            transcendentals=0,
        ),
        name="project_kv",
    )(hidden, wk, wv)


def query_kernel(hidden_ref, wq_ref, out_ref, hidden_buf, q_buf, sems):
    copies = column_chunks(Q_CHUNKS, hidden_ref, hidden_buf, ((wq_ref, q_buf),), sems)
    (queries,) = accumulate(Q_CHUNKS, copies, hidden_buf, (q_buf,))
    out_ref[...] = queries.astype(out_ref.dtype)


def project_queries(hidden, wq):
    rows, depth = hidden.shape
    width = wq.shape[1]
    hbm = pl.BlockSpec(memory_space=pl.ANY)
    return pl.pallas_call(
        query_kernel,
        in_specs=[hbm] * 2,
        out_specs=pl.BlockSpec(memory_space=pltpu.VMEM),
        out_shape=jax.ShapeDtypeStruct((rows, width), jnp.bfloat16),
        scratch_shapes=[
            pltpu.VMEM((rows, depth), jnp.bfloat16),
            pltpu.VMEM((depth, width), jnp.bfloat16),
            pltpu.SemaphoreType.DMA((len(Q_CHUNKS), 2)),
        ],
        compiler_params=pltpu.CompilerParams(vmem_limit_bytes=PROJECT_LIMIT),
        cost_estimate=pl.CostEstimate(
            flops=2 * rows * depth * width,
            bytes_accessed=2 * (rows * depth + depth * width),
            transcendentals=0,
        ),
        name="project_q",
    )(hidden, wq)


def attention_kernel(
    q_ref, do_ref, far_ref, near_ref, own_ref, low_ref,
    dq_ref, gfar_ref, gnear_ref, gown_ref,
    k_ref, v_ref, dkt_ref, dvt_ref,
):
    rows = q_ref.shape[0]
    window = W + BLOCK
    for at, ref in enumerate((far_ref, near_ref, own_ref)):
        k_ref[at * rows : (at + 1) * rows, :] = ref[:, :HEAD_SIZE]
        v_ref[at * rows : (at + 1) * rows, :] = ref[:, HEAD_SIZE:]
    dkt_ref[...] = jnp.zeros_like(dkt_ref)
    dvt_ref[...] = jnp.zeros_like(dvt_ref)
    for block in range(rows // BLOCK):
        at = slice(block * BLOCK, (block + 1) * BLOCK)
        span = slice(block * BLOCK, block * BLOCK + window)
        q = jnp.concatenate([q_ref[at, :HEAD_SIZE], q_ref[at, HEAD_SIZE:]], axis=0)
        do = jnp.concatenate([do_ref[at, :HEAD_SIZE], do_ref[at, HEAD_SIZE:]], axis=0)
        k = k_ref[span, :]
        v = v_ref[span, :]
        low = low_ref[at, :]
        low = jnp.concatenate([low, low], axis=0) - block * BLOCK
        scores = lax.dot_general(q, k, NT, preferred_element_type=jnp.float32)
        col = lax.broadcasted_iota(jnp.int32, scores.shape, 1)
        row = lax.broadcasted_iota(jnp.int32, scores.shape, 0) & (BLOCK - 1)
        allowed = (col >= low) & (col <= row + W)
        scores = jnp.where(allowed, scores * (SCALE * LOG2E), MASKED)
        top = jnp.max(scores, axis=1, keepdims=True)
        e = jnp.exp2(scores - top)
        inverse = 1.0 / jnp.sum(e, axis=1, keepdims=True)
        probability = e * inverse
        probability_low = probability.astype(jnp.bfloat16)
        d_probs = lax.dot_general(do, v, NT, preferred_element_type=jnp.float32)
        row_dot = jnp.sum(
            probability_low.astype(jnp.float32) * d_probs, axis=1, keepdims=True
        )
        d_scores = (probability * ((d_probs - row_dot) * SCALE)).astype(jnp.bfloat16)
        dq = jnp.dot(d_scores, k, preferred_element_type=jnp.float32).astype(dq_ref.dtype)
        dq_ref[at, :HEAD_SIZE] = dq[:BLOCK]
        dq_ref[at, HEAD_SIZE:] = dq[BLOCK:]
        dkt_ref[:, span] += jnp.dot(q.T, d_scores, preferred_element_type=jnp.float32)
        dvt_ref[:, span] += jnp.dot(do.T, probability_low, preferred_element_type=jnp.float32)
    for at, ref in enumerate((gfar_ref, gnear_ref, gown_ref)):
        part = slice(at * rows, (at + 1) * rows)
        ref[:, :HEAD_SIZE] = dkt_ref[:, part].T.astype(ref.dtype)
        ref[:, HEAD_SIZE:] = dvt_ref[:, part].T.astype(ref.dtype)


def attend(head, queries, cotangent, far, near, own, low):
    rows = queries.shape[0]
    pair = 2 * HEAD_SIZE
    covered = (HALO + 1) * rows
    whole = pl.BlockSpec((rows, pair), lambda i: (0, 0))
    column = pl.BlockSpec((rows, pair), lambda i: (0, head))
    work = 2 * rows * (W + BLOCK) * HEAD_SIZE
    return pl.pallas_call(
        attention_kernel,
        grid=(1,),
        in_specs=[column, column, whole, whole, whole, pl.BlockSpec((rows, 1), lambda i: (0, 0))],
        out_specs=[whole] * 4,
        out_shape=[
            jax.ShapeDtypeStruct((rows, pair), jnp.bfloat16),
            jax.ShapeDtypeStruct((rows, pair), jnp.bfloat16),
            jax.ShapeDtypeStruct((rows, pair), jnp.bfloat16),
            jax.ShapeDtypeStruct((rows, pair), jnp.float32),
        ],
        scratch_shapes=[
            pltpu.VMEM((covered, HEAD_SIZE), jnp.bfloat16),
            pltpu.VMEM((covered, HEAD_SIZE), jnp.bfloat16),
            pltpu.VMEM((HEAD_SIZE, covered), jnp.float32),
            pltpu.VMEM((HEAD_SIZE, covered), jnp.float32),
        ],
        compiler_params=pltpu.CompilerParams(vmem_limit_bytes=ATTENTION_LIMIT),
        cost_estimate=pl.CostEstimate(
            flops=16 * work, bytes_accessed=16 * rows * pair, transcendentals=work // HEAD_SIZE
        ),
        name="attention",
    )(queries, cotangent, far, near, own, low)


def nt(x, w):
    return lax.dot_general(x, w, NT, preferred_element_type=jnp.float32)


def back_kernel(dq0_ref, dq1_ref, g0_ref, g1_ref, wq_ref, wk_ref, wv_ref, out_ref):
    size = HEAD_SIZE
    dk = jnp.concatenate([g0_ref[:, :size], g1_ref[:, :size]], axis=1)
    dv = jnp.concatenate([g0_ref[:, size:], g1_ref[:, size:]], axis=1)
    dq = jnp.concatenate([dq0_ref[...], dq1_ref[...]], axis=1)
    total = nt(dq, wq_ref[...]) + nt(dk, wk_ref[...]) + nt(dv, wv_ref[...])
    out_ref[...] = total.astype(out_ref.dtype)


def back_project(dq0, dq1, g0, g1, wq, wk, wv, first, columns, tile):
    rows = dq0.shape[0]
    base = first // tile
    return pl.pallas_call(
        back_kernel,
        grid=(columns // tile,),
        in_specs=[pl.BlockSpec(x.shape, lambda j: (0, 0)) for x in (dq0, dq1, g0, g1)]
        + [pl.BlockSpec((tile, w.shape[1]), lambda j: (base + j, 0)) for w in (wq, wk, wv)],
        out_specs=pl.BlockSpec((rows, tile), lambda j: (0, j)),
        out_shape=jax.ShapeDtypeStruct((rows, columns), jnp.bfloat16),
        compiler_params=pltpu.CompilerParams(vmem_limit_bytes=BACK_LIMIT),
        cost_estimate=pl.CostEstimate(
            flops=2 * rows * columns * 1024,
            bytes_accessed=2 * columns * (1024 + rows),
            transcendentals=0,
        ),
        name="back_project",
    )(dq0, dq1, g0, g1, wq, wk, wv)


def add(a, b):
    return (a.astype(jnp.float32) + b.astype(jnp.float32)).astype(jnp.bfloat16)


def shards(hidden, w_query, w_key, w_value, cotangent, doc_start):
    rows = hidden.shape[0]
    contexts = lax.axis_size("ctx")
    planes = lax.axis_size("head")
    ctx = lax.axis_index("ctx")
    plane = lax.axis_index("head")
    odd = (ctx % 2) == 1
    outer = (plane == 0) | (plane == planes - 1)
    heads = w_key.shape[1] // HEAD_SIZE
    chunk = rows // planes
    swap = [(i, i ^ 1) for i in range(contexts)]
    ahead = [(i, i + 2) for i in range(contexts - 2)]
    behind = [(i + 2, i) for i in range(contexts - 2)]
    inward = [(0, 1), (3, 2)]
    middle = [(1, 2), (2, 1)]
    outward = [(1, 0), (2, 3)]
    hidden, *weights = (
        pltpu.with_memory_space_constraint(x, pltpu.HBM)
        for x in (hidden, w_query, w_key, w_value)
    )

    low = jnp.maximum(
        doc_start - ctx * rows + HALO * rows,
        jnp.arange(rows, dtype=jnp.int32) + (HALO * rows - W + 1),
    ).reshape(rows, 1)
    own = project_keys_values(hidden, *weights[1:])
    far = [lax.ppermute(x, "ctx", ahead) for x in own]
    queries = project_queries(hidden, weights[0])
    d_queries, gradients = [], []
    for h in range(heads):
        near = lax.ppermute(jnp.where(odd, far[h], own[h]), "ctx", swap)
        dq, gfar, gnear, gown = attend(h, queries, cotangent, far[h], near, own[h], low)
        swapped = lax.ppermute(gnear, "ctx", swap)
        passed = jnp.where(odd, add(gfar, swapped), gfar)
        if h + 1 < heads:
            passed, queries = lax.optimization_barrier((passed, queries))
        returned = lax.ppermute(passed, "ctx", behind)
        total = gown + returned.astype(jnp.float32)
        total = total + jnp.where(odd, 0.0, swapped.astype(jnp.float32))
        d_queries.append(dq)
        gradients.append(total.astype(jnp.bfloat16))

    def take(array, index):
        return lax.dynamic_slice_in_dim(array, jnp.clip(index, 0, planes - 1) * chunk, chunk, 0)

    low_side = plane < 2

    def toward(array, low_index, high_index):
        return take(array, jnp.where(low_side, low_index, high_index))

    blocks = [back_project(*d_queries, *gradients, *weights, *piece) for piece in PIECES]
    r0 = [lax.ppermute(toward(block, 3, 0), "head", inward) for block in blocks]
    r1, m1 = [], []
    for n, block in enumerate(blocks):
        m1.append(lax.ppermute(add(toward(block, 3, 0), r0[n]), "head", middle))
        payload, _ = lax.optimization_barrier((toward(block, 2, 1), r0[n]))
        r1.append(lax.ppermute(payload, "head", inward))
    r2, m2 = [], []
    for n, block in enumerate(blocks):
        m2.append(lax.ppermute(add(toward(block, 2, 1), r1[n]), "head", middle))
        payload = jnp.where(outer, toward(block, 1, 2), add(toward(block, 0, 3), m1[n]))
        payload, _ = lax.optimization_barrier((payload, r1[n]))
        r2.append(lax.ppermute(payload, "head", inward + outward))
    return jnp.concatenate(
        [
            sum(part.astype(jnp.float32) for part in (take(block, plane), *parts))
            for block, *parts in zip(blocks, m2, r2)
        ],
        axis=1,
    )


def solution(mesh):
    in_specs = (
        P("ctx", None),
        P(None, "head"),
        P(None, "head"),
        P(None, "head"),
        P("ctx", "head"),
        P("ctx"),
    )
    out_specs = P(("ctx", "head"), None)
    return jax.shard_map(shards, mesh=mesh, in_specs=in_specs, out_specs=out_specs, check_vma=False)
```

time: 176 us -> 162 us (0.920)
  waiting for transfers between devices: 80.2 us -> 70.4 us
  matrix products: 5.56 us -> 0 us
  Pallas kernels: 29.3 us -> 34.8 us
  local copies, waits for them, and re-layouts: 5.5 us -> 1.94 us
  other arithmetic: 8.46 us -> 5.48 us
  starting transfers between devices: 45.6 us -> 48 us
    ppermute x18 -> x20, waiting for transfers between devices: 64.9 us -> 52.2 us  [the longest x4 18.9 us: shards(): r2.append(lax.ppermute(payload, 'head', inward + outward))]
    dot_general x1 -> x0, matrix products: 5.56 us -> none  [shards(): jnp.dot(hidden, w_query, preferred_element_type=jnp.float32)]
    pallas_call x4 -> x6, Pallas kernels: 18.9 us -> 24.3 us  [the longest x4 13 us: back_project(): pl.pallas_call(back_kernel, grid=(columns // tile,), in_specs=[pl.BlockSp...]
    unnamed x18 -> x10, local copies, waits for them, and re-layouts: 5.15 us -> 1.66 us
    ppermute x18 -> x20, starting transfers between devices: 35 us -> 37.2 us  [the longest x4 13.9 us: shards(): m1.append(lax.ppermute(add(toward(block, 3, 0), r0[n]), 'head', middle))]
  transfers between devices with their start and end apart: 26 -> 28, of which waited for: 14 -> 16; matrix products, arithmetic and copies ran while one was open for 6% -> 2% of each run, Pallas kernels for 8% -> 9%
where the time goes in v2:
time: 162 us; the launch traced here: 161 us
  waiting for transfers between devices  70.4 us (43%)
  starting transfers between devices  48 us (30%)
  Pallas kernels  34.8 us (21%)
  other arithmetic  5.48 us (3%)
  local copies, waits for them, and re-layouts  1.94 us (1%)
    ppermute x4, waiting for transfers between devices, shards(): r2.append(lax.ppermute(payload, 'head', inward + outward))  18.9 us
    ppermute x4, waiting for transfers between devices, shards(): r1.append(lax.ppermute(payload, 'head', inward))  15.2 us
    ppermute x4, starting transfers between devices, shards(): m1.append(lax.ppermute(add(toward(block, 3, 0), r0[n]), 'head', middle))  13.9 us
    pallas_call x4, Pallas kernels, back_project(): pl.pallas_call(back_kernel, grid=(columns // tile,), in_specs=[pl.BlockSp...  13 us
    ppermute x4, starting transfers between devices, shards(): m2.append(lax.ppermute(add(toward(block, 2, 1), r1[n]), 'head', middle))  12.8 us
    ppermute x4, waiting for transfers between devices, shards(): r0 = [lax.ppermute(toward(block, 3, 0), 'head', inward) for block in blocks]  11.3 us
    pallas_call x2, Pallas kernels, attend(): pl.pallas_call(attention_kernel, grid=(1,), in_specs=[column, column, who...  10.6 us
    ppermute x2, waiting for transfers between devices, shards(): returned = lax.ppermute(passed, 'ctx', behind)  10.5 us
  transfers between devices with their start and end apart: 28, of which 16 were waited for; matrix products, arithmetic and copies ran while one was open for 2% of the time, Pallas kernels for 9%

profile of v2, /device:TPU:12, one launch (start us, length us, event | category | flops | bytes accessed | tf_op | source)
XLA Modules:
  0.0 161.2 jit_solution(7435855530207167369)
XLA Ops:
  0.0 5.6 %project_kv.1 = (bf16[512,256]{1,0:T(8,128)(2,1)S(1)}, bf16[512,256]{1,0:T(8,128)(2,1)S(1)}) custom-call(bf16[512,5376]{1,0:T(8,128)(2,1)} %hidden_ref.3, bf16[5376,256]{1,0:T(8,128)(2,1)} %wk_ref.9, bf16[5376,256]{1,0:T(8,128)(2,1)} %wv_ref.9), custom_call_target="tpu_custom_call" | custom-call | flops 2818572288 | bytes 11010048 | tf_op jit(solution)/shard_map/project_kv/pallas_call | solution.py:75
  5.6 3.4 %collective-permute-start = (bf16[512,256]{1,0:T(8,128)(2,1)S(1)}, bf16[512,256]{1,0:T(8,128)(2,1)S(1)}, u32[]{:S(2)}, u32[]{:S(2)}) collective-permute-start(bf16[512,256]{1,0:T(8,128)(2,1)S(1)} %get-tuple-element.25.own_ref), channel_id=1, source_target_pairs={{0,8},{4,12},{8,16},{12,20},{16,24},{20,28},{1,9},{5,13},{9,17},{1... | collective-permute-start | bytes 786440 | tf_op jit(solution)/shard_map/ppermute | solution.py:268
  9.0 1.9 %collective-permute-start.3 = (bf16[512,256]{1,0:T(8,128)(2,1)S(1)}, bf16[512,256]{1,0:T(8,128)(2,1)S(1)}, u32[]{:S(2)}, u32[]{:S(2)}) collective-permute-start(bf16[512,256]{1,0:T(8,128)(2,1)S(1)} %get-tuple-element.30.own_ref), channel_id=1, source_target_pairs={{0,8},{4,12},{8,16},{12,20},{16,24},{20,28},{1,9},{5,13},{9,17},{1... | collective-permute-start | bytes 786440 | tf_op jit(solution)/shard_map/ppermute | solution.py:268
  11.0 6.6 %collective-permute-done.far_ref = bf16[512,256]{1,0:T(8,128)(2,1)S(1)} collective-permute-done((bf16[512,256]{1,0:T(8,128)(2,1)S(1)}, bf16[512,256]{1,0:T(8,128)(2,1)S(1)}, u32[]{:S(2)}, u32[]{:S(2)}) %collective-permute-start) | collective-permute-done | bytes 262176 | tf_op jit(solution)/shard_map/ppermute | solution.py:268
  17.8 5.6 %project_q.1.q_ref = bf16[512,512]{1,0:T(8,128)(2,1)S(1)} custom-call(bf16[512,5376]{1,0:T(8,128)(2,1)} %hidden_ref.3, bf16[5376,512]{1,0:T(8,128)(2,1)} %wq_ref.9), custom_call_target="tpu_custom_call" | custom-call | flops 2818572288 | bytes 11010048 | tf_op jit(solution)/shard_map/project_q/pallas_call | solution.py:106
  23.4 0.1 copy.7.low_ref
  23.6 0.7 copy-done.1
  24.3 0.9 copy-done.2
  25.2 5.2 %attention.2 = (bf16[512,256]{1,0:T(8,128)(2,1)S(1)}, bf16[512,256]{1,0:T(8,128)(2,1)S(1)}, bf16[512,256]{1,0:T(8,128)(2,1)S(1)}, f32[512,256]{1,0:T(8,128)S(1)}) custom-call(bf16[512,512]{1,0:T(8,128)(2,1)S(1)} %project_q.1.q_ref, bf16[512,512]{1,0:T(8,128)(2,1)S(1)} %copy-done, bf16[512,256]{1,0:T(8,128)(2,1)S(1)} %collective-permute-done.far_ref, ...), custom_call_target="tpu_custom_call" | custom-call | flops 2415919104 | bytes 2097152 | tf_op jit(solution)/shard_map/attention/pallas_call | solution.py:180
  30.4 0.5 collective-permute-start.2
  31.0 0.1 collective-permute-start.4
  31.1 1.0 collective-permute-done.2
  32.1 0.8 fusion.7
  32.9 5.4 %attention.3 = (bf16[512,256]{1,0:T(8,128)(2,1)S(1)}, bf16[512,256]{1,0:T(8,128)(2,1)S(1)}, bf16[512,256]{1,0:T(8,128)(2,1)S(1)}, f32[512,256]{1,0:T(8,128)S(1)}) custom-call(bf16[512,512]{1,0:T(8,128)(2,1)S(1)} %project_q.1.q_ref, bf16[512,512]{1,0:T(8,128)(2,1)S(1)} %copy-done, bf16[512,256]{1,0:T(8,128)(2,1)S(1)} %collective-permute-done.3.far_ref, ...), custom_call_target="tpu_custom_call" | custom-call | flops 2415919104 | bytes 2097152 | tf_op jit(solution)/shard_map/attention/pallas_call | solution.py:180
  38.3 0.4 collective-permute-start.6
  38.7 2.4 %collective-permute-start.5 = (bf16[512,256]{1,0:T(8,128)(2,1)}, bf16[512,256]{1,0:T(8,128)(2,1)S(1)}, u32[]{:S(2)}, u32[]{:S(2)}) collective-permute-start(bf16[512,256]{1,0:T(8,128)(2,1)} %fusion.7), channel_id=1, source_target_pairs={{8,0},{12,4},{16,8},{20,12},{24,16},{28,20},{9,1},{13,5},{17,9},{2... | collective-permute-start | bytes 786440 | tf_op jit(solution)/shard_map/ppermute | solution.py:278
  41.2 1.9 %collective-permute-start.7 = (bf16[512,256]{1,0:T(8,128)(2,1)S(1)}, bf16[512,256]{1,0:T(8,128)(2,1)S(1)}, u32[]{:S(2)}, u32[]{:S(2)}) collective-permute-start(bf16[512,256]{1,0:T(8,128)(2,1)S(1)} %fusion.6), channel_id=1, source_target_pairs={{8,0},{12,4},{16,8},{20,12},{24,16},{28,20},{9,1},{13,5},{17,9},{2... | collective-permute-start | bytes 786440 | tf_op jit(solution)/shard_map/ppermute | solution.py:278
  43.2 6.7 %collective-permute-done.5 = bf16[512,256]{1,0:T(8,128)(2,1)S(1)} collective-permute-done((bf16[512,256]{1,0:T(8,128)(2,1)}, bf16[512,256]{1,0:T(8,128)(2,1)S(1)}, u32[]{:S(2)}, u32[]{:S(2)}) %collective-permute-start.5) | collective-permute-done | bytes 262176 | tf_op jit(solution)/shard_map/ppermute | solution.py:278
  49.9 1.0 fusion.2.g0_ref
  51.0 3.8 %collective-permute-done.7 = bf16[512,256]{1,0:T(8,128)(2,1)S(1)} collective-permute-done((bf16[512,256]{1,0:T(8,128)(2,1)S(1)}, bf16[512,256]{1,0:T(8,128)(2,1)S(1)}, u32[]{:S(2)}, u32[]{:S(2)}) %collective-permute-start.7) | collective-permute-done | bytes 262176 | tf_op jit(solution)/shard_map/ppermute | solution.py:278
  54.8 0.1 fusion.5.g1_ref
  54.9 2.4 %back_project.4 = bf16[512,768]{1,0:T(8,128)(2,1)S(1)} custom-call(bf16[512,256]{1,0:T(8,128)(2,1)S(1)} %get-tuple-element.26.dq0_ref, bf16[512,256]{1,0:T(8,128)(2,1)S(1)} %get-tuple-element.31.dq1_ref, bf16[512,256]{1,0:T(8,128)(2,1)S(1)} %fusion.2.g0_ref, bf16[512,256]{1,0:T(8,128)(2,1)S(1)} %fusion.5.g1_ref, bf16[5376,512]{1,0:T(8,128)(2,1)} %wq_ref.9, ...), custom_call_target="tpu_custom_call" | custom-call | flops 805306368 | bytes 2359296 | tf_op jit(solution)/shard_map/back_project/pallas_call | solution.py:221
  57.2 3.6 %back_project.7 = bf16[512,1536]{1,0:T(8,128)(2,1)S(1)} custom-call(bf16[512,256]{1,0:T(8,128)(2,1)S(1)} %get-tuple-element.26.dq0_ref, bf16[512,256]{1,0:T(8,128)(2,1)S(1)} %get-tuple-element.31.dq1_ref, bf16[512,256]{1,0:T(8,128)(2,1)S(1)} %fusion.2.g0_ref, bf16[512,256]{1,0:T(8,128)(2,1)S(1)} %fusion.5.g1_ref, bf16[5376,512]{1,0:T(8,128)(2,1)} %wq_ref.9, ...), custom_call_target="tpu_custom_call" | custom-call | flops 1610612736 | bytes 4718592 | tf_op jit(solution)/shard_map/back_project/pallas_call | solution.py:221
  60.8 3.6 %back_project.6 = bf16[512,1536]{1,0:T(8,128)(2,1)S(1)} custom-call(bf16[512,256]{1,0:T(8,128)(2,1)S(1)} %get-tuple-element.26.dq0_ref, bf16[512,256]{1,0:T(8,128)(2,1)S(1)} %get-tuple-element.31.dq1_ref, bf16[512,256]{1,0:T(8,128)(2,1)S(1)} %fusion.2.g0_ref, bf16[512,256]{1,0:T(8,128)(2,1)S(1)} %fusion.5.g1_ref, bf16[5376,512]{1,0:T(8,128)(2,1)} %wq_ref.9, ...), custom_call_target="tpu_custom_call" | custom-call | flops 1610612736 | bytes 4718592 | tf_op jit(solution)/shard_map/back_project/pallas_call | solution.py:221
  64.4 1.3 collective-permute-start.8
  65.7 1.3 collective-permute-start.23
  67.1 1.3 collective-permute-start.18
  68.4 3.6 %back_project.5 = bf16[512,1536]{1,0:T(8,128)(2,1)S(1)} custom-call(bf16[512,256]{1,0:T(8,128)(2,1)S(1)} %get-tuple-element.26.dq0_ref, bf16[512,256]{1,0:T(8,128)(2,1)S(1)} %get-tuple-element.31.dq1_ref, bf16[512,256]{1,0:T(8,128)(2,1)S(1)} %fusion.2.g0_ref, bf16[512,256]{1,0:T(8,128)(2,1)S(1)} %fusion.5.g1_ref, bf16[5376,512]{1,0:T(8,128)(2,1)} %wq_ref.9, ...), custom_call_target="tpu_custom_call" | custom-call | flops 1610612736 | bytes 4718592 | tf_op jit(solution)/shard_map/back_project/pallas_call | solution.py:221
  71.9 2.2 %collective-permute-done.8 = bf16[128,768]{1,0:T(8,128)(2,1)S(1)} collective-permute-done((bf16[128,768]{1,0:T(8,128)(2,1)S(1)}, bf16[128,768]{1,0:T(8,128)(2,1)S(1)}, u32[]{:S(2)}, u32[]{:S(2)}) %collective-permute-start.8) | collective-permute-done | bytes 196640 | tf_op jit(solution)/shard_map/ppermute | solution.py:293
  74.2 3.5 %collective-permute-start.11 = (bf16[128,768]{1,0:T(8,128)(2,1)S(1)}, bf16[128,768]{1,0:T(8,128)(2,1)S(1)}, u32[]{:S(2)}, u32[]{:S(2)}) collective-permute-start(bf16[128,768]{1,0:T(8,128)(2,1)S(1)} %add_convert_fusion.10), channel_id=1, source_target_pairs={{1,2},{2,1},{5,6},{6,5},{9,10},{10,9},{13,14},{14,13},{17,18},{18,... | collective-permute-start | bytes 589832 | tf_op jit(solution)/shard_map/ppermute | solution.py:296
  77.7 1.3 collective-permute-start.13
  79.0 2.7 %collective-permute-done.11 = bf16[128,768]{1,0:T(8,128)(2,1)S(1)} collective-permute-done((bf16[128,768]{1,0:T(8,128)(2,1)S(1)}, bf16[128,768]{1,0:T(8,128)(2,1)S(1)}, u32[]{:S(2)}, u32[]{:S(2)}) %collective-permute-start.11) | collective-permute-done | bytes 196640 | tf_op jit(solution)/shard_map/ppermute | solution.py:296
  81.8 1.3 collective-permute-start.9
  83.1 0.1 add_convert_fusion.1
  83.2 3.5 %collective-permute-start.26 = (bf16[128,1536]{1,0:T(8,128)(2,1)S(1)}, bf16[128,1536]{1,0:T(8,128)(2,1)S(1)}, u32[]{:S(2)}, u32[]{:S(2)}) collective-permute-start(bf16[128,1536]{1,0:T(8,128)(2,1)S(1)} %add_convert_fusion.1), channel_id=1, source_target_pairs={{1,2},{2,1},{5,6},{6,5},{9,10},{10,9},{13,14},{14,13},{17,18},{18,... | collective-permute-start | bytes 1179656 | tf_op jit(solution)/shard_map/ppermute | solution.py:296
  86.7 4.2 %collective-permute-done.18 = bf16[128,1536]{1,0:T(8,128)(2,1)S(1)} collective-permute-done((bf16[128,1536]{1,0:T(8,128)(2,1)S(1)}, bf16[128,1536]{1,0:T(8,128)(2,1)S(1)}, u32[]{:S(2)}, u32[]{:S(2)}) %collective-permute-start.18) | collective-permute-done | bytes 393248 | tf_op jit(solution)/shard_map/ppermute | solution.py:293
  91.0 0.1 add_convert_fusion.4
  91.1 3.5 %collective-permute-start.21 = (bf16[128,1536]{1,0:T(8,128)(2,1)S(1)}, bf16[128,1536]{1,0:T(8,128)(2,1)S(1)}, u32[]{:S(2)}, u32[]{:S(2)}) collective-permute-start(bf16[128,1536]{1,0:T(8,128)(2,1)S(1)} %add_convert_fusion.4), channel_id=1, source_target_pairs={{1,2},{2,1},{5,6},{6,5},{9,10},{10,9},{13,14},{14,13},{17,18},{18,... | collective-permute-start | bytes 1179656 | tf_op jit(solution)/shard_map/ppermute | solution.py:296
  94.6 4.8 %collective-permute-done.13 = bf16[128,1536]{1,0:T(8,128)(2,1)S(1)} collective-permute-done((bf16[128,1536]{1,0:T(8,128)(2,1)S(1)}, bf16[128,1536]{1,0:T(8,128)(2,1)S(1)}, u32[]{:S(2)}, u32[]{:S(2)}) %collective-permute-start.13) | collective-permute-done | bytes 393248 | tf_op jit(solution)/shard_map/ppermute | solution.py:293
  99.4 0.1 add_convert_fusion.7
  99.5 3.5 %collective-permute-start.16 = (bf16[128,1536]{1,0:T(8,128)(2,1)S(1)}, bf16[128,1536]{1,0:T(8,128)(2,1)S(1)}, u32[]{:S(2)}, u32[]{:S(2)}) collective-permute-start(bf16[128,1536]{1,0:T(8,128)(2,1)S(1)} %add_convert_fusion.7), channel_id=1, source_target_pairs={{1,2},{2,1},{5,6},{6,5},{9,10},{10,9},{13,14},{14,13},{17,18},{18,... | collective-permute-start | bytes 1179656 | tf_op jit(solution)/shard_map/ppermute | solution.py:296
  103.1 2.4 %collective-permute-start.10 = (bf16[128,768]{1,0:T(8,128)(2,1)S(1)}, bf16[128,768]{1,0:T(8,128)(2,1)S(1)}, u32[]{:S(2)}, u32[]{:S(2)}) collective-permute-start(bf16[128,768]{1,0:T(8,128)(2,1)S(1)} %add_convert_fusion.11), channel_id=1, source_target_pairs={{1,2},{2,1},{5,6},{6,5},{9,10},{10,9},{13,14},{14,13},{17,18},{18,... | collective-permute-start | bytes 589832 | tf_op jit(solution)/shard_map/ppermute | solution.py:301
  105.5 0.2 constant_dynamic-slice_fusion.5
  105.7 1.3 collective-permute-start.24
  107.0 0.2 constant_dynamic-slice_fusion.1
  107.2 1.3 collective-permute-start.19
  108.5 3.4 %collective-permute-done.16 = bf16[128,1536]{1,0:T(8,128)(2,1)S(1)} collective-permute-done((bf16[128,1536]{1,0:T(8,128)(2,1)S(1)}, bf16[128,1536]{1,0:T(8,128)(2,1)S(1)}, u32[]{:S(2)}, u32[]{:S(2)}) %collective-permute-start.16) | collective-permute-done | bytes 393248 | tf_op jit(solution)/shard_map/ppermute | solution.py:296
  111.9 0.2 constant_dynamic-slice_fusion.4
  112.0 1.3 collective-permute-start.14
  113.3 0.6 collective-permute-done.10
  114.1 5.6 %collective-permute-done.24 = bf16[128,1536]{1,0:T(8,128)(2,1)S(1)} collective-permute-done((bf16[128,1536]{1,0:T(8,128)(2,1)S(1)}, bf16[128,1536]{1,0:T(8,128)(2,1)S(1)}, u32[]{:S(2)}, u32[]{:S(2)}) %collective-permute-start.24) | collective-permute-done | bytes 393248 | tf_op jit(solution)/shard_map/ppermute | solution.py:298
  119.6 0.1 add_convert_fusion.2
  119.7 3.5 %collective-permute-start.25 = (bf16[128,1536]{1,0:T(8,128)(2,1)S(1)}, bf16[128,1536]{1,0:T(8,128)(2,1)S(1)}, u32[]{:S(2)}, u32[]{:S(2)}) collective-permute-start(bf16[128,1536]{1,0:T(8,128)(2,1)S(1)} %add_convert_fusion.2), channel_id=1, source_target_pairs={{1,2},{2,1},{5,6},{6,5},{9,10},{10,9},{13,14},{14,13},{17,18},{18,... | collective-permute-start | bytes 1179656 | tf_op jit(solution)/shard_map/ppermute | solution.py:301
  123.2 4.8 %collective-permute-done.19 = bf16[128,1536]{1,0:T(8,128)(2,1)S(1)} collective-permute-done((bf16[128,1536]{1,0:T(8,128)(2,1)S(1)}, bf16[128,1536]{1,0:T(8,128)(2,1)S(1)}, u32[]{:S(2)}, u32[]{:S(2)}) %collective-permute-start.19) | collective-permute-done | bytes 393248 | tf_op jit(solution)/shard_map/ppermute | solution.py:298
  128.2 3.5 %collective-permute-start.20 = (bf16[128,1536]{1,0:T(8,128)(2,1)S(1)}, bf16[128,1536]{1,0:T(8,128)(2,1)S(1)}, u32[]{:S(2)}, u32[]{:S(2)}) collective-permute-start(bf16[128,1536]{1,0:T(8,128)(2,1)S(1)} %add_convert_fusion.5), channel_id=1, source_target_pairs={{1,2},{2,1},{5,6},{6,5},{9,10},{10,9},{13,14},{14,13},{17,18},{18,... | collective-permute-start | bytes 1179656 | tf_op jit(solution)/shard_map/ppermute | solution.py:301
  131.7 4.8 %collective-permute-done.14 = bf16[128,1536]{1,0:T(8,128)(2,1)S(1)} collective-permute-done((bf16[128,1536]{1,0:T(8,128)(2,1)S(1)}, bf16[128,1536]{1,0:T(8,128)(2,1)S(1)}, u32[]{:S(2)}, u32[]{:S(2)}) %collective-permute-start.14) | collective-permute-done | bytes 393248 | tf_op jit(solution)/shard_map/ppermute | solution.py:298
  136.6 8.3 %collective-permute-done.27 = bf16[128,1536]{1,0:T(8,128)(2,1)S(1)} collective-permute-done((bf16[128,1536]{1,0:T(8,128)(2,1)S(1)}, bf16[128,1536]{1,0:T(8,128)(2,1)S(1)}, u32[]{:S(2)}, u32[]{:S(2)}) %collective-permute-start.27) | collective-permute-done | bytes 393248 | tf_op jit(solution)/shard_map/ppermute | solution.py:304
  144.9 3.5 %collective-permute-start.15 = (bf16[128,1536]{1,0:T(8,128)(2,1)S(1)}, bf16[128,1536]{1,0:T(8,128)(2,1)S(1)}, u32[]{:S(2)}, u32[]{:S(2)}) collective-permute-start(bf16[128,1536]{1,0:T(8,128)(2,1)S(1)} %add_convert_fusion.8), channel_id=1, source_target_pairs={{1,2},{2,1},{5,6},{6,5},{9,10},{10,9},{13,14},{14,13},{17,18},{18,... | collective-permute-start | bytes 1179656 | tf_op jit(solution)/shard_map/ppermute | solution.py:301
  148.4 0.1 convert_add_fusion
  148.6 4.8 %collective-permute-done.22 = bf16[128,1536]{1,0:T(8,128)(2,1)S(1)} collective-permute-done((bf16[128,1536]{1,0:T(8,128)(2,1)S(1)}, bf16[128,1536]{1,0:T(8,128)(2,1)S(1)}, u32[]{:S(2)}, u32[]{:S(2)}) %collective-permute-start.22) | collective-permute-done | bytes 393248 | tf_op jit(solution)/shard_map/ppermute | solution.py:304
  153.3 0.1 convert_add_fusion.1
  153.5 5.8 %collective-permute-done.17 = bf16[128,1536]{1,0:T(8,128)(2,1)S(1)} collective-permute-done((bf16[128,1536]{1,0:T(8,128)(2,1)S(1)}, bf16[128,1536]{1,0:T(8,128)(2,1)S(1)}, u32[]{:S(2)}, u32[]{:S(2)}) %collective-permute-start.17) | collective-permute-done | bytes 393248 | tf_op jit(solution)/shard_map/ppermute | solution.py:304
  159.3 0.1 convert_add_fusion.2
  159.4 1.7 %pad_maximum_fusion = f32[128,5376]{1,0:T(8,128)} fusion(f32[128,1536]{1,0:T(8,128)S(1)} %convert_add_fusion, f32[128,1536]{1,0:T(8,128)S(1)} %convert_add_fusion.1, f32[128,1536]{1,0:T(8,128)S(1)} %convert_add_fusion.2, f32[128,768]{1,0:T(8,128)S(1)} %convert_add_fusion.5), kind=kLoop, calls=%fused_computation | loop fusion | flops 2064384 | bytes 5505024 | tf_op jit(solution)/shard_map/concatenate | solution.py:305
  (39 shorter events, 0.9 us)
Async XLA Ops:
  5.6 12.0 %collective-permute-start = (bf16[512,256]{1,0:T(8,128)(2,1)S(1)}, bf16[512,256]{1,0:T(8,128)(2,1)S(1)}, u32[]{:S(2)}, u32[]{:S(2)}) collective-permute-start(bf16[512,256]{1,0:T(8,128)(2,1)S(1)} %get-tuple-element.25.own_ref), channel_id=1, source_target_pairs={{0,8},{4,12},{8,16},{12,20},{16,24},{20,28},{1,9},{5,13},{9,17},{1... | collective-permute-start | bytes 786440 | tf_op jit(solution)/shard_map/ppermute | solution.py:268
  9.0 21.9 %collective-permute-start.3 = (bf16[512,256]{1,0:T(8,128)(2,1)S(1)}, bf16[512,256]{1,0:T(8,128)(2,1)S(1)}, u32[]{:S(2)}, u32[]{:S(2)}) collective-permute-start(bf16[512,256]{1,0:T(8,128)(2,1)S(1)} %get-tuple-element.30.own_ref), channel_id=1, source_target_pairs={{0,8},{4,12},{8,16},{12,20},{16,24},{20,28},{1,9},{5,13},{9,17},{1... | collective-permute-start | bytes 786440 | tf_op jit(solution)/shard_map/ppermute | solution.py:268
  17.7 5.7 %copy-start.4 = (s32[512]{0:T(512)S(1)}, s32[512]{0:T(512)}, u32[]{:S(2)}) copy-start(s32[512]{0:T(512)} %param.11) | copy-start | bytes 6148
  17.7 6.6 %copy-start = (bf16[512,512]{1,0:T(8,128)(2,1)S(1)}, bf16[512,512]{1,0:T(8,128)(2,1)}, u32[]{:S(2)}) copy-start(bf16[512,512]{1,0:T(8,128)(2,1)} %do_ref.3) | copy-start | bytes 1572868
  17.7 5.9 %collective-permute-start.1 = (bf16[512,256]{1,0:T(8,128)(2,1)S(1)}, bf16[512,256]{1,0:T(8,128)(2,1)S(1)}, u32[]{:S(2)}, u32[]{:S(2)}) collective-permute-start(bf16[512,256]{1,0:T(8,128)(2,1)S(1)} %broadcast_select_fusion.1), channel_id=1, source_target_pairs={{0,4},{4,0},{8,12},{12,8},{16,20},{20,16},{24,28},{28,24},{1,5},{5... | collective-permute-start | bytes 786440 | tf_op jit(solution)/shard_map/ppermute | solution.py:272
  23.6 0.7 copy-start.1
  24.3 1.0 copy-start.2
  30.4 1.7 %collective-permute-start.2 = (bf16[512,256]{1,0:T(8,128)(2,1)S(1)}, bf16[512,256]{1,0:T(8,128)(2,1)S(1)}, u32[]{:S(2)}, u32[]{:S(2)}) collective-permute-start(bf16[512,256]{1,0:T(8,128)(2,1)S(1)} %get-tuple-element.28), channel_id=1, source_target_pairs={{0,4},{4,0},{8,12},{12,8},{16,20},{20,16},{24,28},{28,24},{1,5},{5... | collective-permute-start | bytes 786440 | tf_op jit(solution)/shard_map/ppermute | solution.py:274
  31.0 1.9 %collective-permute-start.4 = (bf16[512,256]{1,0:T(8,128)(2,1)S(1)}, bf16[512,256]{1,0:T(8,128)(2,1)S(1)}, u32[]{:S(2)}, u32[]{:S(2)}) collective-permute-start(bf16[512,256]{1,0:T(8,128)(2,1)S(1)} %broadcast_select_fusion), channel_id=1, source_target_pairs={{0,4},{4,0},{8,12},{12,8},{16,20},{20,16},{24,28},{28,24},{1,5},{5... | collective-permute-start | bytes 786440 | tf_op jit(solution)/shard_map/ppermute | solution.py:272
  32.1 0.8 copy-start.3
  38.3 2.9 %collective-permute-start.6 = (bf16[512,256]{1,0:T(8,128)(2,1)S(1)}, bf16[512,256]{1,0:T(8,128)(2,1)S(1)}, u32[]{:S(2)}, u32[]{:S(2)}) collective-permute-start(bf16[512,256]{1,0:T(8,128)(2,1)S(1)} %get-tuple-element.36), channel_id=1, source_target_pairs={{0,4},{4,0},{8,12},{12,8},{16,20},{20,16},{24,28},{28,24},{1,5},{5... | collective-permute-start | bytes 786440 | tf_op jit(solution)/shard_map/ppermute | solution.py:274
  38.7 11.2 %collective-permute-start.5 = (bf16[512,256]{1,0:T(8,128)(2,1)}, bf16[512,256]{1,0:T(8,128)(2,1)S(1)}, u32[]{:S(2)}, u32[]{:S(2)}) collective-permute-start(bf16[512,256]{1,0:T(8,128)(2,1)} %fusion.7), channel_id=1, source_target_pairs={{8,0},{12,4},{16,8},{20,12},{24,16},{28,20},{9,1},{13,5},{17,9},{2... | collective-permute-start | bytes 786440 | tf_op jit(solution)/shard_map/ppermute | solution.py:278
  41.2 13.5 %collective-permute-start.7 = (bf16[512,256]{1,0:T(8,128)(2,1)S(1)}, bf16[512,256]{1,0:T(8,128)(2,1)S(1)}, u32[]{:S(2)}, u32[]{:S(2)}) collective-permute-start(bf16[512,256]{1,0:T(8,128)(2,1)S(1)} %fusion.6), channel_id=1, source_target_pairs={{8,0},{12,4},{16,8},{20,12},{24,16},{28,20},{9,1},{13,5},{17,9},{2... | collective-permute-start | bytes 786440 | tf_op jit(solution)/shard_map/ppermute | solution.py:278
  64.4 9.7 %collective-permute-start.8 = (bf16[128,768]{1,0:T(8,128)(2,1)S(1)}, bf16[128,768]{1,0:T(8,128)(2,1)S(1)}, u32[]{:S(2)}, u32[]{:S(2)}) collective-permute-start(bf16[128,768]{1,0:T(8,128)(2,1)S(1)} %constant_dynamic-slice_fusion.6), channel_id=1, source_target_pairs={{0,1},{3,2},{4,5},{7,6},{8,9},{11,10},{12,13},{15,14},{16,17},{19,... | collective-permute-start | bytes 589832 | tf_op jit(solution)/shard_map/ppermute | solution.py:293
  65.7 17.4 %collective-permute-start.23 = (bf16[128,1536]{1,0:T(8,128)(2,1)S(1)}, bf16[128,1536]{1,0:T(8,128)(2,1)S(1)}, u32[]{:S(2)}, u32[]{:S(2)}) collective-permute-start(bf16[128,1536]{1,0:T(8,128)(2,1)S(1)} %constant_dynamic-slice_fusion.2), channel_id=1, source_target_pairs={{0,1},{3,2},{4,5},{7,6},{8,9},{11,10},{12,13},{15,14},{16,17},{19,... | collective-permute-start | bytes 1179656 | tf_op jit(solution)/shard_map/ppermute | solution.py:293
  67.1 23.9 %collective-permute-start.18 = (bf16[128,1536]{1,0:T(8,128)(2,1)S(1)}, bf16[128,1536]{1,0:T(8,128)(2,1)S(1)}, u32[]{:S(2)}, u32[]{:S(2)}) collective-permute-start(bf16[128,1536]{1,0:T(8,128)(2,1)S(1)} %constant_dynamic-slice_fusion), channel_id=1, source_target_pairs={{0,1},{3,2},{4,5},{7,6},{8,9},{11,10},{12,13},{15,14},{16,17},{19,... | collective-permute-start | bytes 1179656 | tf_op jit(solution)/shard_map/ppermute | solution.py:293
  74.2 7.6 %collective-permute-start.11 = (bf16[128,768]{1,0:T(8,128)(2,1)S(1)}, bf16[128,768]{1,0:T(8,128)(2,1)S(1)}, u32[]{:S(2)}, u32[]{:S(2)}) collective-permute-start(bf16[128,768]{1,0:T(8,128)(2,1)S(1)} %add_convert_fusion.10), channel_id=1, source_target_pairs={{1,2},{2,1},{5,6},{6,5},{9,10},{10,9},{13,14},{14,13},{17,18},{18,... | collective-permute-start | bytes 589832 | tf_op jit(solution)/shard_map/ppermute | solution.py:296
  77.7 21.7 %collective-permute-start.13 = (bf16[128,1536]{1,0:T(8,128)(2,1)S(1)}, bf16[128,1536]{1,0:T(8,128)(2,1)S(1)}, u32[]{:S(2)}, u32[]{:S(2)}) collective-permute-start(bf16[128,1536]{1,0:T(8,128)(2,1)S(1)} %constant_dynamic-slice_fusion.3), channel_id=1, source_target_pairs={{0,1},{3,2},{4,5},{7,6},{8,9},{11,10},{12,13},{15,14},{16,17},{19,... | collective-permute-start | bytes 1179656 | tf_op jit(solution)/shard_map/ppermute | solution.py:293
  81.8 21.2 %collective-permute-start.9 = (bf16[128,768]{1,0:T(8,128)(2,1)S(1)}, bf16[128,768]{1,0:T(8,128)(2,1)S(1)}, u32[]{:S(2)}, u32[]{:S(2)}) collective-permute-start(bf16[128,768]{1,0:T(8,128)(2,1)S(1)} %get-tuple-element.37), channel_id=1, source_target_pairs={{0,1},{3,2},{4,5},{7,6},{8,9},{11,10},{12,13},{15,14},{16,17},{19,... | collective-permute-start | bytes 589832 | tf_op jit(solution)/shard_map/ppermute | solution.py:298
  83.2 22.3 %collective-permute-start.26 = (bf16[128,1536]{1,0:T(8,128)(2,1)S(1)}, bf16[128,1536]{1,0:T(8,128)(2,1)S(1)}, u32[]{:S(2)}, u32[]{:S(2)}) collective-permute-start(bf16[128,1536]{1,0:T(8,128)(2,1)S(1)} %add_convert_fusion.1), channel_id=1, source_target_pairs={{1,2},{2,1},{5,6},{6,5},{9,10},{10,9},{13,14},{14,13},{17,18},{18,... | collective-permute-start | bytes 1179656 | tf_op jit(solution)/shard_map/ppermute | solution.py:296
  91.1 15.9 %collective-permute-start.21 = (bf16[128,1536]{1,0:T(8,128)(2,1)S(1)}, bf16[128,1536]{1,0:T(8,128)(2,1)S(1)}, u32[]{:S(2)}, u32[]{:S(2)}) collective-permute-start(bf16[128,1536]{1,0:T(8,128)(2,1)S(1)} %add_convert_fusion.4), channel_id=1, source_target_pairs={{1,2},{2,1},{5,6},{6,5},{9,10},{10,9},{13,14},{14,13},{17,18},{18,... | collective-permute-start | bytes 1179656 | tf_op jit(solution)/shard_map/ppermute | solution.py:296
  99.5 12.4 %collective-permute-start.16 = (bf16[128,1536]{1,0:T(8,128)(2,1)S(1)}, bf16[128,1536]{1,0:T(8,128)(2,1)S(1)}, u32[]{:S(2)}, u32[]{:S(2)}) collective-permute-start(bf16[128,1536]{1,0:T(8,128)(2,1)S(1)} %add_convert_fusion.7), channel_id=1, source_target_pairs={{1,2},{2,1},{5,6},{6,5},{9,10},{10,9},{13,14},{14,13},{17,18},{18,... | collective-permute-start | bytes 1179656 | tf_op jit(solution)/shard_map/ppermute | solution.py:296
  103.0 10.3 %collective-permute-start.12 = (bf16[128,768]{1,0:T(8,128)(2,1)S(1)}, bf16[128,768]{1,0:T(8,128)(2,1)S(1)}, u32[]{:S(2)}, u32[]{:S(2)}) collective-permute-start(bf16[128,768]{1,0:T(8,128)(2,1)S(1)} %get-tuple-element.38), channel_id=1, source_target_pairs={{0,1},{3,2},{1,0},{2,3},{4,5},{7,6},{5,4},{6,7},{8,9},{11,10},{9,8... | collective-permute-start | bytes 589832 | tf_op jit(solution)/shard_map/ppermute | solution.py:304
  103.1 10.8 %collective-permute-start.10 = (bf16[128,768]{1,0:T(8,128)(2,1)S(1)}, bf16[128,768]{1,0:T(8,128)(2,1)S(1)}, u32[]{:S(2)}, u32[]{:S(2)}) collective-permute-start(bf16[128,768]{1,0:T(8,128)(2,1)S(1)} %add_convert_fusion.11), channel_id=1, source_target_pairs={{1,2},{2,1},{5,6},{6,5},{9,10},{10,9},{13,14},{14,13},{17,18},{18,... | collective-permute-start | bytes 589832 | tf_op jit(solution)/shard_map/ppermute | solution.py:301
  105.7 13.9 %collective-permute-start.24 = (bf16[128,1536]{1,0:T(8,128)(2,1)S(1)}, bf16[128,1536]{1,0:T(8,128)(2,1)S(1)}, u32[]{:S(2)}, u32[]{:S(2)}) collective-permute-start(bf16[128,1536]{1,0:T(8,128)(2,1)S(1)} %get-tuple-element.43), channel_id=1, source_target_pairs={{0,1},{3,2},{4,5},{7,6},{8,9},{11,10},{12,13},{15,14},{16,17},{19,... | collective-permute-start | bytes 1179656 | tf_op jit(solution)/shard_map/ppermute | solution.py:298
  107.2 20.9 %collective-permute-start.19 = (bf16[128,1536]{1,0:T(8,128)(2,1)S(1)}, bf16[128,1536]{1,0:T(8,128)(2,1)S(1)}, u32[]{:S(2)}, u32[]{:S(2)}) collective-permute-start(bf16[128,1536]{1,0:T(8,128)(2,1)S(1)} %get-tuple-element.41), channel_id=1, source_target_pairs={{0,1},{3,2},{4,5},{7,6},{8,9},{11,10},{12,13},{15,14},{16,17},{19,... | collective-permute-start | bytes 1179656 | tf_op jit(solution)/shard_map/ppermute | solution.py:298
  112.0 24.5 %collective-permute-start.14 = (bf16[128,1536]{1,0:T(8,128)(2,1)S(1)}, bf16[128,1536]{1,0:T(8,128)(2,1)S(1)}, u32[]{:S(2)}, u32[]{:S(2)}) collective-permute-start(bf16[128,1536]{1,0:T(8,128)(2,1)S(1)} %get-tuple-element.39), channel_id=1, source_target_pairs={{0,1},{3,2},{4,5},{7,6},{8,9},{11,10},{12,13},{15,14},{16,17},{19,... | collective-permute-start | bytes 1179656 | tf_op jit(solution)/shard_map/ppermute | solution.py:298
  119.6 25.3 %collective-permute-start.27 = (bf16[128,1536]{1,0:T(8,128)(2,1)S(1)}, bf16[128,1536]{1,0:T(8,128)(2,1)S(1)}, u32[]{:S(2)}, u32[]{:S(2)}) collective-permute-start(bf16[128,1536]{1,0:T(8,128)(2,1)S(1)} %get-tuple-element.44), channel_id=1, source_target_pairs={{0,1},{3,2},{1,0},{2,3},{4,5},{7,6},{5,4},{6,7},{8,9},{11,10},{9,8... | collective-permute-start | bytes 1179656 | tf_op jit(solution)/shard_map/ppermute | solution.py:304
  119.7 28.7 %collective-permute-start.25 = (bf16[128,1536]{1,0:T(8,128)(2,1)S(1)}, bf16[128,1536]{1,0:T(8,128)(2,1)S(1)}, u32[]{:S(2)}, u32[]{:S(2)}) collective-permute-start(bf16[128,1536]{1,0:T(8,128)(2,1)S(1)} %add_convert_fusion.2), channel_id=1, source_target_pairs={{1,2},{2,1},{5,6},{6,5},{9,10},{10,9},{13,14},{14,13},{17,18},{18,... | collective-permute-start | bytes 1179656 | tf_op jit(solution)/shard_map/ppermute | solution.py:301
  128.1 25.3 %collective-permute-start.22 = (bf16[128,1536]{1,0:T(8,128)(2,1)S(1)}, bf16[128,1536]{1,0:T(8,128)(2,1)S(1)}, u32[]{:S(2)}, u32[]{:S(2)}) collective-permute-start(bf16[128,1536]{1,0:T(8,128)(2,1)S(1)} %get-tuple-element.42), channel_id=1, source_target_pairs={{0,1},{3,2},{1,0},{2,3},{4,5},{7,6},{5,4},{6,7},{8,9},{11,10},{9,8... | collective-permute-start | bytes 1179656 | tf_op jit(solution)/shard_map/ppermute | solution.py:304
  128.2 25.2 %collective-permute-start.20 = (bf16[128,1536]{1,0:T(8,128)(2,1)S(1)}, bf16[128,1536]{1,0:T(8,128)(2,1)S(1)}, u32[]{:S(2)}, u32[]{:S(2)}) collective-permute-start(bf16[128,1536]{1,0:T(8,128)(2,1)S(1)} %add_convert_fusion.5), channel_id=1, source_target_pairs={{1,2},{2,1},{5,6},{6,5},{9,10},{10,9},{13,14},{14,13},{17,18},{18,... | collective-permute-start | bytes 1179656 | tf_op jit(solution)/shard_map/ppermute | solution.py:301
  136.5 22.8 %collective-permute-start.17 = (bf16[128,1536]{1,0:T(8,128)(2,1)S(1)}, bf16[128,1536]{1,0:T(8,128)(2,1)S(1)}, u32[]{:S(2)}, u32[]{:S(2)}) collective-permute-start(bf16[128,1536]{1,0:T(8,128)(2,1)S(1)} %get-tuple-element.40), channel_id=1, source_target_pairs={{0,1},{3,2},{1,0},{2,3},{4,5},{7,6},{5,4},{6,7},{8,9},{11,10},{9,8... | collective-permute-start | bytes 1179656 | tf_op jit(solution)/shard_map/ppermute | solution.py:304
  144.9 14.4 %collective-permute-start.15 = (bf16[128,1536]{1,0:T(8,128)(2,1)S(1)}, bf16[128,1536]{1,0:T(8,128)(2,1)S(1)}, u32[]{:S(2)}, u32[]{:S(2)}) collective-permute-start(bf16[128,1536]{1,0:T(8,128)(2,1)S(1)} %add_convert_fusion.8), channel_id=1, source_target_pairs={{1,2},{2,1},{5,6},{6,5},{9,10},{10,9},{13,14},{14,13},{17,18},{18,... | collective-permute-start | bytes 1179656 | tf_op jit(solution)/shard_map/ppermute | solution.py:301

commit v3 on v2

--- a/solution.py
+++ b/solution.py
@@ -17,9 +17,11 @@
 MIB = 1024 * 1024
 KV_CHUNKS = ((0, 768), (768, 1536), (2304, 1536), (3840, 1024), (4864, 512))
 Q_CHUNKS = ((0, 768), (768, 1536), (2304, 1536), (3840, 1536))
-PIECES = ((0, 768, 768), (768, 1536, 768), (2304, 1536, 768), (3840, 1536, 768))
+TILE = 768
+PIECES = ((0, 768), (768, 2304), (3072, 2304))
+OUTER_DEPTH, MIDDLE_DEPTH = 3, 2
 PROJECT_LIMIT = 18 * MIB
-ATTENTION_LIMIT = 24 * MIB
+ATTENTION_LIMIT = 14 * MIB
 BACK_LIMIT = 20 * MIB
 
 NT = (((1,), (1,)), ((), ()))
@@ -206,33 +208,69 @@
     return lax.dot_general(x, w, NT, preferred_element_type=jnp.float32)
 
 
-def back_kernel(dq0_ref, dq1_ref, g0_ref, g1_ref, wq_ref, wk_ref, wv_ref, out_ref):
+def back_kernel(spans, place_ref, dq0_ref, dq1_ref, g0_ref, g1_ref, wq_ref, wk_ref, wv_ref, *refs):
+    outs, buf = refs[:-1], refs[-1]
+    count = len(outs) // len(spans)
     size = HEAD_SIZE
-    dk = jnp.concatenate([g0_ref[:, :size], g1_ref[:, :size]], axis=1)
-    dv = jnp.concatenate([g0_ref[:, size:], g1_ref[:, size:]], axis=1)
-    dq = jnp.concatenate([dq0_ref[...], dq1_ref[...]], axis=1)
-    total = nt(dq, wq_ref[...]) + nt(dk, wk_ref[...]) + nt(dv, wv_ref[...])
-    out_ref[...] = total.astype(out_ref.dtype)
-
-
-def back_project(dq0, dq1, g0, g1, wq, wk, wv, first, columns, tile):
-    rows = dq0.shape[0]
-    base = first // tile
-    return pl.pallas_call(
-        back_kernel,
-        grid=(columns // tile,),
-        in_specs=[pl.BlockSpec(x.shape, lambda j: (0, 0)) for x in (dq0, dq1, g0, g1)]
-        + [pl.BlockSpec((tile, w.shape[1]), lambda j: (base + j, 0)) for w in (wq, wk, wv)],
-        out_specs=pl.BlockSpec((rows, tile), lambda j: (0, j)),
-        out_shape=jax.ShapeDtypeStruct((rows, columns), jnp.bfloat16),
+    pair = 2 * size
+    step = pl.program_id(0)
+
+    @pl.when(step == 0)
+    def _():
+        for n in range(count):
+            span = pl.ds(pl.multiple_of(place_ref[n] * size, size), size)
+            here = slice(n * size, (n + 1) * size)
+            buf[here, :pair] = dq0_ref[span, :]
+            buf[here, pair : 2 * pair] = dq1_ref[span, :]
+            for at, ref in enumerate((g0_ref, g1_ref)):
+                rows = ref[span, :]
+                buf[here, 2 * pair + at * size : 2 * pair + (at + 1) * size] = rows[:, :size]
+                buf[here, 3 * pair + at * size : 3 * pair + (at + 1) * size] = rows[:, size:]
+
+    total = nt(buf[:, : 2 * pair], wq_ref[...]) + nt(buf[:, 2 * pair : 3 * pair], wk_ref[...])
+    total = (total + nt(buf[:, 3 * pair :], wv_ref[...])).astype(jnp.bfloat16)
+    for at, (first, steps) in enumerate(spans):
+
+        @pl.when((step >= first) & (step < first + steps))
+        def _():
+            for n in range(count):
+                outs[at * count + n][...] = total[n * size : (n + 1) * size]
+
+
+def back_project(chunks, count, grads, weights, pieces):
+    base = pieces[0][0] // TILE
+    spans = [(first // TILE - base, columns // TILE) for first, columns in pieces]
+    columns = sum(columns for _, columns in pieces)
+    rows = HEAD_SIZE
+
+    def out_spec(first, steps):
+        return pl.BlockSpec((rows, TILE), lambda j, place: (0, jnp.clip(j - first, 0, steps - 1)))
+
+    grid_spec = pltpu.PrefetchScalarGridSpec(
+        num_scalar_prefetch=1,
+        grid=(columns // TILE,),
+        in_specs=[pl.BlockSpec(x.shape, lambda j, place: (0, 0)) for x in grads]
+        + [pl.BlockSpec((TILE, w.shape[1]), lambda j, place: (base + j, 0)) for w in weights],
+        out_specs=[out_spec(*span) for span in spans for _ in range(count)],
+        scratch_shapes=[pltpu.VMEM((count * rows, 1024), jnp.bfloat16)],
+    )
+    outs = pl.pallas_call(
+        functools.partial(back_kernel, spans),
+        grid_spec=grid_spec,
+        out_shape=[
+            jax.ShapeDtypeStruct((rows, columns), jnp.bfloat16)
+            for _, columns in pieces
+            for _ in range(count)
+        ],
         compiler_params=pltpu.CompilerParams(vmem_limit_bytes=BACK_LIMIT),
         cost_estimate=pl.CostEstimate(
-            flops=2 * rows * columns * 1024,
-            bytes_accessed=2 * columns * (1024 + rows),
+            flops=2 * count * rows * columns * 1024,
+            bytes_accessed=2 * columns * (1024 + count * rows),
             transcendentals=0,
         ),
         name="back_project",
-    )(dq0, dq1, g0, g1, wq, wk, wv)
+    )(chunks, *grads, *weights)
+    return [outs[at * count : (at + 1) * count] for at in range(len(pieces))]
 
 
 def add(a, b):
@@ -267,44 +305,67 @@
     own = project_keys_values(hidden, *weights[1:])
     far = [lax.ppermute(x, "ctx", ahead) for x in own]
     queries = project_queries(hidden, weights[0])
-    d_queries, gradients = [], []
+    far[0], queries = lax.optimization_barrier((far[0], queries))
+    d_queries, gradients, waiting = [], [], []
+
+    def finish():
+        gown, swapped = waiting.pop()
+        total = gown + returned.astype(jnp.float32)
+        total = total + jnp.where(odd, 0.0, swapped.astype(jnp.float32))
+        gradients.append(total.astype(jnp.bfloat16))
+
     for h in range(heads):
         near = lax.ppermute(jnp.where(odd, far[h], own[h]), "ctx", swap)
         dq, gfar, gnear, gown = attend(h, queries, cotangent, far[h], near, own[h], low)
+        if h > 0:
+            gnear, returned = lax.optimization_barrier((gnear, returned))
+            finish()
         swapped = lax.ppermute(gnear, "ctx", swap)
         passed = jnp.where(odd, add(gfar, swapped), gfar)
         if h + 1 < heads:
             passed, queries = lax.optimization_barrier((passed, queries))
         returned = lax.ppermute(passed, "ctx", behind)
-        total = gown + returned.astype(jnp.float32)
-        total = total + jnp.where(odd, 0.0, swapped.astype(jnp.float32))
         d_queries.append(dq)
-        gradients.append(total.astype(jnp.bfloat16))
-
-    def take(array, index):
-        return lax.dynamic_slice_in_dim(array, jnp.clip(index, 0, planes - 1) * chunk, chunk, 0)
+        waiting.append((gown, swapped))
+    finish()
 
     low_side = plane < 2
 
-    def toward(array, low_index, high_index):
-        return take(array, jnp.where(low_side, low_index, high_index))
-
-    blocks = [back_project(*d_queries, *gradients, *weights, *piece) for piece in PIECES]
-    r0 = [lax.ppermute(toward(block, 3, 0), "head", inward) for block in blocks]
-    r1, m1 = [], []
-    for n, block in enumerate(blocks):
-        m1.append(lax.ppermute(add(toward(block, 3, 0), r0[n]), "head", middle))
-        payload, _ = lax.optimization_barrier((toward(block, 2, 1), r0[n]))
-        r1.append(lax.ppermute(payload, "head", inward))
-    r2, m2 = [], []
-    for n, block in enumerate(blocks):
-        m2.append(lax.ppermute(add(toward(block, 2, 1), r1[n]), "head", middle))
-        payload = jnp.where(outer, toward(block, 1, 2), add(toward(block, 0, 3), m1[n]))
-        payload, _ = lax.optimization_barrier((payload, r1[n]))
-        r2.append(lax.ppermute(payload, "head", inward + outward))
+    side = jnp.where(low_side, 3, 0)
+    step = jnp.where(low_side, -1, 1)
+    order = [(side + step * n).astype(jnp.int32) for n in range(planes)]
+    last = jnp.where(outer, order[2], order[3])
+    home = jnp.where(outer, order[3], order[2])
+    grads = (*d_queries, *gradients)
+    edge = [
+        back_project(order[0].reshape(1), 1, grads, weights, [piece])[0][0] for piece in PIECES
+    ]
+    sent_outer, sent_middle = [], []
+
+    def send(payload, pairs, sent, depth):
+        if len(sent) >= depth:
+            payload, _ = lax.optimization_barrier((payload, sent[-depth]))
+        sent.append(lax.ppermute(payload, "head", pairs))
+        return sent[-1]
+
+    def send_outer(payload, pairs):
+        return send(payload, pairs, sent_outer, OUTER_DEPTH)
+
+    def send_middle(payload):
+        return send(payload, middle, sent_middle, MIDDLE_DEPTH)
+
+    r0 = [send_outer(block, inward) for block in edge]
+    *grads, _ = lax.optimization_barrier((*grads, r0[0]))
+    others = jnp.stack([order[1], last, home])
+    blocks = back_project(others, 3, grads, weights, PIECES)
+    m1 = [send_middle(add(block, r)) for block, r in zip(edge, r0)]
+    r1 = [send_outer(block[0], inward) for block in blocks]
+    m2 = [send_middle(add(block[0], r)) for block, r in zip(blocks, r1)]
+    r2 = [send_outer(add(block[1], m), inward + outward) for block, m in zip(blocks, m1)]
+    blocks = [block[2] for block in blocks]
     return jnp.concatenate(
         [
-            sum(part.astype(jnp.float32) for part in (take(block, plane), *parts))
+            sum(part.astype(jnp.float32) for part in (block, *parts))
             for block, *parts in zip(blocks, m2, r2)
         ],
         axis=1,

time: 162 us -> 153 us (0.944)
  starting transfers between devices: 48 us -> 40.3 us
  Pallas kernels: 34.8 us -> 42 us
  waiting for transfers between devices: 70.4 us -> 63.9 us
  local copies, waits for them, and re-layouts: 1.94 us -> 0.17 us
    ppermute x20 -> x15, starting transfers between devices: 37.2 us -> 28.5 us  [send(): sent.append(lax.ppermute(payload, 'head', pairs))]
    pallas_call x4, Pallas kernels: 13 us -> 20.3 us  [back_project(): pl.pallas_call(functools.partial(back_kernel, spans), grid_spec=grid_spec...]
    ppermute x20 -> x15, waiting for transfers between devices: 52.2 us -> 48.2 us  [send(): sent.append(lax.ppermute(payload, 'head', pairs))]
    unnamed x10 -> x8, local copies, waits for them, and re-layouts: 1.66 us -> 0.02 us
  transfers between devices with their start and end apart: 28 -> 23, of which waited for: 16 -> 12; matrix products, arithmetic and copies ran while one was open for 2% -> 2% of each run, Pallas kernels for 9% -> 23%
where the time goes in v3:
time: 153 us; the launch traced here: 151 us
  waiting for transfers between devices  63.9 us (42%)
  Pallas kernels  42 us (27%)
  starting transfers between devices  40.3 us (26%)
  other arithmetic  4.7 us (3%)
    ppermute x15, waiting for transfers between devices, send(): sent.append(lax.ppermute(payload, 'head', pairs))  48.2 us
    ppermute x15, starting transfers between devices, send(): sent.append(lax.ppermute(payload, 'head', pairs))  28.5 us
    pallas_call x4, Pallas kernels, back_project(): pl.pallas_call(functools.partial(back_kernel, spans), grid_spec=grid_spec...  20.3 us
    pallas_call x2, Pallas kernels, attend(): pl.pallas_call(attention_kernel, grid=(1,), in_specs=[column, column, who...  10.4 us
    ppermute x2, waiting for transfers between devices, shards(): returned = lax.ppermute(passed, 'ctx', behind)  9.01 us
    ppermute x2, starting transfers between devices, shards(): far = [lax.ppermute(x, 'ctx', ahead) for x in own]  5.9 us
    pallas_call x1, Pallas kernels, project_keys_values(): pl.pallas_call(project_kernel, in_specs=[hbm] * 3, out_specs=[vmem] * hea...  5.63 us
    pallas_call x1, Pallas kernels, project_queries(): pl.pallas_call(query_kernel, in_specs=[hbm] * 2, out_specs=pl.BlockSpec(m...  5.6 us
  transfers between devices with their start and end apart: 23, of which 12 were waited for; matrix products, arithmetic and copies ran while one was open for 2% of the time, Pallas kernels for 23%

profile of v3, /device:TPU:12, one launch (start us, length us, event | category | flops | bytes accessed | tf_op | source)
XLA Modules:
  0.0 151.5 jit_solution(3980095384878451451)
XLA Ops:
  0.0 5.6 %project_kv.1 = (bf16[512,256]{1,0:T(8,128)(2,1)S(1)}, bf16[512,256]{1,0:T(8,128)(2,1)S(1)}) custom-call(bf16[512,5376]{1,0:T(8,128)(2,1)} %hidden_ref.3, bf16[5376,256]{1,0:T(8,128)(2,1)} %wk_ref.9, bf16[5376,256]{1,0:T(8,128)(2,1)} %wv_ref.9), custom_call_target="tpu_custom_call" | custom-call | flops 2818572288 | bytes 11010048 | tf_op jit(solution)/shard_map/project_kv/pallas_call | solution.py:77
  5.6 3.4 %collective-permute-start = (bf16[512,256]{1,0:T(8,128)(2,1)S(1)}, bf16[512,256]{1,0:T(8,128)(2,1)S(1)}, u32[]{:S(2)}, u32[]{:S(2)}) collective-permute-start(bf16[512,256]{1,0:T(8,128)(2,1)S(1)} %get-tuple-element.44.own_ref), channel_id=1, source_target_pairs={{0,8},{4,12},{8,16},{12,20},{16,24},{20,28},{1,9},{5,13},{9,17},{1... | collective-permute-start | bytes 786440 | tf_op jit(solution)/shard_map/ppermute | solution.py:306
  9.1 0.0 copy-start.3
  9.1 0.0 copy-start
  9.1 5.6 %project_q.1.q_ref = bf16[512,512]{1,0:T(8,128)(2,1)S(1)} custom-call(bf16[512,5376]{1,0:T(8,128)(2,1)} %hidden_ref.3, bf16[5376,512]{1,0:T(8,128)(2,1)} %wq_ref.9), custom_call_target="tpu_custom_call" | custom-call | flops 2818572288 | bytes 11010048 | tf_op jit(solution)/shard_map/project_q/pallas_call | solution.py:108
  14.7 1.8 %collective-permute-done.far_ref = bf16[512,256]{1,0:T(8,128)(2,1)S(1)} collective-permute-done((bf16[512,256]{1,0:T(8,128)(2,1)S(1)}, bf16[512,256]{1,0:T(8,128)(2,1)S(1)}, u32[]{:S(2)}, u32[]{:S(2)}) %collective-permute-start) | collective-permute-done | bytes 262176 | tf_op jit(solution)/shard_map/ppermute | solution.py:306
  16.5 0.1 collective-permute-start.1
  16.6 2.5 %collective-permute-start.3 = (bf16[512,256]{1,0:T(8,128)(2,1)S(1)}, bf16[512,256]{1,0:T(8,128)(2,1)S(1)}, u32[]{:S(2)}, u32[]{:S(2)}) collective-permute-start(bf16[512,256]{1,0:T(8,128)(2,1)S(1)} %get-tuple-element.51.own_ref), channel_id=1, source_target_pairs={{0,8},{4,12},{8,16},{12,20},{16,24},{20,28},{1,9},{5,13},{9,17},{1... | collective-permute-start | bytes 786440 | tf_op jit(solution)/shard_map/ppermute | solution.py:306
  19.1 0.1 copy.7.low_ref
  19.3 5.2 %attention.2 = (bf16[512,256]{1,0:T(8,128)(2,1)S(1)}, bf16[512,256]{1,0:T(8,128)(2,1)S(1)}, bf16[512,256]{1,0:T(8,128)(2,1)S(1)}, f32[512,256]{1,0:T(8,128)S(1)}) custom-call(bf16[512,512]{1,0:T(8,128)(2,1)S(1)} %project_q.1.q_ref, bf16[512,512]{1,0:T(8,128)(2,1)S(1)} %copy-done, bf16[512,256]{1,0:T(8,128)(2,1)S(1)} %collective-permute-done.far_ref, ...), custom_call_target="tpu_custom_call" | custom-call | flops 2415919104 | bytes 2097152 | tf_op jit(solution)/shard_map/attention/pallas_call | solution.py:182
  24.5 0.3 collective-permute-start.2
  24.8 3.3 %collective-permute-done.3.far_ref = bf16[512,256]{1,0:T(8,128)(2,1)S(1)} collective-permute-done((bf16[512,256]{1,0:T(8,128)(2,1)S(1)}, bf16[512,256]{1,0:T(8,128)(2,1)S(1)}, u32[]{:S(2)}, u32[]{:S(2)}) %collective-permute-start.3) | collective-permute-done | bytes 262176 | tf_op jit(solution)/shard_map/ppermute | solution.py:306
  28.1 0.1 collective-permute-start.4
  28.2 0.0 collective-permute-done.2
  28.2 0.0 copy-start.1
  28.2 0.1 fusion.7
  28.3 2.3 %collective-permute-start.5 = (bf16[512,256]{1,0:T(8,128)(2,1)S(1)}, bf16[512,256]{1,0:T(8,128)(2,1)S(1)}, u32[]{:S(2)}, u32[]{:S(2)}) collective-permute-start(bf16[512,256]{1,0:T(8,128)(2,1)S(1)} %fusion.7), channel_id=1, source_target_pairs={{8,0},{12,4},{16,8},{20,12},{24,16},{28,20},{9,1},{13,5},{17,9},{2... | collective-permute-start | bytes 786440 | tf_op jit(solution)/shard_map/ppermute | solution.py:327
  30.6 0.0 collective-permute-done.4.near_ref
  30.6 5.2 %attention.3 = (bf16[512,256]{1,0:T(8,128)(2,1)S(1)}, bf16[512,256]{1,0:T(8,128)(2,1)S(1)}, bf16[512,256]{1,0:T(8,128)(2,1)S(1)}, f32[512,256]{1,0:T(8,128)S(1)}) custom-call(bf16[512,512]{1,0:T(8,128)(2,1)S(1)} %project_q.1.q_ref, bf16[512,512]{1,0:T(8,128)(2,1)S(1)} %copy-done, bf16[512,256]{1,0:T(8,128)(2,1)S(1)} %collective-permute-done.3.far_ref, ...), custom_call_target="tpu_custom_call" | custom-call | flops 2415919104 | bytes 2097152 | tf_op jit(solution)/shard_map/attention/pallas_call | solution.py:182
  35.8 3.0 %collective-permute-done.5 = bf16[512,256]{1,0:T(8,128)(2,1)S(1)} collective-permute-done((bf16[512,256]{1,0:T(8,128)(2,1)S(1)}, bf16[512,256]{1,0:T(8,128)(2,1)S(1)}, u32[]{:S(2)}, u32[]{:S(2)}) %collective-permute-start.5) | collective-permute-done | bytes 262176 | tf_op jit(solution)/shard_map/ppermute | solution.py:327
  38.9 1.5 %collective-permute-done.6 = bf16[512,256]{1,0:T(8,128)(2,1)S(1)} collective-permute-done((bf16[512,256]{1,0:T(8,128)(2,1)S(1)}, bf16[512,256]{1,0:T(8,128)(2,1)S(1)}, u32[]{:S(2)}, u32[]{:S(2)}) %collective-permute-start.6) | collective-permute-done | bytes 262176 | tf_op jit(solution)/shard_map/ppermute | solution.py:323
  40.4 0.1 fusion.6
  40.5 3.1 %collective-permute-start.7 = (bf16[512,256]{1,0:T(8,128)(2,1)S(1)}, bf16[512,256]{1,0:T(8,128)(2,1)S(1)}, u32[]{:S(2)}, u32[]{:S(2)}) collective-permute-start(bf16[512,256]{1,0:T(8,128)(2,1)S(1)} %fusion.6), channel_id=1, source_target_pairs={{8,0},{12,4},{16,8},{20,12},{24,16},{28,20},{9,1},{13,5},{17,9},{2... | collective-permute-start | bytes 786440 | tf_op jit(solution)/shard_map/ppermute | solution.py:327
  43.6 1.1 fusion.2.g0_ref
  44.8 6.0 %collective-permute-done.7 = bf16[512,256]{1,0:T(8,128)(2,1)S(1)} collective-permute-done((bf16[512,256]{1,0:T(8,128)(2,1)S(1)}, bf16[512,256]{1,0:T(8,128)(2,1)S(1)}, u32[]{:S(2)}, u32[]{:S(2)}) %collective-permute-start.7) | collective-permute-done | bytes 262176 | tf_op jit(solution)/shard_map/ppermute | solution.py:327
  50.8 0.1 fusion.5.g1_ref
  50.9 2.0 %back_project.4 = bf16[128,768]{1,0:T(8,128)(2,1)S(1)} custom-call(s32[1]{0:T(128)} %bitcast.4.place_ref, bf16[512,256]{1,0:T(8,128)(2,1)S(1)} %get-tuple-element.60.dq0_ref, bf16[512,256]{1,0:T(8,128)(2,1)S(1)} %get-tuple-element.61.dq1_ref, bf16[512,256]{1,0:T(8,128)(2,1)S(1)} %fusion.2.g0_ref, bf16[512,256]{1,0:T(8,128)(2,1)S(1)} %fusion.5.g1_ref, ...), custom_call_target="tpu_custom_call" | custom-call | flops 201326592 | bytes 1769472 | tf_op jit(solution)/shard_map/back_project/pallas_call | solution.py:257
  52.9 1.3 collective-permute-start.8
  54.2 0.1 pad_add_fusion.place_ref
  54.2 4.1 %back_project.6 = bf16[128,2304]{1,0:T(8,128)(2,1)S(1)} custom-call(s32[1]{0:T(128)} %bitcast.4.place_ref, bf16[512,256]{1,0:T(8,128)(2,1)S(1)} %get-tuple-element.60.dq0_ref, bf16[512,256]{1,0:T(8,128)(2,1)S(1)} %get-tuple-element.61.dq1_ref, bf16[512,256]{1,0:T(8,128)(2,1)S(1)} %fusion.2.g0_ref, bf16[512,256]{1,0:T(8,128)(2,1)S(1)} %fusion.5.g1_ref, ...), custom_call_target="tpu_custom_call" | custom-call | flops 603979776 | bytes 5308416 | tf_op jit(solution)/shard_map/back_project/pallas_call | solution.py:257
  58.4 1.3 collective-permute-start.10
  59.7 4.2 %back_project.7 = bf16[128,2304]{1,0:T(8,128)(2,1)S(1)} custom-call(s32[1]{0:T(128)} %bitcast.4.place_ref, bf16[512,256]{1,0:T(8,128)(2,1)S(1)} %get-tuple-element.60.dq0_ref, bf16[512,256]{1,0:T(8,128)(2,1)S(1)} %get-tuple-element.61.dq1_ref, bf16[512,256]{1,0:T(8,128)(2,1)S(1)} %fusion.2.g0_ref, bf16[512,256]{1,0:T(8,128)(2,1)S(1)} %fusion.5.g1_ref, ...), custom_call_target="tpu_custom_call" | custom-call | flops 603979776 | bytes 5308416 | tf_op jit(solution)/shard_map/back_project/pallas_call | solution.py:257
  63.9 1.3 collective-permute-start.16
  65.2 3.5 %collective-permute-start.13 = (bf16[128,768]{1,0:T(8,128)(2,1)S(1)}, bf16[128,768]{1,0:T(8,128)(2,1)S(1)}, u32[]{:S(2)}, u32[]{:S(2)}) collective-permute-start(bf16[128,768]{1,0:T(8,128)(2,1)S(1)} %add_convert_fusion.7), channel_id=1, source_target_pairs={{1,2},{2,1},{5,6},{6,5},{9,10},{10,9},{13,14},{14,13},{17,18},{18,... | collective-permute-start | bytes 589832 | tf_op jit(solution)/shard_map/ppermute | solution.py:348
  68.7 10.0 %back_project.5 = (bf16[128,768]{1,0:T(8,128)(2,1)S(1)}, bf16[128,768]{1,0:T(8,128)(2,1)S(1)}, bf16[128,768]{1,0:T(8,128)(2,1)S(1)}, bf16[128,2304]{1,0:T(8,128)...) custom-call(s32[3]{0:T(128)S(1)} %pad_add_fusion.place_ref, ...), custom_call_target="tpu_custom_call" | custom-call | flops 4227858432 | bytes 15138816 | tf_op jit(solution)/shard_map/back_project/pallas_call | solution.py:257
  78.8 1.3 collective-permute-start.9
  80.1 0.1 add_convert_fusion.6
  80.1 11.6 %collective-permute-done.9 = bf16[128,768]{1,0:T(8,128)(2,1)S(1)} collective-permute-done((bf16[128,768]{1,0:T(8,128)(2,1)S(1)}, bf16[128,768]{1,0:T(8,128)(2,1)S(1)}, u32[]{:S(2)}, u32[]{:S(2)}) %collective-permute-start.9) | collective-permute-done | bytes 196640 | tf_op jit(solution)/shard_map/ppermute | solution.py:348
  91.8 0.1 add_convert_fusion.5
  91.9 3.5 %collective-permute-start.11 = (bf16[128,2304]{1,0:T(8,128)(2,1)S(1)}, bf16[128,2304]{1,0:T(8,128)(2,1)S(1)}, u32[]{:S(2)}, u32[]{:S(2)}) collective-permute-start(bf16[128,2304]{1,0:T(8,128)(2,1)S(1)} %add_convert_fusion.5), channel_id=1, source_target_pairs={{1,2},{2,1},{5,6},{6,5},{9,10},{10,9},{13,14},{14,13},{17,18},{18,... | collective-permute-start | bytes 1769480 | tf_op jit(solution)/shard_map/ppermute | solution.py:348
  95.4 1.3 collective-permute-start.15
  96.7 0.1 add_convert_fusion.3
  96.9 2.4 %collective-permute-start.17 = (bf16[128,2304]{1,0:T(8,128)(2,1)S(1)}, bf16[128,2304]{1,0:T(8,128)(2,1)S(1)}, u32[]{:S(2)}, u32[]{:S(2)}) collective-permute-start(bf16[128,2304]{1,0:T(8,128)(2,1)S(1)} %add_convert_fusion.3), channel_id=1, source_target_pairs={{1,2},{2,1},{5,6},{6,5},{9,10},{10,9},{13,14},{14,13},{17,18},{18,... | collective-permute-start | bytes 1769480 | tf_op jit(solution)/shard_map/ppermute | solution.py:348
  99.2 1.3 collective-permute-start.20
  100.5 9.5 %collective-permute-done.11 = bf16[128,2304]{1,0:T(8,128)(2,1)S(1)} collective-permute-done((bf16[128,2304]{1,0:T(8,128)(2,1)S(1)}, bf16[128,2304]{1,0:T(8,128)(2,1)S(1)}, u32[]{:S(2)}, u32[]{:S(2)}) %collective-permute-start.11) | collective-permute-done | bytes 589856 | tf_op jit(solution)/shard_map/ppermute | solution.py:348
  110.1 3.5 %collective-permute-start.12 = (bf16[128,768]{1,0:T(8,128)(2,1)S(1)}, bf16[128,768]{1,0:T(8,128)(2,1)S(1)}, u32[]{:S(2)}, u32[]{:S(2)}) collective-permute-start(bf16[128,768]{1,0:T(8,128)(2,1)S(1)} %add_convert_fusion.8), channel_id=1, source_target_pairs={{1,2},{2,1},{5,6},{6,5},{9,10},{10,9},{13,14},{14,13},{17,18},{18,... | collective-permute-start | bytes 589832 | tf_op jit(solution)/shard_map/ppermute | solution.py:348
  113.6 0.0 collective-permute-done.15
  113.6 0.1 add_convert_fusion.4
  113.7 8.6 %collective-permute-done.17 = bf16[128,2304]{1,0:T(8,128)(2,1)S(1)} collective-permute-done((bf16[128,2304]{1,0:T(8,128)(2,1)S(1)}, bf16[128,2304]{1,0:T(8,128)(2,1)S(1)}, u32[]{:S(2)}, u32[]{:S(2)}) %collective-permute-start.17) | collective-permute-done | bytes 589856 | tf_op jit(solution)/shard_map/ppermute | solution.py:348
  122.3 3.5 %collective-permute-start.18 = (bf16[128,2304]{1,0:T(8,128)(2,1)S(1)}, bf16[128,2304]{1,0:T(8,128)(2,1)S(1)}, u32[]{:S(2)}, u32[]{:S(2)}) collective-permute-start(bf16[128,2304]{1,0:T(8,128)(2,1)S(1)} %add_convert_fusion.4), channel_id=1, source_target_pairs={{1,2},{2,1},{5,6},{6,5},{9,10},{10,9},{13,14},{14,13},{17,18},{18,... | collective-permute-start | bytes 1769480 | tf_op jit(solution)/shard_map/ppermute | solution.py:348
  125.8 0.1 add_convert_fusion.2
  125.9 0.1 collective-permute-start.19
  126.0 0.1 add_convert_fusion
  126.1 2.1 %collective-permute-start.22 = (bf16[128,2304]{1,0:T(8,128)(2,1)S(1)}, bf16[128,2304]{1,0:T(8,128)(2,1)S(1)}, u32[]{:S(2)}, u32[]{:S(2)}) collective-permute-start(bf16[128,2304]{1,0:T(8,128)(2,1)S(1)} %add_convert_fusion), channel_id=1, source_target_pairs={{0,1},{3,2},{1,0},{2,3},{4,5},{7,6},{5,4},{6,7},{8,9},{11,10},{9,8... | collective-permute-start | bytes 1769480 | tf_op jit(solution)/shard_map/ppermute | solution.py:348
  128.2 0.1 add_convert_fusion.1
  128.4 2.4 %collective-permute-start.21 = (bf16[128,2304]{1,0:T(8,128)(2,1)S(1)}, bf16[128,2304]{1,0:T(8,128)(2,1)S(1)}, u32[]{:S(2)}, u32[]{:S(2)}) collective-permute-start(bf16[128,2304]{1,0:T(8,128)(2,1)S(1)} %add_convert_fusion.1), channel_id=1, source_target_pairs={{1,2},{2,1},{5,6},{6,5},{9,10},{10,9},{13,14},{14,13},{17,18},{18,... | collective-permute-start | bytes 1769480 | tf_op jit(solution)/shard_map/ppermute | solution.py:348
  130.7 0.1 convert_add_fusion.4
  130.8 9.6 %collective-permute-done.18 = bf16[128,2304]{1,0:T(8,128)(2,1)S(1)} collective-permute-done((bf16[128,2304]{1,0:T(8,128)(2,1)S(1)}, bf16[128,2304]{1,0:T(8,128)(2,1)S(1)}, u32[]{:S(2)}, u32[]{:S(2)}) %collective-permute-start.18) | collective-permute-done | bytes 589856 | tf_op jit(solution)/shard_map/ppermute | solution.py:348
  140.4 1.8 %collective-permute-done.19 = bf16[128,2304]{1,0:T(8,128)(2,1)S(1)} collective-permute-done((bf16[128,2304]{1,0:T(8,128)(2,1)S(1)}, bf16[128,2304]{1,0:T(8,128)(2,1)S(1)}, u32[]{:S(2)}, u32[]{:S(2)}) %collective-permute-start.19) | collective-permute-done | bytes 589856 | tf_op jit(solution)/shard_map/ppermute | solution.py:348
  142.2 0.2 convert_add_fusion.1
  142.4 6.4 %collective-permute-done.22 = bf16[128,2304]{1,0:T(8,128)(2,1)S(1)} collective-permute-done((bf16[128,2304]{1,0:T(8,128)(2,1)S(1)}, bf16[128,2304]{1,0:T(8,128)(2,1)S(1)}, u32[]{:S(2)}, u32[]{:S(2)}) %collective-permute-start.22) | collective-permute-done | bytes 589856 | tf_op jit(solution)/shard_map/ppermute | solution.py:348
  148.8 0.7 collective-permute-done.21
  149.6 0.2 convert_add_fusion
  149.8 1.7 %pad_maximum_fusion = f32[128,5376]{1,0:T(8,128)} fusion(f32[128,2304]{1,0:T(8,128)S(1)} %convert_add_fusion, f32[128,2304]{1,0:T(8,128)S(1)} %convert_add_fusion.1, f32[128,768]{1,0:T(8,128)S(1)} %convert_add_fusion.4), kind=kLoop, calls=%fused_computation | loop fusion | flops 1376256 | bytes 5505024 | tf_op jit(solution)/shard_map/concatenate | solution.py:366
  (20 shorter events, 0.2 us)
Async XLA Ops:
  5.6 10.8 %collective-permute-start = (bf16[512,256]{1,0:T(8,128)(2,1)S(1)}, bf16[512,256]{1,0:T(8,128)(2,1)S(1)}, u32[]{:S(2)}, u32[]{:S(2)}) collective-permute-start(bf16[512,256]{1,0:T(8,128)(2,1)S(1)} %get-tuple-element.44.own_ref), channel_id=1, source_target_pairs={{0,8},{4,12},{8,16},{12,20},{16,24},{20,28},{1,9},{5,13},{9,17},{1... | collective-permute-start | bytes 786440 | tf_op jit(solution)/shard_map/ppermute | solution.py:306
  9.1 10.0 %copy-start.3 = (s32[512]{0:T(512)S(1)}, s32[512]{0:T(512)}, u32[]{:S(2)}) copy-start(s32[512]{0:T(512)} %param.11) | copy-start | bytes 6148
  9.1 10.2 %copy-start = (bf16[512,512]{1,0:T(8,128)(2,1)S(1)}, bf16[512,512]{1,0:T(8,128)(2,1)}, u32[]{:S(2)}) copy-start(bf16[512,512]{1,0:T(8,128)(2,1)} %do_ref.3) | copy-start | bytes 1572868
  16.5 2.8 %collective-permute-start.1 = (bf16[512,256]{1,0:T(8,128)(2,1)S(1)}, bf16[512,256]{1,0:T(8,128)(2,1)S(1)}, u32[]{:S(2)}, u32[]{:S(2)}) collective-permute-start(bf16[512,256]{1,0:T(8,128)(2,1)S(1)} %broadcast_select_fusion.1), channel_id=1, source_target_pairs={{0,4},{4,0},{8,12},{12,8},{16,20},{20,16},{24,28},{28,24},{1,5},{5... | collective-permute-start | bytes 786440 | tf_op jit(solution)/shard_map/ppermute | solution.py:318
  16.6 11.5 %collective-permute-start.3 = (bf16[512,256]{1,0:T(8,128)(2,1)S(1)}, bf16[512,256]{1,0:T(8,128)(2,1)S(1)}, u32[]{:S(2)}, u32[]{:S(2)}) collective-permute-start(bf16[512,256]{1,0:T(8,128)(2,1)S(1)} %get-tuple-element.51.own_ref), channel_id=1, source_target_pairs={{0,8},{4,12},{8,16},{12,20},{16,24},{20,28},{1,9},{5,13},{9,17},{1... | collective-permute-start | bytes 786440 | tf_op jit(solution)/shard_map/ppermute | solution.py:306
  24.5 3.7 %collective-permute-start.2 = (bf16[512,256]{1,0:T(8,128)(2,1)S(1)}, bf16[512,256]{1,0:T(8,128)(2,1)S(1)}, u32[]{:S(2)}, u32[]{:S(2)}) collective-permute-start(bf16[512,256]{1,0:T(8,128)(2,1)S(1)} %get-tuple-element.49), channel_id=1, source_target_pairs={{0,4},{4,0},{8,12},{12,8},{16,20},{20,16},{24,28},{28,24},{1,5},{5... | collective-permute-start | bytes 786440 | tf_op jit(solution)/shard_map/ppermute | solution.py:323
  28.1 2.5 %collective-permute-start.4 = (bf16[512,256]{1,0:T(8,128)(2,1)S(1)}, bf16[512,256]{1,0:T(8,128)(2,1)S(1)}, u32[]{:S(2)}, u32[]{:S(2)}) collective-permute-start(bf16[512,256]{1,0:T(8,128)(2,1)S(1)} %broadcast_select_fusion), channel_id=1, source_target_pairs={{0,4},{4,0},{8,12},{12,8},{16,20},{20,16},{24,28},{28,24},{1,5},{5... | collective-permute-start | bytes 786440 | tf_op jit(solution)/shard_map/ppermute | solution.py:318
  28.2 2.4 %copy-start.1 = (bf16[512,256]{1,0:T(8,128)(2,1)}, bf16[512,256]{1,0:T(8,128)(2,1)S(1)}, u32[]{:S(2)}) copy-start(bf16[512,256]{1,0:T(8,128)(2,1)S(1)} %collective-permute-done.2) | copy-start | bytes 786436
  28.3 10.6 %collective-permute-start.5 = (bf16[512,256]{1,0:T(8,128)(2,1)S(1)}, bf16[512,256]{1,0:T(8,128)(2,1)S(1)}, u32[]{:S(2)}, u32[]{:S(2)}) collective-permute-start(bf16[512,256]{1,0:T(8,128)(2,1)S(1)} %fusion.7), channel_id=1, source_target_pairs={{8,0},{12,4},{16,8},{20,12},{24,16},{28,20},{9,1},{13,5},{17,9},{2... | collective-permute-start | bytes 786440 | tf_op jit(solution)/shard_map/ppermute | solution.py:327
  38.9 1.6 %copy-start.2 = (bf16[512,256]{1,0:T(8,128)(2,1)}, bf16[512,256]{1,0:T(8,128)(2,1)S(1)}, u32[]{:S(2)}) copy-start(bf16[512,256]{1,0:T(8,128)(2,1)S(1)} %collective-permute-done.5) | copy-start | bytes 786436
  38.9 1.5 %collective-permute-start.6 = (bf16[512,256]{1,0:T(8,128)(2,1)S(1)}, bf16[512,256]{1,0:T(8,128)(2,1)S(1)}, u32[]{:S(2)}, u32[]{:S(2)}) collective-permute-start(bf16[512,256]{1,0:T(8,128)(2,1)S(1)} %get-tuple-element.59), channel_id=1, source_target_pairs={{0,4},{4,0},{8,12},{12,8},{16,20},{20,16},{24,28},{28,24},{1,5},{5... | collective-permute-start | bytes 786440 | tf_op jit(solution)/shard_map/ppermute | solution.py:323
  40.5 10.2 %collective-permute-start.7 = (bf16[512,256]{1,0:T(8,128)(2,1)S(1)}, bf16[512,256]{1,0:T(8,128)(2,1)S(1)}, u32[]{:S(2)}, u32[]{:S(2)}) collective-permute-start(bf16[512,256]{1,0:T(8,128)(2,1)S(1)} %fusion.6), channel_id=1, source_target_pairs={{8,0},{12,4},{16,8},{20,12},{24,16},{28,20},{9,1},{13,5},{17,9},{2... | collective-permute-start | bytes 786440 | tf_op jit(solution)/shard_map/ppermute | solution.py:327
  52.9 12.3 %collective-permute-start.8 = (bf16[128,768]{1,0:T(8,128)(2,1)S(1)}, bf16[128,768]{1,0:T(8,128)(2,1)S(1)}, u32[]{:S(2)}, u32[]{:S(2)}) collective-permute-start(bf16[128,768]{1,0:T(8,128)(2,1)S(1)} %back_project.4), channel_id=1, source_target_pairs={{0,1},{3,2},{4,5},{7,6},{8,9},{11,10},{12,13},{15,14},{16,17},{19,... | collective-permute-start | bytes 589832 | tf_op jit(solution)/shard_map/ppermute | solution.py:348
  58.4 33.4 %collective-permute-start.10 = (bf16[128,2304]{1,0:T(8,128)(2,1)S(1)}, bf16[128,2304]{1,0:T(8,128)(2,1)S(1)}, u32[]{:S(2)}, u32[]{:S(2)}) collective-permute-start(bf16[128,2304]{1,0:T(8,128)(2,1)S(1)} %back_project.6), channel_id=1, source_target_pairs={{0,1},{3,2},{4,5},{7,6},{8,9},{11,10},{12,13},{15,14},{16,17},{19,... | collective-permute-start | bytes 1769480 | tf_op jit(solution)/shard_map/ppermute | solution.py:348
  63.9 32.8 %collective-permute-start.16 = (bf16[128,2304]{1,0:T(8,128)(2,1)S(1)}, bf16[128,2304]{1,0:T(8,128)(2,1)S(1)}, u32[]{:S(2)}, u32[]{:S(2)}) collective-permute-start(bf16[128,2304]{1,0:T(8,128)(2,1)S(1)} %back_project.7), channel_id=1, source_target_pairs={{0,1},{3,2},{4,5},{7,6},{8,9},{11,10},{12,13},{15,14},{16,17},{19,... | collective-permute-start | bytes 1769480 | tf_op jit(solution)/shard_map/ppermute | solution.py:348
  65.2 14.8 %collective-permute-start.13 = (bf16[128,768]{1,0:T(8,128)(2,1)S(1)}, bf16[128,768]{1,0:T(8,128)(2,1)S(1)}, u32[]{:S(2)}, u32[]{:S(2)}) collective-permute-start(bf16[128,768]{1,0:T(8,128)(2,1)S(1)} %add_convert_fusion.7), channel_id=1, source_target_pairs={{1,2},{2,1},{5,6},{6,5},{9,10},{10,9},{13,14},{14,13},{17,18},{18,... | collective-permute-start | bytes 589832 | tf_op jit(solution)/shard_map/ppermute | solution.py:348
  78.8 12.9 %collective-permute-start.9 = (bf16[128,768]{1,0:T(8,128)(2,1)S(1)}, bf16[128,768]{1,0:T(8,128)(2,1)S(1)}, u32[]{:S(2)}, u32[]{:S(2)}) collective-permute-start(bf16[128,768]{1,0:T(8,128)(2,1)S(1)} %get-tuple-element.66), channel_id=1, source_target_pairs={{0,1},{3,2},{4,5},{7,6},{8,9},{11,10},{12,13},{15,14},{16,17},{19,... | collective-permute-start | bytes 589832 | tf_op jit(solution)/shard_map/ppermute | solution.py:348
  91.7 39.0 %collective-permute-start.14 = (bf16[128,768]{1,0:T(8,128)(2,1)S(1)}, bf16[128,768]{1,0:T(8,128)(2,1)S(1)}, u32[]{:S(2)}, u32[]{:S(2)}) collective-permute-start(bf16[128,768]{1,0:T(8,128)(2,1)S(1)} %add_convert_fusion.6), channel_id=1, source_target_pairs={{0,1},{3,2},{1,0},{2,3},{4,5},{7,6},{5,4},{6,7},{8,9},{11,10},{9,8... | collective-permute-start | bytes 589832 | tf_op jit(solution)/shard_map/ppermute | solution.py:348
  91.9 18.2 %collective-permute-start.11 = (bf16[128,2304]{1,0:T(8,128)(2,1)S(1)}, bf16[128,2304]{1,0:T(8,128)(2,1)S(1)}, u32[]{:S(2)}, u32[]{:S(2)}) collective-permute-start(bf16[128,2304]{1,0:T(8,128)(2,1)S(1)} %add_convert_fusion.5), channel_id=1, source_target_pairs={{1,2},{2,1},{5,6},{6,5},{9,10},{10,9},{13,14},{14,13},{17,18},{18,... | collective-permute-start | bytes 1769480 | tf_op jit(solution)/shard_map/ppermute | solution.py:348
  95.4 18.2 %collective-permute-start.15 = (bf16[128,2304]{1,0:T(8,128)(2,1)S(1)}, bf16[128,2304]{1,0:T(8,128)(2,1)S(1)}, u32[]{:S(2)}, u32[]{:S(2)}) collective-permute-start(bf16[128,2304]{1,0:T(8,128)(2,1)S(1)} %get-tuple-element.72), channel_id=1, source_target_pairs={{0,1},{3,2},{4,5},{7,6},{8,9},{11,10},{12,13},{15,14},{16,17},{19,... | collective-permute-start | bytes 1769480 | tf_op jit(solution)/shard_map/ppermute | solution.py:348
  96.9 25.4 %collective-permute-start.17 = (bf16[128,2304]{1,0:T(8,128)(2,1)S(1)}, bf16[128,2304]{1,0:T(8,128)(2,1)S(1)}, u32[]{:S(2)}, u32[]{:S(2)}) collective-permute-start(bf16[128,2304]{1,0:T(8,128)(2,1)S(1)} %add_convert_fusion.3), channel_id=1, source_target_pairs={{1,2},{2,1},{5,6},{6,5},{9,10},{10,9},{13,14},{14,13},{17,18},{18,... | collective-permute-start | bytes 1769480 | tf_op jit(solution)/shard_map/ppermute | solution.py:348
  99.2 26.9 %collective-permute-start.20 = (bf16[128,2304]{1,0:T(8,128)(2,1)S(1)}, bf16[128,2304]{1,0:T(8,128)(2,1)S(1)}, u32[]{:S(2)}, u32[]{:S(2)}) collective-permute-start(bf16[128,2304]{1,0:T(8,128)(2,1)S(1)} %get-tuple-element.79), channel_id=1, source_target_pairs={{0,1},{3,2},{4,5},{7,6},{8,9},{11,10},{12,13},{15,14},{16,17},{19,... | collective-permute-start | bytes 1769480 | tf_op jit(solution)/shard_map/ppermute | solution.py:348
  110.1 18.3 %collective-permute-start.12 = (bf16[128,768]{1,0:T(8,128)(2,1)S(1)}, bf16[128,768]{1,0:T(8,128)(2,1)S(1)}, u32[]{:S(2)}, u32[]{:S(2)}) collective-permute-start(bf16[128,768]{1,0:T(8,128)(2,1)S(1)} %add_convert_fusion.8), channel_id=1, source_target_pairs={{1,2},{2,1},{5,6},{6,5},{9,10},{10,9},{13,14},{14,13},{17,18},{18,... | collective-permute-start | bytes 589832 | tf_op jit(solution)/shard_map/ppermute | solution.py:348
  122.3 18.1 %collective-permute-start.18 = (bf16[128,2304]{1,0:T(8,128)(2,1)S(1)}, bf16[128,2304]{1,0:T(8,128)(2,1)S(1)}, u32[]{:S(2)}, u32[]{:S(2)}) collective-permute-start(bf16[128,2304]{1,0:T(8,128)(2,1)S(1)} %add_convert_fusion.4), channel_id=1, source_target_pairs={{1,2},{2,1},{5,6},{6,5},{9,10},{10,9},{13,14},{14,13},{17,18},{18,... | collective-permute-start | bytes 1769480 | tf_op jit(solution)/shard_map/ppermute | solution.py:348
  125.9 16.3 %collective-permute-start.19 = (bf16[128,2304]{1,0:T(8,128)(2,1)S(1)}, bf16[128,2304]{1,0:T(8,128)(2,1)S(1)}, u32[]{:S(2)}, u32[]{:S(2)}) collective-permute-start(bf16[128,2304]{1,0:T(8,128)(2,1)S(1)} %add_convert_fusion.2), channel_id=1, source_target_pairs={{0,1},{3,2},{1,0},{2,3},{4,5},{7,6},{5,4},{6,7},{8,9},{11,10},{9,8... | collective-permute-start | bytes 1769480 | tf_op jit(solution)/shard_map/ppermute | solution.py:348
  126.1 22.7 %collective-permute-start.22 = (bf16[128,2304]{1,0:T(8,128)(2,1)S(1)}, bf16[128,2304]{1,0:T(8,128)(2,1)S(1)}, u32[]{:S(2)}, u32[]{:S(2)}) collective-permute-start(bf16[128,2304]{1,0:T(8,128)(2,1)S(1)} %add_convert_fusion), channel_id=1, source_target_pairs={{0,1},{3,2},{1,0},{2,3},{4,5},{7,6},{5,4},{6,7},{8,9},{11,10},{9,8... | collective-permute-start | bytes 1769480 | tf_op jit(solution)/shard_map/ppermute | solution.py:348
  128.4 21.2 %collective-permute-start.21 = (bf16[128,2304]{1,0:T(8,128)(2,1)S(1)}, bf16[128,2304]{1,0:T(8,128)(2,1)S(1)}, u32[]{:S(2)}, u32[]{:S(2)}) collective-permute-start(bf16[128,2304]{1,0:T(8,128)(2,1)S(1)} %add_convert_fusion.1), channel_id=1, source_target_pairs={{1,2},{2,1},{5,6},{6,5},{9,10},{10,9},{13,14},{14,13},{17,18},{18,... | collective-permute-start | bytes 1769480 | tf_op jit(solution)/shard_map/ppermute | solution.py:348

commit v4 on v3

--- a/solution.py
+++ b/solution.py
@@ -18,7 +18,7 @@
 KV_CHUNKS = ((0, 768), (768, 1536), (2304, 1536), (3840, 1024), (4864, 512))
 Q_CHUNKS = ((0, 768), (768, 1536), (2304, 1536), (3840, 1536))
 TILE = 768
-PIECES = ((0, 768), (768, 2304), (3072, 2304))
+PIECES = ((0, 1536), (1536, 1536), (3072, 2304))
 OUTER_DEPTH, MIDDLE_DEPTH = 3, 2
 PROJECT_LIMIT = 18 * MIB
 ATTENTION_LIMIT = 14 * MIB

time: 153 us -> 149 us (0.974)
  starting transfers between devices: 40.3 us -> 37.1 us
    ppermute x15, starting transfers between devices: 28.5 us -> 25.3 us  [send(): sent.append(lax.ppermute(payload, 'head', pairs))]
  transfers between devices with their start and end apart: 23 -> 23, of which waited for: 12 -> 14; matrix products, arithmetic and copies ran while one was open for 2% -> 2% of each run, Pallas kernels for 23% -> 22%
where the time goes in v4:
time: 149 us; the launch traced here: 148 us
  waiting for transfers between devices  63.9 us (43%)
  Pallas kernels  41.6 us (28%)
  starting transfers between devices  37.1 us (25%)
  other arithmetic  4.7 us (3%)
    ppermute x15, waiting for transfers between devices, send(): sent.append(lax.ppermute(payload, 'head', pairs))  48.2 us
    ppermute x15, starting transfers between devices, send(): sent.append(lax.ppermute(payload, 'head', pairs))  25.3 us
    pallas_call x4, Pallas kernels, back_project(): pl.pallas_call(functools.partial(back_kernel, spans), grid_spec=grid_spec...  20 us
    pallas_call x2, Pallas kernels, attend(): pl.pallas_call(attention_kernel, grid=(1,), in_specs=[column, column, who...  10.4 us
    ppermute x2, waiting for transfers between devices, shards(): returned = lax.ppermute(passed, 'ctx', behind)  9.02 us
    ppermute x2, starting transfers between devices, shards(): far = [lax.ppermute(x, 'ctx', ahead) for x in own]  5.9 us
    pallas_call x1, Pallas kernels, project_keys_values(): pl.pallas_call(project_kernel, in_specs=[hbm] * 3, out_specs=[vmem] * hea...  5.63 us
    pallas_call x1, Pallas kernels, project_queries(): pl.pallas_call(query_kernel, in_specs=[hbm] * 2, out_specs=pl.BlockSpec(m...  5.6 us
  transfers between devices with their start and end apart: 23, of which 14 were waited for; matrix products, arithmetic and copies ran while one was open for 2% of the time, Pallas kernels for 22%

profile of v4, /device:TPU:12, one launch (start us, length us, event | category | flops | bytes accessed | tf_op | source)
XLA Modules:
  0.0 147.9 jit_solution(13133339738488850828)
XLA Ops:
  0.0 5.6 %project_kv.1 = (bf16[512,256]{1,0:T(8,128)(2,1)S(1)}, bf16[512,256]{1,0:T(8,128)(2,1)S(1)}) custom-call(bf16[512,5376]{1,0:T(8,128)(2,1)} %hidden_ref.3, bf16[5376,256]{1,0:T(8,128)(2,1)} %wk_ref.9, bf16[5376,256]{1,0:T(8,128)(2,1)} %wv_ref.9), custom_call_target="tpu_custom_call" | custom-call | flops 2818572288 | bytes 11010048 | tf_op jit(solution)/shard_map/project_kv/pallas_call | solution.py:77
  5.6 3.4 %collective-permute-start = (bf16[512,256]{1,0:T(8,128)(2,1)S(1)}, bf16[512,256]{1,0:T(8,128)(2,1)S(1)}, u32[]{:S(2)}, u32[]{:S(2)}) collective-permute-start(bf16[512,256]{1,0:T(8,128)(2,1)S(1)} %get-tuple-element.44.own_ref), channel_id=1, source_target_pairs={{0,8},{4,12},{8,16},{12,20},{16,24},{20,28},{1,9},{5,13},{9,17},{1... | collective-permute-start | bytes 786440 | tf_op jit(solution)/shard_map/ppermute | solution.py:306
  9.1 0.0 copy-start.3
  9.1 0.0 copy-start
  9.1 5.6 %project_q.1.q_ref = bf16[512,512]{1,0:T(8,128)(2,1)S(1)} custom-call(bf16[512,5376]{1,0:T(8,128)(2,1)} %hidden_ref.3, bf16[5376,512]{1,0:T(8,128)(2,1)} %wq_ref.9), custom_call_target="tpu_custom_call" | custom-call | flops 2818572288 | bytes 11010048 | tf_op jit(solution)/shard_map/project_q/pallas_call | solution.py:108
  14.7 1.8 %collective-permute-done.far_ref = bf16[512,256]{1,0:T(8,128)(2,1)S(1)} collective-permute-done((bf16[512,256]{1,0:T(8,128)(2,1)S(1)}, bf16[512,256]{1,0:T(8,128)(2,1)S(1)}, u32[]{:S(2)}, u32[]{:S(2)}) %collective-permute-start) | collective-permute-done | bytes 262176 | tf_op jit(solution)/shard_map/ppermute | solution.py:306
  16.5 0.1 collective-permute-start.1
  16.6 2.5 %collective-permute-start.3 = (bf16[512,256]{1,0:T(8,128)(2,1)S(1)}, bf16[512,256]{1,0:T(8,128)(2,1)S(1)}, u32[]{:S(2)}, u32[]{:S(2)}) collective-permute-start(bf16[512,256]{1,0:T(8,128)(2,1)S(1)} %get-tuple-element.51.own_ref), channel_id=1, source_target_pairs={{0,8},{4,12},{8,16},{12,20},{16,24},{20,28},{1,9},{5,13},{9,17},{1... | collective-permute-start | bytes 786440 | tf_op jit(solution)/shard_map/ppermute | solution.py:306
  19.1 0.1 copy.7.low_ref
  19.3 5.2 %attention.2 = (bf16[512,256]{1,0:T(8,128)(2,1)S(1)}, bf16[512,256]{1,0:T(8,128)(2,1)S(1)}, bf16[512,256]{1,0:T(8,128)(2,1)S(1)}, f32[512,256]{1,0:T(8,128)S(1)}) custom-call(bf16[512,512]{1,0:T(8,128)(2,1)S(1)} %project_q.1.q_ref, bf16[512,512]{1,0:T(8,128)(2,1)S(1)} %copy-done, bf16[512,256]{1,0:T(8,128)(2,1)S(1)} %collective-permute-done.far_ref, ...), custom_call_target="tpu_custom_call" | custom-call | flops 2415919104 | bytes 2097152 | tf_op jit(solution)/shard_map/attention/pallas_call | solution.py:182
  24.5 0.3 collective-permute-start.2
  24.8 3.3 %collective-permute-done.3.far_ref = bf16[512,256]{1,0:T(8,128)(2,1)S(1)} collective-permute-done((bf16[512,256]{1,0:T(8,128)(2,1)S(1)}, bf16[512,256]{1,0:T(8,128)(2,1)S(1)}, u32[]{:S(2)}, u32[]{:S(2)}) %collective-permute-start.3) | collective-permute-done | bytes 262176 | tf_op jit(solution)/shard_map/ppermute | solution.py:306
  28.1 0.1 collective-permute-start.4
  28.2 0.0 copy-start.1
  28.2 0.1 fusion.7
  28.3 2.3 %collective-permute-start.5 = (bf16[512,256]{1,0:T(8,128)(2,1)S(1)}, bf16[512,256]{1,0:T(8,128)(2,1)S(1)}, u32[]{:S(2)}, u32[]{:S(2)}) collective-permute-start(bf16[512,256]{1,0:T(8,128)(2,1)S(1)} %fusion.7), channel_id=1, source_target_pairs={{8,0},{12,4},{16,8},{20,12},{24,16},{28,20},{9,1},{13,5},{17,9},{2... | collective-permute-start | bytes 786440 | tf_op jit(solution)/shard_map/ppermute | solution.py:327
  30.6 5.2 %attention.3 = (bf16[512,256]{1,0:T(8,128)(2,1)S(1)}, bf16[512,256]{1,0:T(8,128)(2,1)S(1)}, bf16[512,256]{1,0:T(8,128)(2,1)S(1)}, f32[512,256]{1,0:T(8,128)S(1)}) custom-call(bf16[512,512]{1,0:T(8,128)(2,1)S(1)} %project_q.1.q_ref, bf16[512,512]{1,0:T(8,128)(2,1)S(1)} %copy-done, bf16[512,256]{1,0:T(8,128)(2,1)S(1)} %collective-permute-done.3.far_ref, ...), custom_call_target="tpu_custom_call" | custom-call | flops 2415919104 | bytes 2097152 | tf_op jit(solution)/shard_map/attention/pallas_call | solution.py:182
  35.8 3.0 %collective-permute-done.5 = bf16[512,256]{1,0:T(8,128)(2,1)S(1)} collective-permute-done((bf16[512,256]{1,0:T(8,128)(2,1)S(1)}, bf16[512,256]{1,0:T(8,128)(2,1)S(1)}, u32[]{:S(2)}, u32[]{:S(2)}) %collective-permute-start.5) | collective-permute-done | bytes 262176 | tf_op jit(solution)/shard_map/ppermute | solution.py:327
  38.9 1.5 %collective-permute-done.6 = bf16[512,256]{1,0:T(8,128)(2,1)S(1)} collective-permute-done((bf16[512,256]{1,0:T(8,128)(2,1)S(1)}, bf16[512,256]{1,0:T(8,128)(2,1)S(1)}, u32[]{:S(2)}, u32[]{:S(2)}) %collective-permute-start.6) | collective-permute-done | bytes 262176 | tf_op jit(solution)/shard_map/ppermute | solution.py:323
  40.4 0.1 fusion.6
  40.5 3.1 %collective-permute-start.7 = (bf16[512,256]{1,0:T(8,128)(2,1)S(1)}, bf16[512,256]{1,0:T(8,128)(2,1)S(1)}, u32[]{:S(2)}, u32[]{:S(2)}) collective-permute-start(bf16[512,256]{1,0:T(8,128)(2,1)S(1)} %fusion.6), channel_id=1, source_target_pairs={{8,0},{12,4},{16,8},{20,12},{24,16},{28,20},{9,1},{13,5},{17,9},{2... | collective-permute-start | bytes 786440 | tf_op jit(solution)/shard_map/ppermute | solution.py:327
  43.6 1.1 fusion.2.g0_ref
  44.8 6.0 %collective-permute-done.7 = bf16[512,256]{1,0:T(8,128)(2,1)S(1)} collective-permute-done((bf16[512,256]{1,0:T(8,128)(2,1)S(1)}, bf16[512,256]{1,0:T(8,128)(2,1)S(1)}, u32[]{:S(2)}, u32[]{:S(2)}) %collective-permute-start.7) | collective-permute-done | bytes 262176 | tf_op jit(solution)/shard_map/ppermute | solution.py:327
  50.8 0.1 fusion.5.g1_ref
  50.9 2.8 %back_project.4 = bf16[128,1536]{1,0:T(8,128)(2,1)S(1)} custom-call(s32[1]{0:T(128)} %bitcast.4.place_ref, bf16[512,256]{1,0:T(8,128)(2,1)S(1)} %get-tuple-element.60.dq0_ref, bf16[512,256]{1,0:T(8,128)(2,1)S(1)} %get-tuple-element.61.dq1_ref, bf16[512,256]{1,0:T(8,128)(2,1)S(1)} %fusion.2.g0_ref, bf16[512,256]{1,0:T(8,128)(2,1)S(1)} %fusion.5.g1_ref, ...), custom_call_target="tpu_custom_call" | custom-call | flops 402653184 | bytes 3538944 | tf_op jit(solution)/shard_map/back_project/pallas_call | solution.py:257
  53.7 1.3 collective-permute-start.8
  55.0 0.1 pad_add_fusion.place_ref
  55.1 2.8 %back_project.6 = bf16[128,1536]{1,0:T(8,128)(2,1)S(1)} custom-call(s32[1]{0:T(128)} %bitcast.4.place_ref, bf16[512,256]{1,0:T(8,128)(2,1)S(1)} %get-tuple-element.60.dq0_ref, bf16[512,256]{1,0:T(8,128)(2,1)S(1)} %get-tuple-element.61.dq1_ref, bf16[512,256]{1,0:T(8,128)(2,1)S(1)} %fusion.2.g0_ref, bf16[512,256]{1,0:T(8,128)(2,1)S(1)} %fusion.5.g1_ref, ...), custom_call_target="tpu_custom_call" | custom-call | flops 402653184 | bytes 3538944 | tf_op jit(solution)/shard_map/back_project/pallas_call | solution.py:257
  57.9 1.3 collective-permute-start.10
  59.2 4.2 %back_project.7 = bf16[128,2304]{1,0:T(8,128)(2,1)S(1)} custom-call(s32[1]{0:T(128)} %bitcast.4.place_ref, bf16[512,256]{1,0:T(8,128)(2,1)S(1)} %get-tuple-element.60.dq0_ref, bf16[512,256]{1,0:T(8,128)(2,1)S(1)} %get-tuple-element.61.dq1_ref, bf16[512,256]{1,0:T(8,128)(2,1)S(1)} %fusion.2.g0_ref, bf16[512,256]{1,0:T(8,128)(2,1)S(1)} %fusion.5.g1_ref, ...), custom_call_target="tpu_custom_call" | custom-call | flops 603979776 | bytes 5308416 | tf_op jit(solution)/shard_map/back_project/pallas_call | solution.py:257
  63.4 1.3 collective-permute-start.16
  64.7 3.0 %collective-permute-done.8 = bf16[128,1536]{1,0:T(8,128)(2,1)S(1)} collective-permute-done((bf16[128,1536]{1,0:T(8,128)(2,1)S(1)}, bf16[128,1536]{1,0:T(8,128)(2,1)S(1)}, u32[]{:S(2)}, u32[]{:S(2)}) %collective-permute-start.8) | collective-permute-done | bytes 393248 | tf_op jit(solution)/shard_map/ppermute | solution.py:348
  67.6 0.1 add_convert_fusion.6
  67.7 3.5 %collective-permute-start.13 = (bf16[128,1536]{1,0:T(8,128)(2,1)S(1)}, bf16[128,1536]{1,0:T(8,128)(2,1)S(1)}, u32[]{:S(2)}, u32[]{:S(2)}) collective-permute-start(bf16[128,1536]{1,0:T(8,128)(2,1)S(1)} %add_convert_fusion.6), channel_id=1, source_target_pairs={{1,2},{2,1},{5,6},{6,5},{9,10},{10,9},{13,14},{14,13},{17,18},{18,... | collective-permute-start | bytes 1179656 | tf_op jit(solution)/shard_map/ppermute | solution.py:348
  71.2 10.2 %back_project.5 = (bf16[128,1536]{1,0:T(8,128)(2,1)S(1)}, bf16[128,1536]{1,0:T(8,128)(2,1)S(1)}, bf16[128,1536]{1,0:T(8,128)(2,1)S(1)}, bf16[128,1536]{1,0:T(8,1...) custom-call(s32[3]{0:T(128)S(1)} %pad_add_fusion.place_ref, ...), custom_call_target="tpu_custom_call" | custom-call | flops 4227858432 | bytes 15138816 | tf_op jit(solution)/shard_map/back_project/pallas_call | solution.py:257
  81.4 1.3 collective-permute-start.9
  82.7 0.1 add_convert_fusion.7
  82.8 2.4 %collective-permute-start.11 = (bf16[128,1536]{1,0:T(8,128)(2,1)S(1)}, bf16[128,1536]{1,0:T(8,128)(2,1)S(1)}, u32[]{:S(2)}, u32[]{:S(2)}) collective-permute-start(bf16[128,1536]{1,0:T(8,128)(2,1)S(1)} %add_convert_fusion.7), channel_id=1, source_target_pairs={{1,2},{2,1},{5,6},{6,5},{9,10},{10,9},{13,14},{14,13},{17,18},{18,... | collective-permute-start | bytes 1179656 | tf_op jit(solution)/shard_map/ppermute | solution.py:348
  85.2 1.3 collective-permute-start.15
  86.5 2.2 %collective-permute-done.16 = bf16[128,2304]{1,0:T(8,128)(2,1)S(1)} collective-permute-done((bf16[128,2304]{1,0:T(8,128)(2,1)S(1)}, bf16[128,2304]{1,0:T(8,128)(2,1)S(1)}, u32[]{:S(2)}, u32[]{:S(2)}) %collective-permute-start.16) | collective-permute-done | bytes 589856 | tf_op jit(solution)/shard_map/ppermute | solution.py:348
  88.7 1.3 collective-permute-start.20
  90.0 0.1 add_convert_fusion.2
  90.2 0.1 add_convert_fusion.5
  90.3 6.9 %collective-permute-done.9 = bf16[128,1536]{1,0:T(8,128)(2,1)S(1)} collective-permute-done((bf16[128,1536]{1,0:T(8,128)(2,1)S(1)}, bf16[128,1536]{1,0:T(8,128)(2,1)S(1)}, u32[]{:S(2)}, u32[]{:S(2)}) %collective-permute-start.9) | collective-permute-done | bytes 393248 | tf_op jit(solution)/shard_map/ppermute | solution.py:348
  97.1 0.1 add_convert_fusion.8
  97.2 3.5 %collective-permute-start.12 = (bf16[128,1536]{1,0:T(8,128)(2,1)S(1)}, bf16[128,1536]{1,0:T(8,128)(2,1)S(1)}, u32[]{:S(2)}, u32[]{:S(2)}) collective-permute-start(bf16[128,1536]{1,0:T(8,128)(2,1)S(1)} %add_convert_fusion.8), channel_id=1, source_target_pairs={{1,2},{2,1},{5,6},{6,5},{9,10},{10,9},{13,14},{14,13},{17,18},{18,... | collective-permute-start | bytes 1179656 | tf_op jit(solution)/shard_map/ppermute | solution.py:348
  100.7 2.4 %collective-permute-start.17 = (bf16[128,2304]{1,0:T(8,128)(2,1)S(1)}, bf16[128,2304]{1,0:T(8,128)(2,1)S(1)}, u32[]{:S(2)}, u32[]{:S(2)}) collective-permute-start(bf16[128,2304]{1,0:T(8,128)(2,1)S(1)} %add_convert_fusion.2), channel_id=1, source_target_pairs={{1,2},{2,1},{5,6},{6,5},{9,10},{10,9},{13,14},{14,13},{17,18},{18,... | collective-permute-start | bytes 1769480 | tf_op jit(solution)/shard_map/ppermute | solution.py:348
  103.1 0.1 add_convert_fusion.3
  103.2 2.4 %collective-permute-done.15 = bf16[128,1536]{1,0:T(8,128)(2,1)S(1)} collective-permute-done((bf16[128,1536]{1,0:T(8,128)(2,1)S(1)}, bf16[128,1536]{1,0:T(8,128)(2,1)S(1)}, u32[]{:S(2)}, u32[]{:S(2)}) %collective-permute-start.15) | collective-permute-done | bytes 393248 | tf_op jit(solution)/shard_map/ppermute | solution.py:348
  105.6 0.1 add_convert_fusion.4
  105.7 12.5 %collective-permute-done.20 = bf16[128,2304]{1,0:T(8,128)(2,1)S(1)} collective-permute-done((bf16[128,2304]{1,0:T(8,128)(2,1)S(1)}, bf16[128,2304]{1,0:T(8,128)(2,1)S(1)}, u32[]{:S(2)}, u32[]{:S(2)}) %collective-permute-start.20) | collective-permute-done | bytes 589856 | tf_op jit(solution)/shard_map/ppermute | solution.py:348
  118.2 0.1 add_convert_fusion.1
  118.4 3.5 %collective-permute-start.21 = (bf16[128,2304]{1,0:T(8,128)(2,1)S(1)}, bf16[128,2304]{1,0:T(8,128)(2,1)S(1)}, u32[]{:S(2)}, u32[]{:S(2)}) collective-permute-start(bf16[128,2304]{1,0:T(8,128)(2,1)S(1)} %add_convert_fusion.1), channel_id=1, source_target_pairs={{1,2},{2,1},{5,6},{6,5},{9,10},{10,9},{13,14},{14,13},{17,18},{18,... | collective-permute-start | bytes 1769480 | tf_op jit(solution)/shard_map/ppermute | solution.py:348
  121.9 2.4 %collective-permute-start.18 = (bf16[128,1536]{1,0:T(8,128)(2,1)S(1)}, bf16[128,1536]{1,0:T(8,128)(2,1)S(1)}, u32[]{:S(2)}, u32[]{:S(2)}) collective-permute-start(bf16[128,1536]{1,0:T(8,128)(2,1)S(1)} %add_convert_fusion.4), channel_id=1, source_target_pairs={{1,2},{2,1},{5,6},{6,5},{9,10},{10,9},{13,14},{14,13},{17,18},{18,... | collective-permute-start | bytes 1179656 | tf_op jit(solution)/shard_map/ppermute | solution.py:348
  124.2 0.1 add_convert_fusion
  124.4 0.1 collective-permute-start.22
  124.4 2.2 %collective-permute-done.14 = bf16[128,1536]{1,0:T(8,128)(2,1)S(1)} collective-permute-done((bf16[128,1536]{1,0:T(8,128)(2,1)S(1)}, bf16[128,1536]{1,0:T(8,128)(2,1)S(1)}, u32[]{:S(2)}, u32[]{:S(2)}) %collective-permute-start.14) | collective-permute-done | bytes 393248 | tf_op jit(solution)/shard_map/ppermute | solution.py:348
  126.6 0.1 convert_add_fusion.2
  126.8 8.3 %collective-permute-done.19 = bf16[128,1536]{1,0:T(8,128)(2,1)S(1)} collective-permute-done((bf16[128,1536]{1,0:T(8,128)(2,1)S(1)}, bf16[128,1536]{1,0:T(8,128)(2,1)S(1)}, u32[]{:S(2)}, u32[]{:S(2)}) %collective-permute-start.19) | collective-permute-done | bytes 393248 | tf_op jit(solution)/shard_map/ppermute | solution.py:348
  135.1 5.5 %collective-permute-done.18 = bf16[128,1536]{1,0:T(8,128)(2,1)S(1)} collective-permute-done((bf16[128,1536]{1,0:T(8,128)(2,1)S(1)}, bf16[128,1536]{1,0:T(8,128)(2,1)S(1)}, u32[]{:S(2)}, u32[]{:S(2)}) %collective-permute-start.18) | collective-permute-done | bytes 393248 | tf_op jit(solution)/shard_map/ppermute | solution.py:348
  140.6 0.1 convert_add_fusion.1
  140.7 5.3 %collective-permute-done.22 = bf16[128,2304]{1,0:T(8,128)(2,1)S(1)} collective-permute-done((bf16[128,2304]{1,0:T(8,128)(2,1)S(1)}, bf16[128,2304]{1,0:T(8,128)(2,1)S(1)}, u32[]{:S(2)}, u32[]{:S(2)}) %collective-permute-start.22) | collective-permute-done | bytes 589856 | tf_op jit(solution)/shard_map/ppermute | solution.py:348
  146.0 0.2 convert_add_fusion
  146.2 1.7 %pad_maximum_fusion = f32[128,5376]{1,0:T(8,128)} fusion(f32[128,2304]{1,0:T(8,128)S(1)} %convert_add_fusion, f32[128,1536]{1,0:T(8,128)S(1)} %convert_add_fusion.1, f32[128,1536]{1,0:T(8,128)S(1)} %convert_add_fusion.2), kind=kLoop, calls=%fused_computation | loop fusion | flops 1376256 | bytes 5505024 | tf_op jit(solution)/shard_map/concatenate | solution.py:366
  (20 shorter events, 0.1 us)
Async XLA Ops:
  5.6 10.8 %collective-permute-start = (bf16[512,256]{1,0:T(8,128)(2,1)S(1)}, bf16[512,256]{1,0:T(8,128)(2,1)S(1)}, u32[]{:S(2)}, u32[]{:S(2)}) collective-permute-start(bf16[512,256]{1,0:T(8,128)(2,1)S(1)} %get-tuple-element.44.own_ref), channel_id=1, source_target_pairs={{0,8},{4,12},{8,16},{12,20},{16,24},{20,28},{1,9},{5,13},{9,17},{1... | collective-permute-start | bytes 786440 | tf_op jit(solution)/shard_map/ppermute | solution.py:306
  9.1 10.0 %copy-start.3 = (s32[512]{0:T(512)S(1)}, s32[512]{0:T(512)}, u32[]{:S(2)}) copy-start(s32[512]{0:T(512)} %param.11) | copy-start | bytes 6148
  9.1 10.2 %copy-start = (bf16[512,512]{1,0:T(8,128)(2,1)S(1)}, bf16[512,512]{1,0:T(8,128)(2,1)}, u32[]{:S(2)}) copy-start(bf16[512,512]{1,0:T(8,128)(2,1)} %do_ref.3) | copy-start | bytes 1572868
  16.5 2.8 %collective-permute-start.1 = (bf16[512,256]{1,0:T(8,128)(2,1)S(1)}, bf16[512,256]{1,0:T(8,128)(2,1)S(1)}, u32[]{:S(2)}, u32[]{:S(2)}) collective-permute-start(bf16[512,256]{1,0:T(8,128)(2,1)S(1)} %broadcast_select_fusion.1), channel_id=1, source_target_pairs={{0,4},{4,0},{8,12},{12,8},{16,20},{20,16},{24,28},{28,24},{1,5},{5... | collective-permute-start | bytes 786440 | tf_op jit(solution)/shard_map/ppermute | solution.py:318
  16.6 11.5 %collective-permute-start.3 = (bf16[512,256]{1,0:T(8,128)(2,1)S(1)}, bf16[512,256]{1,0:T(8,128)(2,1)S(1)}, u32[]{:S(2)}, u32[]{:S(2)}) collective-permute-start(bf16[512,256]{1,0:T(8,128)(2,1)S(1)} %get-tuple-element.51.own_ref), channel_id=1, source_target_pairs={{0,8},{4,12},{8,16},{12,20},{16,24},{20,28},{1,9},{5,13},{9,17},{1... | collective-permute-start | bytes 786440 | tf_op jit(solution)/shard_map/ppermute | solution.py:306
  24.5 3.7 %collective-permute-start.2 = (bf16[512,256]{1,0:T(8,128)(2,1)S(1)}, bf16[512,256]{1,0:T(8,128)(2,1)S(1)}, u32[]{:S(2)}, u32[]{:S(2)}) collective-permute-start(bf16[512,256]{1,0:T(8,128)(2,1)S(1)} %get-tuple-element.49), channel_id=1, source_target_pairs={{0,4},{4,0},{8,12},{12,8},{16,20},{20,16},{24,28},{28,24},{1,5},{5... | collective-permute-start | bytes 786440 | tf_op jit(solution)/shard_map/ppermute | solution.py:323
  28.1 2.5 %collective-permute-start.4 = (bf16[512,256]{1,0:T(8,128)(2,1)S(1)}, bf16[512,256]{1,0:T(8,128)(2,1)S(1)}, u32[]{:S(2)}, u32[]{:S(2)}) collective-permute-start(bf16[512,256]{1,0:T(8,128)(2,1)S(1)} %broadcast_select_fusion), channel_id=1, source_target_pairs={{0,4},{4,0},{8,12},{12,8},{16,20},{20,16},{24,28},{28,24},{1,5},{5... | collective-permute-start | bytes 786440 | tf_op jit(solution)/shard_map/ppermute | solution.py:318
  28.2 2.4 %copy-start.1 = (bf16[512,256]{1,0:T(8,128)(2,1)}, bf16[512,256]{1,0:T(8,128)(2,1)S(1)}, u32[]{:S(2)}) copy-start(bf16[512,256]{1,0:T(8,128)(2,1)S(1)} %collective-permute-done.2) | copy-start | bytes 786436
  28.3 10.6 %collective-permute-start.5 = (bf16[512,256]{1,0:T(8,128)(2,1)S(1)}, bf16[512,256]{1,0:T(8,128)(2,1)S(1)}, u32[]{:S(2)}, u32[]{:S(2)}) collective-permute-start(bf16[512,256]{1,0:T(8,128)(2,1)S(1)} %fusion.7), channel_id=1, source_target_pairs={{8,0},{12,4},{16,8},{20,12},{24,16},{28,20},{9,1},{13,5},{17,9},{2... | collective-permute-start | bytes 786440 | tf_op jit(solution)/shard_map/ppermute | solution.py:327
  38.9 1.6 %copy-start.2 = (bf16[512,256]{1,0:T(8,128)(2,1)}, bf16[512,256]{1,0:T(8,128)(2,1)S(1)}, u32[]{:S(2)}) copy-start(bf16[512,256]{1,0:T(8,128)(2,1)S(1)} %collective-permute-done.5) | copy-start | bytes 786436
  38.9 1.5 %collective-permute-start.6 = (bf16[512,256]{1,0:T(8,128)(2,1)S(1)}, bf16[512,256]{1,0:T(8,128)(2,1)S(1)}, u32[]{:S(2)}, u32[]{:S(2)}) collective-permute-start(bf16[512,256]{1,0:T(8,128)(2,1)S(1)} %get-tuple-element.59), channel_id=1, source_target_pairs={{0,4},{4,0},{8,12},{12,8},{16,20},{20,16},{24,28},{28,24},{1,5},{5... | collective-permute-start | bytes 786440 | tf_op jit(solution)/shard_map/ppermute | solution.py:323
  40.5 10.2 %collective-permute-start.7 = (bf16[512,256]{1,0:T(8,128)(2,1)S(1)}, bf16[512,256]{1,0:T(8,128)(2,1)S(1)}, u32[]{:S(2)}, u32[]{:S(2)}) collective-permute-start(bf16[512,256]{1,0:T(8,128)(2,1)S(1)} %fusion.6), channel_id=1, source_target_pairs={{8,0},{12,4},{16,8},{20,12},{24,16},{28,20},{9,1},{13,5},{17,9},{2... | collective-permute-start | bytes 786440 | tf_op jit(solution)/shard_map/ppermute | solution.py:327
  53.7 13.9 %collective-permute-start.8 = (bf16[128,1536]{1,0:T(8,128)(2,1)S(1)}, bf16[128,1536]{1,0:T(8,128)(2,1)S(1)}, u32[]{:S(2)}, u32[]{:S(2)}) collective-permute-start(bf16[128,1536]{1,0:T(8,128)(2,1)S(1)} %back_project.4), channel_id=1, source_target_pairs={{0,1},{3,2},{4,5},{7,6},{8,9},{11,10},{12,13},{15,14},{16,17},{19,... | collective-permute-start | bytes 1179656 | tf_op jit(solution)/shard_map/ppermute | solution.py:348
  57.9 24.8 %collective-permute-start.10 = (bf16[128,1536]{1,0:T(8,128)(2,1)S(1)}, bf16[128,1536]{1,0:T(8,128)(2,1)S(1)}, u32[]{:S(2)}, u32[]{:S(2)}) collective-permute-start(bf16[128,1536]{1,0:T(8,128)(2,1)S(1)} %back_project.6), channel_id=1, source_target_pairs={{0,1},{3,2},{4,5},{7,6},{8,9},{11,10},{12,13},{15,14},{16,17},{19,... | collective-permute-start | bytes 1179656 | tf_op jit(solution)/shard_map/ppermute | solution.py:348
  63.4 25.3 %collective-permute-start.16 = (bf16[128,2304]{1,0:T(8,128)(2,1)S(1)}, bf16[128,2304]{1,0:T(8,128)(2,1)S(1)}, u32[]{:S(2)}, u32[]{:S(2)}) collective-permute-start(bf16[128,2304]{1,0:T(8,128)(2,1)S(1)} %back_project.7), channel_id=1, source_target_pairs={{0,1},{3,2},{4,5},{7,6},{8,9},{11,10},{12,13},{15,14},{16,17},{19,... | collective-permute-start | bytes 1769480 | tf_op jit(solution)/shard_map/ppermute | solution.py:348
  67.7 22.4 %collective-permute-start.13 = (bf16[128,1536]{1,0:T(8,128)(2,1)S(1)}, bf16[128,1536]{1,0:T(8,128)(2,1)S(1)}, u32[]{:S(2)}, u32[]{:S(2)}) collective-permute-start(bf16[128,1536]{1,0:T(8,128)(2,1)S(1)} %add_convert_fusion.6), channel_id=1, source_target_pairs={{1,2},{2,1},{5,6},{6,5},{9,10},{10,9},{13,14},{14,13},{17,18},{18,... | collective-permute-start | bytes 1179656 | tf_op jit(solution)/shard_map/ppermute | solution.py:348
  81.4 15.7 %collective-permute-start.9 = (bf16[128,1536]{1,0:T(8,128)(2,1)S(1)}, bf16[128,1536]{1,0:T(8,128)(2,1)S(1)}, u32[]{:S(2)}, u32[]{:S(2)}) collective-permute-start(bf16[128,1536]{1,0:T(8,128)(2,1)S(1)} %get-tuple-element.66), channel_id=1, source_target_pairs={{0,1},{3,2},{4,5},{7,6},{8,9},{11,10},{12,13},{15,14},{16,17},{19,... | collective-permute-start | bytes 1179656 | tf_op jit(solution)/shard_map/ppermute | solution.py:348
  82.8 14.4 %collective-permute-start.11 = (bf16[128,1536]{1,0:T(8,128)(2,1)S(1)}, bf16[128,1536]{1,0:T(8,128)(2,1)S(1)}, u32[]{:S(2)}, u32[]{:S(2)}) collective-permute-start(bf16[128,1536]{1,0:T(8,128)(2,1)S(1)} %add_convert_fusion.7), channel_id=1, source_target_pairs={{1,2},{2,1},{5,6},{6,5},{9,10},{10,9},{13,14},{14,13},{17,18},{18,... | collective-permute-start | bytes 1179656 | tf_op jit(solution)/shard_map/ppermute | solution.py:348
  85.2 20.4 %collective-permute-start.15 = (bf16[128,1536]{1,0:T(8,128)(2,1)S(1)}, bf16[128,1536]{1,0:T(8,128)(2,1)S(1)}, u32[]{:S(2)}, u32[]{:S(2)}) collective-permute-start(bf16[128,1536]{1,0:T(8,128)(2,1)S(1)} %get-tuple-element.72), channel_id=1, source_target_pairs={{0,1},{3,2},{4,5},{7,6},{8,9},{11,10},{12,13},{15,14},{16,17},{19,... | collective-permute-start | bytes 1179656 | tf_op jit(solution)/shard_map/ppermute | solution.py:348
  88.7 29.5 %collective-permute-start.20 = (bf16[128,2304]{1,0:T(8,128)(2,1)S(1)}, bf16[128,2304]{1,0:T(8,128)(2,1)S(1)}, u32[]{:S(2)}, u32[]{:S(2)}) collective-permute-start(bf16[128,2304]{1,0:T(8,128)(2,1)S(1)} %get-tuple-element.79), channel_id=1, source_target_pairs={{0,1},{3,2},{4,5},{7,6},{8,9},{11,10},{12,13},{15,14},{16,17},{19,... | collective-permute-start | bytes 1769480 | tf_op jit(solution)/shard_map/ppermute | solution.py:348
  97.1 29.5 %collective-permute-start.14 = (bf16[128,1536]{1,0:T(8,128)(2,1)S(1)}, bf16[128,1536]{1,0:T(8,128)(2,1)S(1)}, u32[]{:S(2)}, u32[]{:S(2)}) collective-permute-start(bf16[128,1536]{1,0:T(8,128)(2,1)S(1)} %add_convert_fusion.5), channel_id=1, source_target_pairs={{0,1},{3,2},{1,0},{2,3},{4,5},{7,6},{5,4},{6,7},{8,9},{11,10},{9,8... | collective-permute-start | bytes 1179656 | tf_op jit(solution)/shard_map/ppermute | solution.py:348
  97.2 21.1 %collective-permute-start.12 = (bf16[128,1536]{1,0:T(8,128)(2,1)S(1)}, bf16[128,1536]{1,0:T(8,128)(2,1)S(1)}, u32[]{:S(2)}, u32[]{:S(2)}) collective-permute-start(bf16[128,1536]{1,0:T(8,128)(2,1)S(1)} %add_convert_fusion.8), channel_id=1, source_target_pairs={{1,2},{2,1},{5,6},{6,5},{9,10},{10,9},{13,14},{14,13},{17,18},{18,... | collective-permute-start | bytes 1179656 | tf_op jit(solution)/shard_map/ppermute | solution.py:348
  100.7 21.1 %collective-permute-start.17 = (bf16[128,2304]{1,0:T(8,128)(2,1)S(1)}, bf16[128,2304]{1,0:T(8,128)(2,1)S(1)}, u32[]{:S(2)}, u32[]{:S(2)}) collective-permute-start(bf16[128,2304]{1,0:T(8,128)(2,1)S(1)} %add_convert_fusion.2), channel_id=1, source_target_pairs={{1,2},{2,1},{5,6},{6,5},{9,10},{10,9},{13,14},{14,13},{17,18},{18,... | collective-permute-start | bytes 1769480 | tf_op jit(solution)/shard_map/ppermute | solution.py:348
  105.6 29.5 %collective-permute-start.19 = (bf16[128,1536]{1,0:T(8,128)(2,1)S(1)}, bf16[128,1536]{1,0:T(8,128)(2,1)S(1)}, u32[]{:S(2)}, u32[]{:S(2)}) collective-permute-start(bf16[128,1536]{1,0:T(8,128)(2,1)S(1)} %add_convert_fusion.3), channel_id=1, source_target_pairs={{0,1},{3,2},{1,0},{2,3},{4,5},{7,6},{5,4},{6,7},{8,9},{11,10},{9,8... | collective-permute-start | bytes 1179656 | tf_op jit(solution)/shard_map/ppermute | solution.py:348
  118.4 22.3 %collective-permute-start.21 = (bf16[128,2304]{1,0:T(8,128)(2,1)S(1)}, bf16[128,2304]{1,0:T(8,128)(2,1)S(1)}, u32[]{:S(2)}, u32[]{:S(2)}) collective-permute-start(bf16[128,2304]{1,0:T(8,128)(2,1)S(1)} %add_convert_fusion.1), channel_id=1, source_target_pairs={{1,2},{2,1},{5,6},{6,5},{9,10},{10,9},{13,14},{14,13},{17,18},{18,... | collective-permute-start | bytes 1769480 | tf_op jit(solution)/shard_map/ppermute | solution.py:348
  121.9 18.7 %collective-permute-start.18 = (bf16[128,1536]{1,0:T(8,128)(2,1)S(1)}, bf16[128,1536]{1,0:T(8,128)(2,1)S(1)}, u32[]{:S(2)}, u32[]{:S(2)}) collective-permute-start(bf16[128,1536]{1,0:T(8,128)(2,1)S(1)} %add_convert_fusion.4), channel_id=1, source_target_pairs={{1,2},{2,1},{5,6},{6,5},{9,10},{10,9},{13,14},{14,13},{17,18},{18,... | collective-permute-start | bytes 1179656 | tf_op jit(solution)/shard_map/ppermute | solution.py:348
  124.4 21.6 %collective-permute-start.22 = (bf16[128,2304]{1,0:T(8,128)(2,1)S(1)}, bf16[128,2304]{1,0:T(8,128)(2,1)S(1)}, u32[]{:S(2)}, u32[]{:S(2)}) collective-permute-start(bf16[128,2304]{1,0:T(8,128)(2,1)S(1)} %add_convert_fusion), channel_id=1, source_target_pairs={{0,1},{3,2},{1,0},{2,3},{4,5},{7,6},{5,4},{6,7},{8,9},{11,10},{9,8... | collective-permute-start | bytes 1769480 | tf_op jit(solution)/shard_map/ppermute | solution.py:348

commit v5 on v4

--- a/solution.py
+++ b/solution.py
@@ -222,8 +222,9 @@
             here = slice(n * size, (n + 1) * size)
             buf[here, :pair] = dq0_ref[span, :]
             buf[here, pair : 2 * pair] = dq1_ref[span, :]
-            for at, ref in enumerate((g0_ref, g1_ref)):
-                rows = ref[span, :]
+            late = pl.ds(pl.multiple_of(place_ref[count + n] * size, size), size)
+            for at, (ref, here_rows) in enumerate(((g0_ref, span), (g1_ref, late))):
+                rows = ref[here_rows, :]
                 buf[here, 2 * pair + at * size : 2 * pair + (at + 1) * size] = rows[:, :size]
                 buf[here, 3 * pair + at * size : 3 * pair + (at + 1) * size] = rows[:, size:]
 
@@ -324,21 +325,35 @@
         passed = jnp.where(odd, add(gfar, swapped), gfar)
         if h + 1 < heads:
             passed, queries = lax.optimization_barrier((passed, queries))
-        returned = lax.ppermute(passed, "ctx", behind)
         d_queries.append(dq)
         waiting.append((gown, swapped))
-    finish()
+        if h + 1 < heads:
+            returned = lax.ppermute(passed, "ctx", behind)
 
     low_side = plane < 2
+    gown, swapped = waiting.pop()
+    local = gown + jnp.where(odd, 0.0, swapped.astype(jnp.float32))
+
+    def come_back(first, count, *after):
+        part = lax.dynamic_slice_in_dim(passed, first, count, 0)
+        if after:
+            part, *_ = lax.optimization_barrier((part, *after))
+        part = lax.ppermute(part, "ctx", behind).astype(jnp.float32)
+        part = lax.dynamic_slice_in_dim(local, first, count, 0) + part
+        return part.astype(jnp.bfloat16)
+
+    early = come_back(jnp.where(low_side, rows - chunk, 0), chunk)
 
     side = jnp.where(low_side, 3, 0)
     step = jnp.where(low_side, -1, 1)
     order = [(side + step * n).astype(jnp.int32) for n in range(planes)]
     last = jnp.where(outer, order[2], order[3])
     home = jnp.where(outer, order[3], order[2])
-    grads = (*d_queries, *gradients)
+    grads = (*d_queries, *gradients, early)
+    zero = jnp.zeros((), jnp.int32)
     edge = [
-        back_project(order[0].reshape(1), 1, grads, weights, [piece])[0][0] for piece in PIECES
+        back_project(jnp.stack([order[0], zero]), 1, grads, weights, [piece])[0][0]
+        for piece in PIECES
     ]
     sent_outer, sent_middle = [], []
 
@@ -355,9 +370,13 @@
         return send(payload, middle, sent_middle, MIDDLE_DEPTH)
 
     r0 = [send_outer(block, inward) for block in edge]
-    *grads, _ = lax.optimization_barrier((*grads, r0[0]))
-    others = jnp.stack([order[1], last, home])
-    blocks = back_project(others, 3, grads, weights, PIECES)
+    late_rows = come_back(jnp.where(low_side, 0, chunk), rows - chunk, r0[0])
+    *grads, _ = lax.optimization_barrier((*grads[:-1], late_rows, r0[0]))
+    others = [order[1], last, home]
+    late = jnp.where(low_side, 0, 1).astype(jnp.int32)
+    others = jnp.stack(others + [at - late for at in others])
+    blocks = back_project(others, 3, grads, weights, PIECES[:1])
+    blocks += back_project(others, 3, grads, weights, PIECES[1:])
     m1 = [send_middle(add(block, r)) for block, r in zip(edge, r0)]
     r1 = [send_outer(block[0], inward) for block in blocks]
     m2 = [send_middle(add(block[0], r)) for block, r in zip(blocks, r1)]

time: 149 us -> 147 us (0.987)
  waiting for transfers between devices: 63.9 us -> 50.2 us
  starting transfers between devices: 37.1 us -> 42.3 us
  Pallas kernels: 41.6 us -> 45.4 us
    ppermute x15, waiting for transfers between devices: 48.2 us -> 40 us  [send(): sent.append(lax.ppermute(payload, 'head', pairs))]
    ppermute x2 -> x1, waiting for transfers between devices: 9.02 us -> 1.65 us  [shards(): returned = lax.ppermute(passed, 'ctx', behind)]
    ppermute x0 -> x2, starting transfers between devices: none -> 7.07 us  [come_back(): part = lax.ppermute(part, 'ctx', behind).astype(jnp.float32)]
    pallas_call x4 -> x5, Pallas kernels: 20 us -> 23.1 us  [back_project(): pl.pallas_call(functools.partial(back_kernel, spans), grid_spec=grid_spec...]
    ppermute x2 -> x1, starting transfers between devices: 5.41 us -> 2.31 us  [shards(): returned = lax.ppermute(passed, 'ctx', behind)]
    ppermute x0 -> x2, waiting for transfers between devices: none -> 2.99 us  [come_back(): part = lax.ppermute(part, 'ctx', behind).astype(jnp.float32)]
  transfers between devices with their start and end apart: 23 -> 24, of which waited for: 14 -> 13; matrix products, arithmetic and copies ran while one was open for 2% -> 3% of each run, Pallas kernels for 22% -> 25%
where the time goes in v5:
time: 147 us; the launch traced here: 145 us
  waiting for transfers between devices  50.2 us (34%)
  Pallas kernels  45.4 us (31%)
  starting transfers between devices  42.3 us (29%)
  other arithmetic  5.43 us (4%)
    ppermute x15, waiting for transfers between devices, send(): sent.append(lax.ppermute(payload, 'head', pairs))  40 us
    ppermute x15, starting transfers between devices, send(): sent.append(lax.ppermute(payload, 'head', pairs))  26.6 us
    pallas_call x5, Pallas kernels, back_project(): pl.pallas_call(functools.partial(back_kernel, spans), grid_spec=grid_spec...  23.1 us
    pallas_call x2, Pallas kernels, attend(): pl.pallas_call(attention_kernel, grid=(1,), in_specs=[column, column, who...  11.1 us
    ppermute x2, starting transfers between devices, come_back(): part = lax.ppermute(part, 'ctx', behind).astype(jnp.float32)  7.07 us
    ppermute x2, starting transfers between devices, shards(): far = [lax.ppermute(x, 'ctx', ahead) for x in own]  5.9 us
    pallas_call x1, Pallas kernels, project_keys_values(): pl.pallas_call(project_kernel, in_specs=[hbm] * 3, out_specs=[vmem] * hea...  5.63 us
    pallas_call x1, Pallas kernels, project_queries(): pl.pallas_call(query_kernel, in_specs=[hbm] * 2, out_specs=pl.BlockSpec(m...  5.6 us
  transfers between devices with their start and end apart: 24, of which 13 were waited for; matrix products, arithmetic and copies ran while one was open for 3% of the time, Pallas kernels for 25%

profile of v5, /device:TPU:12, one launch (start us, length us, event | category | flops | bytes accessed | tf_op | source)
XLA Modules:
  0.0 145.2 jit_solution(5301502961043920230)
XLA Ops:
  0.0 5.6 %project_kv.1 = (bf16[512,256]{1,0:T(8,128)(2,1)S(1)}, bf16[512,256]{1,0:T(8,128)(2,1)S(1)}) custom-call(bf16[512,5376]{1,0:T(8,128)(2,1)} %hidden_ref.3, bf16[5376,256]{1,0:T(8,128)(2,1)} %wk_ref.11, bf16[5376,256]{1,0:T(8,128)(2,1)} %wv_ref.11), custom_call_target="tpu_custom_call" | custom-call | flops 2818572288 | bytes 11010048 | tf_op jit(solution)/shard_map/project_kv/pallas_call | solution.py:77
  5.6 3.4 %collective-permute-start = (bf16[512,256]{1,0:T(8,128)(2,1)S(1)}, bf16[512,256]{1,0:T(8,128)(2,1)S(1)}, u32[]{:S(2)}, u32[]{:S(2)}) collective-permute-start(bf16[512,256]{1,0:T(8,128)(2,1)S(1)} %get-tuple-element.45.own_ref), channel_id=1, source_target_pairs={{0,8},{4,12},{8,16},{12,20},{16,24},{20,28},{1,9},{5,13},{9,17},{1... | collective-permute-start | bytes 786440 | tf_op jit(solution)/shard_map/ppermute | solution.py:307
  9.1 5.6 %project_q.1.q_ref = bf16[512,512]{1,0:T(8,128)(2,1)S(1)} custom-call(bf16[512,5376]{1,0:T(8,128)(2,1)} %hidden_ref.3, bf16[5376,512]{1,0:T(8,128)(2,1)} %wq_ref.11), custom_call_target="tpu_custom_call" | custom-call | flops 2818572288 | bytes 11010048 | tf_op jit(solution)/shard_map/project_q/pallas_call | solution.py:108
  14.7 1.8 %collective-permute-done.far_ref = bf16[512,256]{1,0:T(8,128)(2,1)S(1)} collective-permute-done((bf16[512,256]{1,0:T(8,128)(2,1)S(1)}, bf16[512,256]{1,0:T(8,128)(2,1)S(1)}, u32[]{:S(2)}, u32[]{:S(2)}) %collective-permute-start) | collective-permute-done | bytes 262176 | tf_op jit(solution)/shard_map/ppermute | solution.py:307
  16.5 0.1 collective-permute-start.1
  16.6 2.5 %collective-permute-start.3 = (bf16[512,256]{1,0:T(8,128)(2,1)S(1)}, bf16[512,256]{1,0:T(8,128)(2,1)S(1)}, u32[]{:S(2)}, u32[]{:S(2)}) collective-permute-start(bf16[512,256]{1,0:T(8,128)(2,1)S(1)} %get-tuple-element.52.own_ref), channel_id=1, source_target_pairs={{0,8},{4,12},{8,16},{12,20},{16,24},{20,28},{1,9},{5,13},{9,17},{1... | collective-permute-start | bytes 786440 | tf_op jit(solution)/shard_map/ppermute | solution.py:307
  19.1 0.1 copy.7.low_ref
  19.3 5.2 %attention.2 = (bf16[512,256]{1,0:T(8,128)(2,1)S(1)}, bf16[512,256]{1,0:T(8,128)(2,1)S(1)}, bf16[512,256]{1,0:T(8,128)(2,1)S(1)}, f32[512,256]{1,0:T(8,128)S(1)}) custom-call(bf16[512,512]{1,0:T(8,128)(2,1)S(1)} %project_q.1.q_ref, bf16[512,512]{1,0:T(8,128)(2,1)S(1)} %copy-done, bf16[512,256]{1,0:T(8,128)(2,1)S(1)} %collective-permute-done.far_ref, ...), custom_call_target="tpu_custom_call" | custom-call | flops 2415919104 | bytes 2097152 | tf_op jit(solution)/shard_map/attention/pallas_call | solution.py:182
  24.5 0.3 collective-permute-start.2
  24.8 3.3 %collective-permute-done.3.far_ref = bf16[512,256]{1,0:T(8,128)(2,1)S(1)} collective-permute-done((bf16[512,256]{1,0:T(8,128)(2,1)S(1)}, bf16[512,256]{1,0:T(8,128)(2,1)S(1)}, u32[]{:S(2)}, u32[]{:S(2)}) %collective-permute-start.3) | collective-permute-done | bytes 262176 | tf_op jit(solution)/shard_map/ppermute | solution.py:307
  28.1 0.1 collective-permute-start.4
  28.2 0.8 fusion.6
  29.0 2.3 %collective-permute-start.5 = (bf16[512,256]{1,0:T(8,128)(2,1)}, bf16[512,256]{1,0:T(8,128)(2,1)}, u32[]{:S(2)}, u32[]{:S(2)}) collective-permute-start(bf16[512,256]{1,0:T(8,128)(2,1)} %fusion.6), channel_id=1, source_target_pairs={{8,0},{12,4},{16,8},{20,12},{24,16},{28,20},{9,1},{13,5},{17,9},{2... | collective-permute-start | bytes 786440 | tf_op jit(solution)/shard_map/ppermute | solution.py:331
  31.4 1.0 copy-done.1
  32.4 5.8 %attention.3 = (bf16[512,256]{1,0:T(8,128)(2,1)S(1)}, bf16[512,256]{1,0:T(8,128)(2,1)S(1)}, bf16[512,256]{1,0:T(8,128)(2,1)}, f32[512,256]{1,0:T(8,128)S(1)}) custom-call(bf16[512,512]{1,0:T(8,128)(2,1)S(1)} %project_q.1.q_ref, bf16[512,512]{1,0:T(8,128)(2,1)S(1)} %copy-done.1, bf16[512,256]{1,0:T(8,128)(2,1)S(1)} %collective-permute-done.3.far_ref, ...), custom_call_target="tpu_custom_call" | custom-call | flops 2415919104 | bytes 2097152 | tf_op jit(solution)/shard_map/attention/pallas_call | solution.py:182
  38.3 1.7 %collective-permute-done.5 = bf16[512,256]{1,0:T(8,128)(2,1)} collective-permute-done((bf16[512,256]{1,0:T(8,128)(2,1)}, bf16[512,256]{1,0:T(8,128)(2,1)}, u32[]{:S(2)}, u32[]{:S(2)}) %collective-permute-start.5) | collective-permute-done | bytes 262176 | tf_op jit(solution)/shard_map/ppermute | solution.py:331
  39.9 0.1 pad_add_fusion.place_ref
  40.0 1.1 fusion.2.g0_ref
  41.1 0.5 collective-permute-done.6
  41.7 0.1 fusion.5
  41.8 3.1 %collective-permute-start.7 = (bf16[128,256]{1,0:T(8,128)(2,1)S(1)}, bf16[128,256]{1,0:T(8,128)(2,1)S(1)}, u32[]{:S(2)}, u32[]{:S(2)}) collective-permute-start(bf16[128,256]{1,0:T(8,128)(2,1)S(1)} %constant_dynamic-slice_fusion), channel_id=1, source_target_pairs={{8,0},{12,4},{16,8},{20,12},{24,16},{28,20},{9,1},{13,5},{17,9},{2... | collective-permute-start | bytes 196616 | tf_op jit(solution)/shard_map/ppermute | solution.py:341
  44.9 3.0 %collective-permute-done.7 = bf16[128,256]{1,0:T(8,128)(2,1)S(1)} collective-permute-done((bf16[128,256]{1,0:T(8,128)(2,1)S(1)}, bf16[128,256]{1,0:T(8,128)(2,1)S(1)}, u32[]{:S(2)}, u32[]{:S(2)}) %collective-permute-start.7) | collective-permute-done | bytes 65568 | tf_op jit(solution)/shard_map/ppermute | solution.py:341
  48.0 3.4 %back_project.5 = bf16[128,1536]{1,0:T(8,128)(2,1)S(1)} custom-call(s32[2]{0:T(128)S(1)} %pad_add_fusion.place_ref, bf16[512,256]{1,0:T(8,128)(2,1)S(1)} %get-tuple-element.62.dq0_ref, bf16[512,256]{1,0:T(8,128)(2,1)S(1)} %get-tuple-element.63.dq1_ref, bf16[512,256]{1,0:T(8,128)(2,1)S(1)} %fusion.2.g0_ref, bf16[128,256]{1,0:T(8,128)(2,1)S(1)} %add_convert_fusion.10.g1_ref, ...), custom_call_target="tpu_custom_call" | custom-call | flops 402653184 | bytes 3538944 | tf_op jit(solution)/shard_map/back_project/pallas_call | solution.py:258
  51.3 1.3 collective-permute-start.8
  52.7 0.1 stack.37.place_ref
  52.8 3.4 %back_project.7 = bf16[128,1536]{1,0:T(8,128)(2,1)S(1)} custom-call(s32[2]{0:T(128)S(1)} %pad_add_fusion.place_ref, bf16[512,256]{1,0:T(8,128)(2,1)S(1)} %get-tuple-element.62.dq0_ref, bf16[512,256]{1,0:T(8,128)(2,1)S(1)} %get-tuple-element.63.dq1_ref, bf16[512,256]{1,0:T(8,128)(2,1)S(1)} %fusion.2.g0_ref, bf16[128,256]{1,0:T(8,128)(2,1)S(1)} %add_convert_fusion.10.g1_ref, ...), custom_call_target="tpu_custom_call" | custom-call | flops 402653184 | bytes 3538944 | tf_op jit(solution)/shard_map/back_project/pallas_call | solution.py:258
  56.1 1.3 collective-permute-start.11
  57.4 4.7 %back_project.9 = bf16[128,2304]{1,0:T(8,128)(2,1)S(1)} custom-call(s32[2]{0:T(128)S(1)} %pad_add_fusion.place_ref, bf16[512,256]{1,0:T(8,128)(2,1)S(1)} %get-tuple-element.62.dq0_ref, bf16[512,256]{1,0:T(8,128)(2,1)S(1)} %get-tuple-element.63.dq1_ref, bf16[512,256]{1,0:T(8,128)(2,1)S(1)} %fusion.2.g0_ref, bf16[128,256]{1,0:T(8,128)(2,1)S(1)} %add_convert_fusion.10.g1_ref, ...), custom_call_target="tpu_custom_call" | custom-call | flops 603979776 | bytes 5308416 | tf_op jit(solution)/shard_map/back_project/pallas_call | solution.py:258
  62.2 1.3 collective-permute-start.17
  63.5 1.8 %collective-permute-done.8 = bf16[128,1536]{1,0:T(8,128)(2,1)S(1)} collective-permute-done((bf16[128,1536]{1,0:T(8,128)(2,1)S(1)}, bf16[128,1536]{1,0:T(8,128)(2,1)S(1)}, u32[]{:S(2)}, u32[]{:S(2)}) %collective-permute-start.8) | collective-permute-done | bytes 393248 | tf_op jit(solution)/shard_map/ppermute | solution.py:363
  65.3 4.0 %collective-permute-start.9 = (bf16[384,256]{1,0:T(8,128)(2,1)S(1)}, bf16[384,256]{1,0:T(8,128)(2,1)S(1)}, u32[]{:S(2)}, u32[]{:S(2)}) collective-permute-start(bf16[384,256]{1,0:T(8,128)(2,1)S(1)} %constant_dynamic-slice_fusion.1), channel_id=1, source_target_pairs={{8,0},{12,4},{16,8},{20,12},{24,16},{28,20},{9,1},{13,5},{17,9},{2... | collective-permute-start | bytes 589832 | tf_op jit(solution)/shard_map/ppermute | solution.py:341
  69.3 0.1 add_convert_fusion.6
  69.4 3.5 %collective-permute-start.14 = (bf16[128,1536]{1,0:T(8,128)(2,1)S(1)}, bf16[128,1536]{1,0:T(8,128)(2,1)S(1)}, u32[]{:S(2)}, u32[]{:S(2)}) collective-permute-start(bf16[128,1536]{1,0:T(8,128)(2,1)S(1)} %add_convert_fusion.6), channel_id=1, source_target_pairs={{1,2},{2,1},{5,6},{6,5},{9,10},{10,9},{13,14},{14,13},{17,18},{18,... | collective-permute-start | bytes 1179656 | tf_op jit(solution)/shard_map/ppermute | solution.py:363
  72.9 0.8 collective-permute-done.11
  73.7 0.1 add_convert_fusion.7
  73.8 3.5 %collective-permute-start.12 = (bf16[128,1536]{1,0:T(8,128)(2,1)S(1)}, bf16[128,1536]{1,0:T(8,128)(2,1)S(1)}, u32[]{:S(2)}, u32[]{:S(2)}) collective-permute-start(bf16[128,1536]{1,0:T(8,128)(2,1)S(1)} %add_convert_fusion.7), channel_id=1, source_target_pairs={{1,2},{2,1},{5,6},{6,5},{9,10},{10,9},{13,14},{14,13},{17,18},{18,... | collective-permute-start | bytes 1179656 | tf_op jit(solution)/shard_map/ppermute | solution.py:363
  77.4 3.9 %back_project.6 = (bf16[128,1536]{1,0:T(8,128)(2,1)S(1)}, bf16[128,1536]{1,0:T(8,128)(2,1)S(1)}, bf16[128,1536]{1,0:T(8,128)(2,1)S(1)}) custom-call(s32[6]{0:T(128)S(1)} %stack.37.place_ref, bf16[512,256]{1,0:T(8,128)(2,1)S(1)} %get-tuple-element.62.dq0_ref, bf16[512,256]{1,0:T(8,128)(2,1)S(1)} %get-tuple-element.63.dq1_ref, ...), custom_call_target="tpu_custom_call" | custom-call | flops 1207959552 | bytes 4325376 | tf_op jit(solution)/shard_map/back_project/pallas_call | solution.py:258
  81.3 1.3 collective-permute-start.10
  82.6 7.7 %back_project.8 = (bf16[128,1536]{1,0:T(8,128)(2,1)S(1)}, bf16[128,1536]{1,0:T(8,128)(2,1)S(1)}, bf16[128,1536]{1,0:T(8,128)(2,1)S(1)}, bf16[128,2304]{1,0:T(8,1...) custom-call(s32[6]{0:T(128)S(1)} %stack.37.place_ref, ...), custom_call_target="tpu_custom_call" | custom-call | flops 3019898880 | bytes 10813440 | tf_op jit(solution)/shard_map/back_project/pallas_call | solution.py:258
  90.3 1.3 collective-permute-start.16
  91.6 1.3 collective-permute-start.21
  92.9 0.1 add_convert_fusion.2
  93.1 2.4 %collective-permute-start.18 = (bf16[128,2304]{1,0:T(8,128)(2,1)S(1)}, bf16[128,2304]{1,0:T(8,128)(2,1)S(1)}, u32[]{:S(2)}, u32[]{:S(2)}) collective-permute-start(bf16[128,2304]{1,0:T(8,128)(2,1)S(1)} %add_convert_fusion.2), channel_id=1, source_target_pairs={{1,2},{2,1},{5,6},{6,5},{9,10},{10,9},{13,14},{14,13},{17,18},{18,... | collective-permute-start | bytes 1769480 | tf_op jit(solution)/shard_map/ppermute | solution.py:363
  95.5 0.1 add_convert_fusion.5
  95.6 0.1 add_convert_fusion.3
  95.7 1.1 collective-permute-start.15
  96.8 0.1 add_convert_fusion.8
  96.9 2.4 %collective-permute-start.13 = (bf16[128,1536]{1,0:T(8,128)(2,1)S(1)}, bf16[128,1536]{1,0:T(8,128)(2,1)S(1)}, u32[]{:S(2)}, u32[]{:S(2)}) collective-permute-start(bf16[128,1536]{1,0:T(8,128)(2,1)S(1)} %add_convert_fusion.8), channel_id=1, source_target_pairs={{1,2},{2,1},{5,6},{6,5},{9,10},{10,9},{13,14},{14,13},{17,18},{18,... | collective-permute-start | bytes 1179656 | tf_op jit(solution)/shard_map/ppermute | solution.py:363
  99.4 4.9 %collective-permute-done.16 = bf16[128,1536]{1,0:T(8,128)(2,1)S(1)} collective-permute-done((bf16[128,1536]{1,0:T(8,128)(2,1)S(1)}, bf16[128,1536]{1,0:T(8,128)(2,1)S(1)}, u32[]{:S(2)}, u32[]{:S(2)}) %collective-permute-start.16) | collective-permute-done | bytes 393248 | tf_op jit(solution)/shard_map/ppermute | solution.py:363
  104.3 0.1 add_convert_fusion.4
  104.4 12.5 %collective-permute-done.21 = bf16[128,2304]{1,0:T(8,128)(2,1)S(1)} collective-permute-done((bf16[128,2304]{1,0:T(8,128)(2,1)S(1)}, bf16[128,2304]{1,0:T(8,128)(2,1)S(1)}, u32[]{:S(2)}, u32[]{:S(2)}) %collective-permute-start.21) | collective-permute-done | bytes 589856 | tf_op jit(solution)/shard_map/ppermute | solution.py:363
  116.9 0.1 add_convert_fusion.1
  117.1 2.4 %collective-permute-start.19 = (bf16[128,1536]{1,0:T(8,128)(2,1)S(1)}, bf16[128,1536]{1,0:T(8,128)(2,1)S(1)}, u32[]{:S(2)}, u32[]{:S(2)}) collective-permute-start(bf16[128,1536]{1,0:T(8,128)(2,1)S(1)} %add_convert_fusion.4), channel_id=1, source_target_pairs={{1,2},{2,1},{5,6},{6,5},{9,10},{10,9},{13,14},{14,13},{17,18},{18,... | collective-permute-start | bytes 1179656 | tf_op jit(solution)/shard_map/ppermute | solution.py:363
  119.5 3.5 %collective-permute-start.22 = (bf16[128,2304]{1,0:T(8,128)(2,1)S(1)}, bf16[128,2304]{1,0:T(8,128)(2,1)S(1)}, u32[]{:S(2)}, u32[]{:S(2)}) collective-permute-start(bf16[128,2304]{1,0:T(8,128)(2,1)S(1)} %add_convert_fusion.1), channel_id=1, source_target_pairs={{1,2},{2,1},{5,6},{6,5},{9,10},{10,9},{13,14},{14,13},{17,18},{18,... | collective-permute-start | bytes 1769480 | tf_op jit(solution)/shard_map/ppermute | solution.py:363
  123.0 0.1 add_convert_fusion
  123.1 0.1 collective-permute-start.23
  123.2 2.2 %collective-permute-done.15 = bf16[128,1536]{1,0:T(8,128)(2,1)S(1)} collective-permute-done((bf16[128,1536]{1,0:T(8,128)(2,1)S(1)}, bf16[128,1536]{1,0:T(8,128)(2,1)S(1)}, u32[]{:S(2)}, u32[]{:S(2)}) %collective-permute-start.15) | collective-permute-done | bytes 393248 | tf_op jit(solution)/shard_map/ppermute | solution.py:363
  125.4 0.1 convert_add_fusion.2
  125.5 8.3 %collective-permute-done.20 = bf16[128,1536]{1,0:T(8,128)(2,1)S(1)} collective-permute-done((bf16[128,1536]{1,0:T(8,128)(2,1)S(1)}, bf16[128,1536]{1,0:T(8,128)(2,1)S(1)}, u32[]{:S(2)}, u32[]{:S(2)}) %collective-permute-start.20) | collective-permute-done | bytes 393248 | tf_op jit(solution)/shard_map/ppermute | solution.py:363
  133.8 0.1 convert_add_fusion.1
  133.9 3.4 %collective-permute-done.22 = bf16[128,2304]{1,0:T(8,128)(2,1)S(1)} collective-permute-done((bf16[128,2304]{1,0:T(8,128)(2,1)S(1)}, bf16[128,2304]{1,0:T(8,128)(2,1)S(1)}, u32[]{:S(2)}, u32[]{:S(2)}) %collective-permute-start.22) | collective-permute-done | bytes 589856 | tf_op jit(solution)/shard_map/ppermute | solution.py:363
  137.4 5.9 %collective-permute-done.23 = bf16[128,2304]{1,0:T(8,128)(2,1)S(1)} collective-permute-done((bf16[128,2304]{1,0:T(8,128)(2,1)S(1)}, bf16[128,2304]{1,0:T(8,128)(2,1)S(1)}, u32[]{:S(2)}, u32[]{:S(2)}) %collective-permute-start.23) | collective-permute-done | bytes 589856 | tf_op jit(solution)/shard_map/ppermute | solution.py:363
  143.3 0.2 convert_add_fusion
  143.5 1.7 %pad_maximum_fusion = f32[128,5376]{1,0:T(8,128)} fusion(f32[128,2304]{1,0:T(8,128)S(1)} %convert_add_fusion, f32[128,1536]{1,0:T(8,128)S(1)} %convert_add_fusion.1, f32[128,1536]{1,0:T(8,128)S(1)} %convert_add_fusion.2), kind=kLoop, calls=%fused_computation | loop fusion | flops 1376256 | bytes 5505024 | tf_op jit(solution)/shard_map/concatenate | solution.py:385
  (28 shorter events, 0.3 us)
Async XLA Ops:
  5.6 10.8 %collective-permute-start = (bf16[512,256]{1,0:T(8,128)(2,1)S(1)}, bf16[512,256]{1,0:T(8,128)(2,1)S(1)}, u32[]{:S(2)}, u32[]{:S(2)}) collective-permute-start(bf16[512,256]{1,0:T(8,128)(2,1)S(1)} %get-tuple-element.45.own_ref), channel_id=1, source_target_pairs={{0,8},{4,12},{8,16},{12,20},{16,24},{20,28},{1,9},{5,13},{9,17},{1... | collective-permute-start | bytes 786440 | tf_op jit(solution)/shard_map/ppermute | solution.py:307
  9.1 10.0 %copy-start.3 = (s32[512]{0:T(512)S(1)}, s32[512]{0:T(512)}, u32[]{:S(2)}) copy-start(s32[512]{0:T(512)} %param.11) | copy-start | bytes 6148
  9.1 10.2 %copy-start = (bf16[512,512]{1,0:T(8,128)(2,1)S(1)}, bf16[512,512]{1,0:T(8,128)(2,1)}, u32[]{:S(2)}) copy-start(bf16[512,512]{1,0:T(8,128)(2,1)} %do_ref.3) | copy-start | bytes 1572868
  16.5 2.8 %collective-permute-start.1 = (bf16[512,256]{1,0:T(8,128)(2,1)S(1)}, bf16[512,256]{1,0:T(8,128)(2,1)S(1)}, u32[]{:S(2)}, u32[]{:S(2)}) collective-permute-start(bf16[512,256]{1,0:T(8,128)(2,1)S(1)} %broadcast_select_fusion.1), channel_id=1, source_target_pairs={{0,4},{4,0},{8,12},{12,8},{16,20},{20,16},{24,28},{28,24},{1,5},{5... | collective-permute-start | bytes 786440 | tf_op jit(solution)/shard_map/ppermute | solution.py:319
  16.6 11.5 %collective-permute-start.3 = (bf16[512,256]{1,0:T(8,128)(2,1)S(1)}, bf16[512,256]{1,0:T(8,128)(2,1)S(1)}, u32[]{:S(2)}, u32[]{:S(2)}) collective-permute-start(bf16[512,256]{1,0:T(8,128)(2,1)S(1)} %get-tuple-element.52.own_ref), channel_id=1, source_target_pairs={{0,8},{4,12},{8,16},{12,20},{16,24},{20,28},{1,9},{5,13},{9,17},{1... | collective-permute-start | bytes 786440 | tf_op jit(solution)/shard_map/ppermute | solution.py:307
  24.5 3.7 %collective-permute-start.2 = (bf16[512,256]{1,0:T(8,128)(2,1)S(1)}, bf16[512,256]{1,0:T(8,128)(2,1)S(1)}, u32[]{:S(2)}, u32[]{:S(2)}) collective-permute-start(bf16[512,256]{1,0:T(8,128)(2,1)S(1)} %get-tuple-element.50), channel_id=1, source_target_pairs={{0,4},{4,0},{8,12},{12,8},{16,20},{20,16},{24,28},{28,24},{1,5},{5... | collective-permute-start | bytes 786440 | tf_op jit(solution)/shard_map/ppermute | solution.py:324
  28.1 3.3 %collective-permute-start.4 = (bf16[512,256]{1,0:T(8,128)(2,1)S(1)}, bf16[512,256]{1,0:T(8,128)(2,1)S(1)}, u32[]{:S(2)}, u32[]{:S(2)}) collective-permute-start(bf16[512,256]{1,0:T(8,128)(2,1)S(1)} %broadcast_select_fusion), channel_id=1, source_target_pairs={{0,4},{4,0},{8,12},{12,8},{16,20},{20,16},{24,28},{28,24},{1,5},{5... | collective-permute-start | bytes 786440 | tf_op jit(solution)/shard_map/ppermute | solution.py:319
  28.2 3.2 %copy-start.2 = (bf16[512,256]{1,0:T(8,128)(2,1)}, bf16[512,256]{1,0:T(8,128)(2,1)S(1)}, u32[]{:S(2)}) copy-start(bf16[512,256]{1,0:T(8,128)(2,1)S(1)} %collective-permute-done.2) | copy-start | bytes 786436
  29.0 10.9 %collective-permute-start.5 = (bf16[512,256]{1,0:T(8,128)(2,1)}, bf16[512,256]{1,0:T(8,128)(2,1)}, u32[]{:S(2)}, u32[]{:S(2)}) collective-permute-start(bf16[512,256]{1,0:T(8,128)(2,1)} %fusion.6), channel_id=1, source_target_pairs={{8,0},{12,4},{16,8},{20,12},{24,16},{28,20},{9,1},{13,5},{17,9},{2... | collective-permute-start | bytes 786440 | tf_op jit(solution)/shard_map/ppermute | solution.py:331
  31.4 1.0 copy-start.1
  39.9 1.7 %collective-permute-start.6 = (bf16[512,256]{1,0:T(8,128)(2,1)}, bf16[512,256]{1,0:T(8,128)(2,1)S(1)}, u32[]{:S(2)}, u32[]{:S(2)}) collective-permute-start(bf16[512,256]{1,0:T(8,128)(2,1)} %get-tuple-element.59), channel_id=1, source_target_pairs={{0,4},{4,0},{8,12},{12,8},{16,20},{20,16},{24,28},{28,24},{1,5},{5... | collective-permute-start | bytes 786440 | tf_op jit(solution)/shard_map/ppermute | solution.py:324
  41.8 6.2 %collective-permute-start.7 = (bf16[128,256]{1,0:T(8,128)(2,1)S(1)}, bf16[128,256]{1,0:T(8,128)(2,1)S(1)}, u32[]{:S(2)}, u32[]{:S(2)}) collective-permute-start(bf16[128,256]{1,0:T(8,128)(2,1)S(1)} %constant_dynamic-slice_fusion), channel_id=1, source_target_pairs={{8,0},{12,4},{16,8},{20,12},{24,16},{28,20},{9,1},{13,5},{17,9},{2... | collective-permute-start | bytes 196616 | tf_op jit(solution)/shard_map/ppermute | solution.py:341
  51.3 13.9 %collective-permute-start.8 = (bf16[128,1536]{1,0:T(8,128)(2,1)S(1)}, bf16[128,1536]{1,0:T(8,128)(2,1)S(1)}, u32[]{:S(2)}, u32[]{:S(2)}) collective-permute-start(bf16[128,1536]{1,0:T(8,128)(2,1)S(1)} %back_project.5), channel_id=1, source_target_pairs={{0,1},{3,2},{4,5},{7,6},{8,9},{11,10},{12,13},{15,14},{16,17},{19,... | collective-permute-start | bytes 1179656 | tf_op jit(solution)/shard_map/ppermute | solution.py:363
  56.1 17.6 %collective-permute-start.11 = (bf16[128,1536]{1,0:T(8,128)(2,1)S(1)}, bf16[128,1536]{1,0:T(8,128)(2,1)S(1)}, u32[]{:S(2)}, u32[]{:S(2)}) collective-permute-start(bf16[128,1536]{1,0:T(8,128)(2,1)S(1)} %back_project.7), channel_id=1, source_target_pairs={{0,1},{3,2},{4,5},{7,6},{8,9},{11,10},{12,13},{15,14},{16,17},{19,... | collective-permute-start | bytes 1179656 | tf_op jit(solution)/shard_map/ppermute | solution.py:363
  62.2 29.5 %collective-permute-start.17 = (bf16[128,2304]{1,0:T(8,128)(2,1)S(1)}, bf16[128,2304]{1,0:T(8,128)(2,1)S(1)}, u32[]{:S(2)}, u32[]{:S(2)}) collective-permute-start(bf16[128,2304]{1,0:T(8,128)(2,1)S(1)} %back_project.9), channel_id=1, source_target_pairs={{0,1},{3,2},{4,5},{7,6},{8,9},{11,10},{12,13},{15,14},{16,17},{19,... | collective-permute-start | bytes 1769480 | tf_op jit(solution)/shard_map/ppermute | solution.py:363
  65.3 12.0 %collective-permute-start.9 = (bf16[384,256]{1,0:T(8,128)(2,1)S(1)}, bf16[384,256]{1,0:T(8,128)(2,1)S(1)}, u32[]{:S(2)}, u32[]{:S(2)}) collective-permute-start(bf16[384,256]{1,0:T(8,128)(2,1)S(1)} %constant_dynamic-slice_fusion.1), channel_id=1, source_target_pairs={{8,0},{12,4},{16,8},{20,12},{24,16},{28,20},{9,1},{13,5},{17,9},{2... | collective-permute-start | bytes 589832 | tf_op jit(solution)/shard_map/ppermute | solution.py:341
  69.4 23.7 %collective-permute-start.14 = (bf16[128,1536]{1,0:T(8,128)(2,1)S(1)}, bf16[128,1536]{1,0:T(8,128)(2,1)S(1)}, u32[]{:S(2)}, u32[]{:S(2)}) collective-permute-start(bf16[128,1536]{1,0:T(8,128)(2,1)S(1)} %add_convert_fusion.6), channel_id=1, source_target_pairs={{1,2},{2,1},{5,6},{6,5},{9,10},{10,9},{13,14},{14,13},{17,18},{18,... | collective-permute-start | bytes 1179656 | tf_op jit(solution)/shard_map/ppermute | solution.py:363
  73.8 21.8 %collective-permute-start.12 = (bf16[128,1536]{1,0:T(8,128)(2,1)S(1)}, bf16[128,1536]{1,0:T(8,128)(2,1)S(1)}, u32[]{:S(2)}, u32[]{:S(2)}) collective-permute-start(bf16[128,1536]{1,0:T(8,128)(2,1)S(1)} %add_convert_fusion.7), channel_id=1, source_target_pairs={{1,2},{2,1},{5,6},{6,5},{9,10},{10,9},{13,14},{14,13},{17,18},{18,... | collective-permute-start | bytes 1179656 | tf_op jit(solution)/shard_map/ppermute | solution.py:363
  81.3 14.4 %collective-permute-start.10 = (bf16[128,1536]{1,0:T(8,128)(2,1)S(1)}, bf16[128,1536]{1,0:T(8,128)(2,1)S(1)}, u32[]{:S(2)}, u32[]{:S(2)}) collective-permute-start(bf16[128,1536]{1,0:T(8,128)(2,1)S(1)} %get-tuple-element.68), channel_id=1, source_target_pairs={{0,1},{3,2},{4,5},{7,6},{8,9},{11,10},{12,13},{15,14},{16,17},{19,... | collective-permute-start | bytes 1179656 | tf_op jit(solution)/shard_map/ppermute | solution.py:363
  90.3 14.0 %collective-permute-start.16 = (bf16[128,1536]{1,0:T(8,128)(2,1)S(1)}, bf16[128,1536]{1,0:T(8,128)(2,1)S(1)}, u32[]{:S(2)}, u32[]{:S(2)}) collective-permute-start(bf16[128,1536]{1,0:T(8,128)(2,1)S(1)} %get-tuple-element.74), channel_id=1, source_target_pairs={{0,1},{3,2},{4,5},{7,6},{8,9},{11,10},{12,13},{15,14},{16,17},{19,... | collective-permute-start | bytes 1179656 | tf_op jit(solution)/shard_map/ppermute | solution.py:363
  91.6 25.3 %collective-permute-start.21 = (bf16[128,2304]{1,0:T(8,128)(2,1)S(1)}, bf16[128,2304]{1,0:T(8,128)(2,1)S(1)}, u32[]{:S(2)}, u32[]{:S(2)}) collective-permute-start(bf16[128,2304]{1,0:T(8,128)(2,1)S(1)} %get-tuple-element.81), channel_id=1, source_target_pairs={{0,1},{3,2},{4,5},{7,6},{8,9},{11,10},{12,13},{15,14},{16,17},{19,... | collective-permute-start | bytes 1769480 | tf_op jit(solution)/shard_map/ppermute | solution.py:363
  93.1 24.0 %collective-permute-start.18 = (bf16[128,2304]{1,0:T(8,128)(2,1)S(1)}, bf16[128,2304]{1,0:T(8,128)(2,1)S(1)}, u32[]{:S(2)}, u32[]{:S(2)}) collective-permute-start(bf16[128,2304]{1,0:T(8,128)(2,1)S(1)} %add_convert_fusion.2), channel_id=1, source_target_pairs={{1,2},{2,1},{5,6},{6,5},{9,10},{10,9},{13,14},{14,13},{17,18},{18,... | collective-permute-start | bytes 1769480 | tf_op jit(solution)/shard_map/ppermute | solution.py:363
  95.7 29.7 %collective-permute-start.15 = (bf16[128,1536]{1,0:T(8,128)(2,1)S(1)}, bf16[128,1536]{1,0:T(8,128)(2,1)S(1)}, u32[]{:S(2)}, u32[]{:S(2)}) collective-permute-start(bf16[128,1536]{1,0:T(8,128)(2,1)S(1)} %add_convert_fusion.5), channel_id=1, source_target_pairs={{0,1},{3,2},{1,0},{2,3},{4,5},{7,6},{5,4},{6,7},{8,9},{11,10},{9,8... | collective-permute-start | bytes 1179656 | tf_op jit(solution)/shard_map/ppermute | solution.py:363
  96.9 22.6 %collective-permute-start.13 = (bf16[128,1536]{1,0:T(8,128)(2,1)S(1)}, bf16[128,1536]{1,0:T(8,128)(2,1)S(1)}, u32[]{:S(2)}, u32[]{:S(2)}) collective-permute-start(bf16[128,1536]{1,0:T(8,128)(2,1)S(1)} %add_convert_fusion.8), channel_id=1, source_target_pairs={{1,2},{2,1},{5,6},{6,5},{9,10},{10,9},{13,14},{14,13},{17,18},{18,... | collective-permute-start | bytes 1179656 | tf_op jit(solution)/shard_map/ppermute | solution.py:363
  104.3 29.5 %collective-permute-start.20 = (bf16[128,1536]{1,0:T(8,128)(2,1)S(1)}, bf16[128,1536]{1,0:T(8,128)(2,1)S(1)}, u32[]{:S(2)}, u32[]{:S(2)}) collective-permute-start(bf16[128,1536]{1,0:T(8,128)(2,1)S(1)} %add_convert_fusion.3), channel_id=1, source_target_pairs={{0,1},{3,2},{1,0},{2,3},{4,5},{7,6},{5,4},{6,7},{8,9},{11,10},{9,8... | collective-permute-start | bytes 1179656 | tf_op jit(solution)/shard_map/ppermute | solution.py:363
  117.1 16.7 %collective-permute-start.19 = (bf16[128,1536]{1,0:T(8,128)(2,1)S(1)}, bf16[128,1536]{1,0:T(8,128)(2,1)S(1)}, u32[]{:S(2)}, u32[]{:S(2)}) collective-permute-start(bf16[128,1536]{1,0:T(8,128)(2,1)S(1)} %add_convert_fusion.4), channel_id=1, source_target_pairs={{1,2},{2,1},{5,6},{6,5},{9,10},{10,9},{13,14},{14,13},{17,18},{18,... | collective-permute-start | bytes 1179656 | tf_op jit(solution)/shard_map/ppermute | solution.py:363
  119.5 17.9 %collective-permute-start.22 = (bf16[128,2304]{1,0:T(8,128)(2,1)S(1)}, bf16[128,2304]{1,0:T(8,128)(2,1)S(1)}, u32[]{:S(2)}, u32[]{:S(2)}) collective-permute-start(bf16[128,2304]{1,0:T(8,128)(2,1)S(1)} %add_convert_fusion.1), channel_id=1, source_target_pairs={{1,2},{2,1},{5,6},{6,5},{9,10},{10,9},{13,14},{14,13},{17,18},{18,... | collective-permute-start | bytes 1769480 | tf_op jit(solution)/shard_map/ppermute | solution.py:363
  123.1 20.2 %collective-permute-start.23 = (bf16[128,2304]{1,0:T(8,128)(2,1)S(1)}, bf16[128,2304]{1,0:T(8,128)(2,1)S(1)}, u32[]{:S(2)}, u32[]{:S(2)}) collective-permute-start(bf16[128,2304]{1,0:T(8,128)(2,1)S(1)} %add_convert_fusion), channel_id=1, source_target_pairs={{0,1},{3,2},{1,0},{2,3},{4,5},{7,6},{5,4},{6,7},{8,9},{11,10},{9,8... | collective-permute-start | bytes 1769480 | tf_op jit(solution)/shard_map/ppermute | solution.py:363
